TPU v7x, 32 devices: a whole 2x2x4 slice. The times are simulated.
32 devices in a mesh: slab: 2 (over y), aa: 4 (over z), ba: 4 (over x, core).
Axes of the slice: x: 2, y: 2, z: 4, core: 2. Of those that a mesh axis runs over, the one named last changes fastest.
Arguments:
- slab_field: float32 [8, 512, 512, 256], P('slab', 'aa', 'ba'), parts along dimension 0, may hold values from -18 to 18
- x_basis: float32 [1024, 128], P('slab'), parts along dimension 0, may hold values from -0.25 to 0.25
- y_basis: float32 [1024, 128], P('slab'), parts along dimension 0, may hold values from -0.25 to 0.25
Outputs:
- new_basis: float32 [1024, 128], P(('slab', 'aa')), parts along dimension 0
- core_tensor: float32 [8, 128, 128, 256], P('slab', None, 'aa', 'ba'), parts along dimension 0
There are 2 independent parts, one for each index of `slab`. A program takes and returns all parts, laid end to end along the dimension named above; each array names one. Nothing has to cross between parts.
All inputs are finite; a program needn't handle non-finite values.
Results may differ from a plain program's by a relative error of at most 0.00023.
Values sent between devices are 32-bit elements; how exact they have to be, the bound alone decides.
No kernel may reach another device: no remote copies, remote signals or barrier semaphores. Data moves between devices by JAX's collectives and lax.ppermute only.
A program may use at most 384 MiB of HBM per device.

v0:
```python
import jax
import jax.numpy as jnp
from jax import lax
from jax.sharding import PartitionSpec as P

ITERS = 2


def orthonormal(images):
    small = jnp.dot(images.T, images, precision=lax.Precision.HIGHEST)
    lower = jnp.linalg.cholesky(small)
    return lax.linalg.triangular_solve(lower, images, left_side=False, lower=True, transpose_a=True)


def body(slab_field, x_basis, y_basis):
    highest = lax.Precision.HIGHEST
    y_rows = slab_field.shape[2]
    y_start = lax.axis_index("ba") * y_rows
    local_basis = lax.dynamic_slice_in_dim(y_basis, y_start, y_rows, 0)
    partial_value = jnp.einsum("sxyz,yr->sxrz", slab_field, local_basis, precision=highest)
    projected = lax.psum_scatter(partial_value, "ba", scatter_dimension=3, tiled=True)
    columns = lax.all_to_all(projected, "aa", split_axis=2, concat_axis=1, tiled=True)
    basis = x_basis
    local_gram = jnp.einsum("sxrz,svrz->xv", columns, columns, precision=highest)
    gram_matrix = lax.psum(local_gram, ("aa", "ba"))
    for step in range(ITERS):
        images = jnp.dot(gram_matrix, basis, precision=highest)
        basis = orthonormal(images)
    core_tensor = jnp.einsum("xk,sxrz->skrz", basis, columns, precision=highest)
    basis_rows = x_basis.shape[0] // lax.axis_size("aa")
    row_start = lax.axis_index("aa") * basis_rows
    new_basis = lax.dynamic_slice_in_dim(basis, row_start, basis_rows, 0)
    return (new_basis, core_tensor)


def solution(mesh):
    return jax.shard_map(
        body,
        mesh=mesh,
        in_specs=(P("slab", "aa", "ba", None), P("slab", None), P("slab", None)),
        out_specs=(P(("slab", "aa"), None), P("slab", None, "aa", "ba")),
        check_vma=False,
    )
```

profile of v0, /device:TPU:0, one launch (start us, length us, event | category | flops | bytes accessed | tf_op | source)
XLA Modules:
  0.0 1218.4 jit_solution(7228787784649367946)
XLA Ops:
  7.2 0.9 copy-done
  8.1 67.1 %convolution_bitcast_fusion = f32[4,128,128,256]{3,2,1,0:T(8,128)} fusion(f32[4,128,128,256]{3,2,1,0:T(8,128)} %param.6, f32[512,128]{1,0:T(8,128)S(1)} %copy-done, s32[]{:T(128)S(6)} %select_n.9), kind=kOutput, calls=%fused_computation | convolution fusion | flops 25769803776 | bytes 134283264 | tf_op jit(solution)/shard_map/sxyz,yr->sxrz/dot_general | solution.py:20
  75.2 70.4 %copy.13 = f32[4,128,128,256]{2,1,0,3:T(8,128)} copy(f32[4,128,128,256]{3,2,1,0:T(8,128)} %convolution_bitcast_fusion) | data formatting | bytes 134217728 | tf_op jit(solution)/shard_map/sxyz,yr->sxrz/transpose | solution.py:20
  145.7 455.5 %reduce-scatter.4.cloned.1.call-done = f32[4,128,128,64]{2,1,0,3:T(8,128)} async-done(((f32[4,128,128,256]{2,1,0,3:T(8,128)}), f32[4,128,128,64]{2,1,0,3:T(8,128)}) %reduce-scatter.4.cloned.1.call-update) | async-done | bytes 16777232
  601.1 16.5 %copy.14 = f32[4,128,128,64]{1,3,0,2:T(8,128)} copy(f32[4,128,128,64]{2,1,0,3:T(8,128)} %reduce-scatter.4.cloned.1.call-done) | data formatting | bytes 33554432 | tf_op jit(solution)/shard_map/reduce_scatter | solution.py:21
  617.6 368.0 %all_to_all.18 = f32[4,128,128,64]{1,3,0,2:T(8,128)S(1)} all-to-all(f32[4,128,128,64]{1,3,0,2:T(8,128)} %copy.14), channel_id=1, replica_groups=mesh['slab'=2,'aa'=4,'ba'=4] {'aa'}, dimensions={2} | all-to-all | bytes 33554432 | tf_op jit(solution)/shard_map/all_to_all | solution.py:22
  985.6 12.0 copy.31
  997.6 19.9 %all_to_all.16 = f32[4,512,32,64]{1,3,0,2:T(8,128)} reshape(f32[4,4,128,32,64]{2,1,4,0,3:T(4,128)} %bitcast.64) | data formatting | bytes 33554432 | tf_op jit(solution)/shard_map/all_to_all | solution.py:22
  1017.5 31.8 %convolution_bitcast_fusion.1 = f32[512,512]{1,0:T(8,128)} fusion(f32[4,512,32,64]{1,3,0,2:T(8,128)} %all_to_all.16), kind=kOutput, calls=%fused_computation.5 | convolution fusion | flops 25769803776 | bytes 17825792 | tf_op jit(solution)/shard_map/sxrz,svrz->xv/dot_general | solution.py:24
  1049.4 91.3 %all-reduce.3.cloned.1.call-done = f32[512,512]{1,0:T(8,128)} async-done(((f32[512,512]{1,0:T(8,128)}), f32[512,512]{1,0:T(8,128)}) %all-reduce.3.cloned.1.call-update) | async-done | bytes 1048592 | tf_op jit(solution)/shard_map/psum | solution.py:25
  1140.7 2.2 fusion.18
  1143.0 0.6 fusion.19
  1143.7 11.7 cholesky.44
  1155.4 0.6 compare_reduce_fusion.1
  1156.1 0.7 fusion.6
  1156.7 9.8 custom-call.6
  1167.0 2.2 fusion.20
  1169.2 0.6 fusion.21
  1169.9 11.9 cholesky.55
  1181.8 0.6 compare_reduce_fusion
  1182.5 0.7 fusion.7
  1183.2 9.8 custom-call.7
  1193.4 17.0 %fusion.2 = f32[4,128,32,64]{1,3,2,0:T(8,128)} fusion(f32[4,512,32,64]{1,3,0,2:T(8,128)} %all_to_all.16, f32[128,512]{1,0:T(8,128)S(1)} %fusion.9), kind=kOutput, calls=%fused_computation.4 | convolution fusion | flops 6442450944 | bytes 21233664 | tf_op jit(solution)/shard_map/xk,sxrz->skrz/dot_general | solution.py:29
  1210.4 0.7 copy.20
  (18 shorter events, 1.2 us)
Async XLA Ops:
  7.2 1.0 copy-start
  7.2 594.0 %reduce-scatter.4.cloned.1.call-start = ((), (), s32[]{:S(2)}) async-start(), calls=%async_computation.3 | async-start | bytes 83886080
  145.6 995.1 %all-reduce.3.cloned.1.call-start = ((), (), s32[]{:S(2)}) async-start(), calls=%async_computation.2 | async-start | bytes 2097152 | tf_op jit(solution)/shard_map/psum | solution.py:25
  1017.5 123.2 %copy-start.2 = (f32[512,128]{1,0:T(8,128)S(1)}, f32[512,128]{1,0:T(8,128)}, u32[]{:S(2)}) copy-start(f32[512,128]{1,0:T(8,128)} %param.7) | copy-start | bytes 786436
  1017.5 193.6 %copy-start.1 = (f32[512,128]{1,0:T(8,128)S(1)}, f32[512,128]{1,0:T(8,128)}, u32[]{:S(2)}) copy-start(f32[512,128]{1,0:T(8,128)} %param.8) | copy-start | bytes 786436
Sparse Core Ops, SparseCore 0:
  145.7 455.3 reduce-scatter.3
  1049.5 91.1 all-reduce.2
where the time goes:
time: 1230 us; the launch traced here: 1220 us
  waiting for transfers between devices  547 us (44%)
  blocking collectives  368 us (30%)
  matrix products  122 us (10%)
  local copies, waits for them, and re-layouts  121 us (10%)
  other arithmetic  45.9 us (4%)
  between operations  14.6 us (1%)
    unnamed x3, waiting for transfers between devices  456 us
    all_to_all x1, blocking collectives, body(): lax.all_to_all(projected, 'aa', split_axis=2, concat_axis=1, tiled=True)  368 us
    psum x1, waiting for transfers between devices, body(): gram_matrix = lax.psum(local_gram, ('aa', 'ba'))  91.3 us
    transpose x1, local copies, waits for them, and re-layouts, body(): jnp.einsum('sxyz,yr->sxrz', slab_field, local_basis, precision=highest)  70.4 us
    dot_general x1, matrix products, body(): jnp.einsum('sxyz,yr->sxrz', slab_field, local_basis, precision=highest)  67.1 us
    all_to_all x2, local copies, waits for them, and re-layouts, body(): lax.all_to_all(projected, 'aa', split_axis=2, concat_axis=1, tiled=True)  31.9 us
    dot_general x1, matrix products, body(): jnp.einsum('sxrz,svrz->xv', columns, columns, precision=highest)  31.8 us
    another operation x6, other arithmetic, orthonormal(): lower = jnp.linalg.cholesky(small)  25 us
  transfers between devices with their start and end apart: 2, of which 2 were waited for; matrix products, arithmetic and copies ran while one was open for 0% of the time, Pallas kernels for 0%

commit v1 on v0

v1 whole, which is shorter than its diff:
```python
import jax
import jax.numpy as jnp
from jax import lax
from jax.experimental import pallas as pl
from jax.experimental.pallas import tpu as pltpu
from jax.sharding import PartitionSpec as P

ITERS = 2
F32 = jnp.float32
BF16 = jnp.bfloat16
HIGHEST = lax.Precision.HIGHEST
MIB = 1 << 20
X_PARTS = 4
R_PARTS = 4
LANES = 128
PAIRS = ((0, 0), (1, 0), (1, 1))


def split(value):
    high = value.astype(BF16)
    return high, (value - high.astype(F32)).astype(BF16)


def nt_dot(left, right):
    return lax.dot_general(left, right, (((1,), (1,)), ((), ())), preferred_element_type=F32)


def tn_dot(left, right):
    return lax.dot_general(left, right, (((0,), (0,)), ((), ())), preferred_element_type=F32)


def call(kernel, grid, in_specs, out_specs, out_shape, scratch=(), vmem=48, flops=0, moved=0):
    return pl.pallas_call(
        kernel,
        grid_spec=pltpu.PrefetchScalarGridSpec(
            num_scalar_prefetch=1, grid=grid, in_specs=in_specs, out_specs=out_specs, scratch_shapes=list(scratch)
        ),
        out_shape=out_shape,
        compiler_params=pltpu.CompilerParams(vmem_limit_bytes=vmem * MIB, dimension_semantics=("arbitrary",) * len(grid)),
        cost_estimate=pl.CostEstimate(flops=flops, bytes_accessed=moved, transcendentals=0),
    )


def project_kernel(parts, place, own_ref, other_ref, basis_ref, *rest):
    outs, basis_split = rest[:-1], rest[-1]
    keeps, sends = outs[:parts], outs[parts:]
    rank = basis_ref.shape[0]

    @pl.when(pl.program_id(0) == 0)
    def _():
        high, low = split(basis_ref[...])
        basis_split[0:rank, :] = high
        basis_split[rank:, :] = low

    first = place[0] == 0
    stacked = basis_split[...]
    for i in range(own_ref.shape[1]):
        high, low = split(jnp.concatenate([own_ref[0, i], other_ref[i]], axis=0))
        both = jnp.dot(stacked, high, preferred_element_type=F32)
        out = both[:rank] + (both[rank:] + jnp.dot(stacked[:rank], low, preferred_element_type=F32))
        left, right = out[:, :LANES], out[:, LANES:]
        keep, send = jnp.where(first, left, right), jnp.where(first, right, left)
        rows = rank // 4 // parts
        for a in range(4):
            for part in range(parts):
                at = (a * parts + part) * rows
                keeps[part][a, :, i, :] = keep[at : at + rows]
                sends[part][a, :, i, :] = send[at : at + rows]


def project(place, field, other, basis, species, x_start, parts):
    xs, ys, zs = other.shape
    rank = basis.shape[0]
    block = 8
    shape = (4, rank // 4 // parts, xs, zs // 2)
    out = pl.BlockSpec((4, shape[1], block, shape[3]), lambda i, place: (0, 0, i, 0))
    kernel = lambda place, *refs: project_kernel(parts, place, *refs)
    result = call(
        kernel,
        (xs // block,),
        [
            pl.BlockSpec((1, block, ys, zs), lambda i, place: (2 * place[1] + species, x_start // block + i, 0, 0)),
            pl.BlockSpec((block, ys, zs), lambda i, place: (i, 0, 0)),
            pl.BlockSpec(basis.shape, lambda i, place: (0, 0)),
        ],
        [out] * (2 * parts),
        [jax.ShapeDtypeStruct(shape, F32)] * (2 * parts),
        [pltpu.VMEM((2 * rank, 2 * ys), BF16)],
        flops=6 * xs * rank * 2 * ys * zs,
        moved=4 * xs * zs * (2 * ys + rank),
    )(place, field, other, basis)
    return result[:parts], result[parts:]


def add_kernel(place, keep_ref, recv_ref, *outs):
    for d in range(4):
        to = lax.rem(place[2] + d, 4)
        outs[d][...] = keep_ref[to] + recv_ref[to]


def add_up(place, keep, recv):
    _, rows, xs, zs = keep.shape
    block = max(1, 4 * LANES // xs)
    spec = pl.BlockSpec((4, block, xs, zs), lambda i, place: (0, i, 0, 0))
    out = pl.BlockSpec((block, xs, zs), lambda i, place: (i, 0, 0))
    return call(
        add_kernel,
        (rows // block,),
        [spec, spec],
        [out] * 4,
        [jax.ShapeDtypeStruct((rows, xs, zs), F32)] * 4,
        moved=12 * keep.size,
    )(place, keep, recv)


def gram_kernel(parts, place, start_ref, *rest):
    lines, (out_ref, high_ref, low_ref) = rest[: 4 * parts], rest[4 * parts :]
    rows, xs = lines[0].shape[:2]

    @pl.when(pl.program_id(0) == 0)
    def _():
        out_ref[...] = start_ref[...]

    for d in range(4):
        base = pl.multiple_of(lax.rem(place[2] + 4 - d, 4) * (parts * xs), parts * xs)
        for r in range(rows):
            block = jnp.concatenate([lines[d * parts + p][r] for p in range(parts)], axis=0)
            high, low = split(block)
            high_ref[pl.ds(base, parts * xs), r * LANES : (r + 1) * LANES] = high
            low_ref[pl.ds(base, parts * xs), r * LANES : (r + 1) * LANES] = low
    size = out_ref.shape[1]
    for index, (i, j) in enumerate(PAIRS):
        hi, li = high_ref[i * size : (i + 1) * size], low_ref[i * size : (i + 1) * size]
        hj, lj = high_ref[j * size : (j + 1) * size], low_ref[j * size : (j + 1) * size]
        out_ref[index * size : (index + 1) * size, :] += nt_dot(hi, hj) + (nt_dot(hi, lj) + nt_dot(li, hj))


def add_gram(place, start, lines):
    parts = len(lines[0])
    rows, xs, zs = lines[0][0].shape
    block = 8
    total = 4 * parts * xs
    line = pl.BlockSpec((block, xs, zs), lambda i, place: (i, 0, 0))
    whole = pl.BlockSpec(start.shape, lambda i, place: (0, 0))
    return call(
        lambda place, *refs: gram_kernel(parts, place, *refs),
        (rows // block,),
        [whole] + [line] * (4 * parts),
        whole,
        jax.ShapeDtypeStruct(start.shape, F32),
        [pltpu.VMEM((total, block * zs), BF16)] * 2,
        flops=6 * start.size * rows * zs,
        moved=4 * total * rows * zs,
    )(place, start, *[piece for group in lines for piece in group])


def inverse_factor(small):
    n = small.shape[0]
    rows = lax.broadcasted_iota(jnp.int32, (n, n), 0)
    cols = lax.broadcasted_iota(jnp.int32, (n, n), 1)
    unit = jnp.where(rows == cols, 1.0, 0.0).astype(F32)
    tiles = [small[8 * t : 8 * t + 8] for t in range(n // 8)]
    units = [unit[8 * t : 8 * t + 8] for t in range(n // 8)]
    sub = lax.broadcasted_iota(jnp.int32, (8, n), 0)
    done = [None] * (n // 8)
    for j in range(n):
        at, r = divmod(j, 8)
        row, unit_row = tiles[at][r : r + 1], units[at][r : r + 1]
        pivot = row[:, j : j + 1]
        inverse = 1.0 / pivot
        scale = lax.rsqrt(pivot)
        scaled = row * inverse
        for t in range(at, n // 8):
            column = tiles[t][:, j : j + 1]
            if t == at:
                column = jnp.where(sub[:, 0:1] > r, column, 0.0)
            factor = column * inverse
            tiles[t] = tiles[t] - factor * row
            units[t] = units[t] - factor * unit_row
        piece = jnp.where(sub == r, unit_row * scale, 0.0)
        done[at] = piece if r == 0 else done[at] + piece
    return jnp.concatenate(done, axis=0)


def basis_kernel(place, pieces_ref, start_ref, out_ref, gram_ref):
    count, size = pieces_ref.shape[0], pieces_ref.shape[1]
    for core in range(2):
        for chip in range(2):
            for d in range(4):
                at = (
                    lax.rem(place[1] + core, 2) * 8
                    + lax.rem(place[0] + chip, 2) * 4
                    + lax.rem(place[2] + 4 - d, 4)
                )
                gram_ref[pl.ds(pl.multiple_of(at * size, 8), size), :] = pieces_ref[(core * 2 + chip) * 4 + d]
    half = gram_ref.shape[1]
    g00, g10, g11 = (gram_ref[i * half : (i + 1) * half, :] for i in range(3))
    g01 = g10.T
    basis = start_ref[...]
    for _ in range(ITERS):
        top, low = basis[:half], basis[half:]
        dot = lambda a, b: jnp.dot(a, b, precision=HIGHEST, preferred_element_type=F32)
        images = jnp.concatenate([dot(g00, top) + dot(g01, low), dot(g10, top) + dot(g11, low)], axis=0)
        small = dot(images.T, images)
        basis = dot(images, inverse_factor(small).T)
    out_ref[...] = basis


def subspace(place, pieces, start):
    count, size, width = pieces.shape
    return call(
        basis_kernel,
        (1,),
        [
            pl.BlockSpec(pieces.shape, lambda i, place: (0, 0, 0)),
            pl.BlockSpec(start.shape, lambda i, place: (0, 0)),
        ],
        pl.BlockSpec(start.shape, lambda i, place: (0, 0)),
        jax.ShapeDtypeStruct(start.shape, F32),
        [pltpu.VMEM((count * size, width), F32)],
    )(place, pieces, start)


def core_kernel(parts, r_parts, place, basis_ref, *rest):
    lines, (keep_ref, send_ref, factor_ref) = rest[:-3], rest[-3:]
    rank = basis_ref.shape[1]
    xs = basis_ref.shape[0] // 4

    @pl.when(pl.program_id(0) == 0)
    def _():
        for d in range(4):
            base = pl.multiple_of(lax.rem(place[2] + 4 - d, 4) * xs, xs)
            high, low = split(basis_ref[pl.ds(base, xs), :])
            factor_ref[d * xs : (d + 1) * xs, 0:rank] = high
            factor_ref[d * xs : (d + 1) * xs, rank:] = low

    factor = factor_ref[...]

    def work(pieces):
        rows, _, zs = pieces[0].shape
        lines = [jnp.concatenate([piece[r] for piece in pieces], axis=0) for r in range(rows)]
        high, low = split(jnp.concatenate(lines, axis=1))
        both = tn_dot(high, factor)
        out = both[:, :rank] + (both[:, rank:] + tn_dot(low, factor[:, :rank]))
        out = out.reshape(rows, 2, zs // 2, rank)
        first = place[1] == 0
        keep_ref[...] = jnp.where(first, out[:, 0], out[:, 1])
        send_ref[...] = jnp.where(first, out[:, 1], out[:, 0])

    if r_parts == 1:
        work(lines)
    else:
        for part in range(r_parts):

            @pl.when(pl.program_id(0) == part)
            def _(part=part):
                work(lines[4 * part : 4 * part + 4])


def core_of(place, basis, lines, r_parts):
    parts = len(lines[0][0])
    rows, xs, zs = lines[0][0][0].shape
    block = 8
    rank = basis.shape[1]
    flat = [piece for group in lines for d in group for piece in d]
    total = rows * r_parts
    return call(
        lambda place, *refs: core_kernel(parts, r_parts, place, *refs),
        (total // block,),
        [pl.BlockSpec(basis.shape, lambda i, place: (0, 0))]
        + [pl.BlockSpec((block, xs, zs), (lambda i, place: (i, 0, 0)) if r_parts == 1 else (lambda i, place: (0, 0, 0)))]
        * len(flat),
        [pl.BlockSpec((block, zs // 2, rank), lambda i, place: (i, 0, 0))] * 2,
        [jax.ShapeDtypeStruct((total, zs // 2, rank), F32)] * 2,
        [pltpu.VMEM((basis.shape[0], 2 * rank), BF16)],
        flops=6 * basis.size * total * zs,
        moved=4 * total * zs * (basis.shape[0] + rank),
    )(place, basis, *flat)


def after(value, *earlier):
    return lax.optimization_barrier((value, *earlier))[0]


def pair_swap(value, distance):
    return lax.ppermute(value, "ba", [(i, i ^ distance) for i in range(4)])


def z_shift(value, d):
    return lax.ppermute(value, "aa", [(i, (i + d) % 4) for i in range(4)])


def reduce_gram(place, gram):
    chip, core, z = place[0], place[1], place[2]
    rows, width = gram.shape
    halves = gram.reshape(2, rows // 2, width)
    take = lambda array, i: lax.dynamic_index_in_dim(array, i, 0, keepdims=False)
    gram = take(halves, core) + pair_swap(take(halves, 1 - core), 1)
    halves = gram.reshape(2, rows // 4, width)
    gram = take(halves, chip) + pair_swap(take(halves, 1 - chip), 2)
    blocks = gram.reshape(4, rows // 16, width)
    came = [z_shift(take(blocks, (z + d) % 4), d) for d in (1, 2, 3)]
    gram = take(blocks, z) + came[0] + came[1] + came[2]
    gram = jnp.stack([gram] + [z_shift(gram, d) for d in (1, 2, 3)])
    gram = jnp.concatenate([gram, pair_swap(gram, 2)])
    return jnp.concatenate([gram, pair_swap(gram, 1)])


def fast_body(slab_field, x_basis, y_basis):
    rank = x_basis.shape[1]
    species, xs, ys, zs = slab_field.shape
    ba = lax.axis_index("ba")
    chip, core, z = ba // 2, ba % 2, lax.axis_index("aa")
    place = jnp.stack([chip, core, z]).astype(jnp.int32)
    rows = lambda index: lax.dynamic_slice_in_dim(y_basis, index * ys, ys, 0)
    basis_t = jnp.concatenate([rows(ba), rows(ba ^ 1)], axis=0).T

    def swap_field(s, start, size, *earlier):
        theirs = lax.dynamic_slice(slab_field, (2 * (1 - core) + s, start, 0, 0), (1, size, ys, zs))
        return pair_swap(after(theirs[0], *earlier), 1)

    def spread(keep, recv):
        mine = add_up(place, keep, recv)
        return [mine[0]] + [z_shift(mine[d], d) for d in (1, 2, 3)]

    keeps, sends = [], []
    step = xs // X_PARTS
    others = []
    for i in range(X_PARTS):
        others.append(swap_field(0, i * step, step, *others[-2:-1]))
    others.append(swap_field(1, 0, xs, others[-1]))
    for i in range(X_PARTS):
        keep, send = project(place, slab_field, others[i], basis_t, 0, i * step, 1)
        keeps += keep
        sends += send
    keep, send = project(place, slab_field, others[-1], basis_t, 1, 0, R_PARTS)
    keeps += keep
    sends += send

    came, lines = [], []
    for i, (keep, send) in enumerate(zip(keeps, sends)):
        if i >= 2:
            send = after(send, came[i - 2], *(lines[i - 3][1:] if i >= 3 else ()))
        came.append(pair_swap(send, 2))
        if i >= 1:
            lines.append(spread(keeps[i - 1], came[i - 1]))
    lines.append(spread(keeps[-1], came[-1]))

    gram = jnp.zeros((len(PAIRS) * xs * 2, xs * 2), F32)
    first = [[lines[p][d] for p in range(X_PARTS)] for d in range(4)]
    second = [[[lines[X_PARTS + p][d]] for d in range(4)] for p in range(R_PARTS)]
    gram = add_gram(place, gram, first)
    for group in second:
        gram = add_gram(place, gram, group)
    basis = subspace(place, reduce_gram(place, gram), x_basis)

    keep0, send0 = core_of(place, basis, [first], 1)
    came0 = pair_swap(send0, 1)
    keep1, send1 = core_of(place, basis, second, R_PARTS)
    came1 = pair_swap(send1, 1)
    mine, theirs = (keep0, keep1), (came0, came1)
    core_tensor = jnp.stack(
        [jnp.where(core == i // 2, mine[i % 2], theirs[i % 2]) for i in range(species)]
    ).transpose(0, 3, 1, 2)
    new_basis = lax.dynamic_slice_in_dim(basis, z * xs, xs, 0)
    return new_basis, core_tensor


def orthonormal(images):
    small = jnp.dot(images.T, images, precision=HIGHEST)
    lower = jnp.linalg.cholesky(small)
    return lax.linalg.triangular_solve(lower, images, left_side=False, lower=True, transpose_a=True)


def plain_body(slab_field, x_basis, y_basis):
    y_rows = slab_field.shape[2]
    local_basis = lax.dynamic_slice_in_dim(y_basis, lax.axis_index("ba") * y_rows, y_rows, 0)
    partial_value = jnp.einsum("sxyz,yr->sxrz", slab_field, local_basis, precision=HIGHEST)
    projected = lax.psum_scatter(partial_value, "ba", scatter_dimension=3, tiled=True)
    columns = lax.all_to_all(projected, "aa", split_axis=2, concat_axis=1, tiled=True)
    basis = x_basis
    local_gram = jnp.einsum("sxrz,svrz->xv", columns, columns, precision=HIGHEST)
    gram_matrix = lax.psum(local_gram, ("aa", "ba"))
    for _ in range(ITERS):
        basis = orthonormal(jnp.dot(gram_matrix, basis, precision=HIGHEST))
    core_tensor = jnp.einsum("xk,sxrz->skrz", basis, columns, precision=HIGHEST)
    basis_rows = x_basis.shape[0] // lax.axis_size("aa")
    new_basis = lax.dynamic_slice_in_dim(basis, lax.axis_index("aa") * basis_rows, basis_rows, 0)
    return new_basis, core_tensor


def solution(mesh):
    def body(slab_field, x_basis, y_basis):
        fits = (
            mesh.shape["aa"] == 4
            and mesh.shape["ba"] == 4
            and slab_field.shape == (4, LANES, LANES, 2 * LANES)
            and x_basis.shape == y_basis.shape == (4 * LANES, LANES)
        )
        return (fast_body if fits else plain_body)(slab_field, x_basis, y_basis)

    return jax.shard_map(
        body,
        mesh=mesh,
        in_specs=(P("slab", "aa", "ba", None), P("slab", None), P("slab", None)),
        out_specs=(P(("slab", "aa"), None), P("slab", None, "aa", "ba")),
        check_vma=False,
    )
```

time: 1230 us -> 614 us (0.50)
  blocking collectives: 368 us -> 0 us
  waiting for transfers between devices: 547 us -> 267 us
  starting transfers between devices: 0.08 us -> 149 us
  Pallas kernels: 0 us -> 138 us
  matrix products: 122 us -> 0 us
  local copies, waits for them, and re-layouts: 121 us -> 42.8 us
  other arithmetic: 45.9 us -> 5.19 us
  between operations: 14.6 us -> 1.99 us
    unnamed x3 -> x0, waiting for transfers between devices: 456 us -> none
    all_to_all x1 -> x0, blocking collectives: 368 us -> none  [body(): lax.all_to_all(projected, 'aa', split_axis=2, concat_axis=1, tiled=True)]
    ppermute x0 -> x49, waiting for transfers between devices: none -> 267 us  [the longest x19 188 us: pair_swap(): return lax.ppermute(value, 'ba', [(i, i ^ distance) for i in range(4)])]
    ppermute x0 -> x49, starting transfers between devices: none -> 149 us  [the longest x30 135 us: z_shift(): return lax.ppermute(value, 'aa', [(i, (i + d) % 4) for i in range(4)])]
    pallas_call x0 -> x21, Pallas kernels: none -> 138 us  [the longest x5 56.4 us: project(): call(kernel, (xs // block,), [pl.BlockSpec((1, block, ys, zs), lambda i,...]
    dot_general x7 -> x0, matrix products: 122 us -> none  [the longest x1 67.1 us: body(): jnp.einsum('sxyz,yr->sxrz', slab_field, local_basis, precision=highest)]
    psum x1 -> x0, waiting for transfers between devices: 91.3 us -> none  [body(): gram_matrix = lax.psum(local_gram, ('aa', 'ba'))]
    transpose x1 -> x0, local copies, waits for them, and re-layouts: 70.4 us -> none  [body(): jnp.einsum('sxyz,yr->sxrz', slab_field, local_basis, precision=highest)]
  transfers between devices with their start and end apart: 2 -> 49, of which waited for: 2 -> 28; matrix products, arithmetic and copies ran while one was open for 0% -> 2% of each run, Pallas kernels for 0% -> 17%
where the time goes in v1:
time: 614 us; the launch traced here: 605 us
  waiting for transfers between devices  267 us (43%)
  starting transfers between devices  149 us (24%)
  Pallas kernels  138 us (22%)
  local copies, waits for them, and re-layouts  42.8 us (7%)
    ppermute x19, waiting for transfers between devices, pair_swap(): return lax.ppermute(value, 'ba', [(i, i ^ distance) for i in range(4)])  188 us
    ppermute x30, starting transfers between devices, z_shift(): return lax.ppermute(value, 'aa', [(i, (i + d) % 4) for i in range(4)])  135 us
    ppermute x30, waiting for transfers between devices, z_shift(): return lax.ppermute(value, 'aa', [(i, (i + d) % 4) for i in range(4)])  78.9 us
    pallas_call x5, Pallas kernels, project(): call(kernel, (xs // block,), [pl.BlockSpec((1, block, ys, zs), lambda i,...  56.4 us
    pallas_call x1, Pallas kernels, subspace(): call(basis_kernel, (1,), [pl.BlockSpec(pieces.shape, lambda i, place: (0,...  25.8 us
    squeeze x2, local copies, waits for them, and re-layouts, swap_field(): return pair_swap(after(theirs[0], *earlier), 1)  23.6 us
    pallas_call x5, Pallas kernels, add_gram(): call(lambda place, *refs: gram_kernel(parts, place, *refs), (rows // bloc...  21.7 us
    pallas_call x8, Pallas kernels, add_up(): call(add_kernel, (rows // block,), [spec, spec], [out] * 4, [jax.ShapeDty...  20.3 us
  transfers between devices with their start and end apart: 49, of which 28 were waited for; matrix products, arithmetic and copies ran while one was open for 2% of the time, Pallas kernels for 17%

profile of v1, /device:TPU:0, one launch (start us, length us, event | category | flops | bytes accessed | tf_op | source)
XLA Modules:
  0.0 604.8 jit_solution(7566480121767447221)
XLA Ops:
  0.7 11.0 %dynamic-slice_bitcast_fusion.1 = (f32[32,128,256]{2,1,0:T(8,128)}, f32[32,128,256]{2,1,0:T(8,128)}, f32[32,128,256]{2,1,0:T(8,128)S(1)}, f32[32,128,256]{2,1,0:T(8,128)}) fusion(f32[4,128,128,256]{3,2,1,0:T(8,128)} %refs_0_.9, s32[]{:T(128)S(6)} %select_n.92), kind=kLoop, calls=%fused_computation.2 | loop fusion | bytes 33554436 | tf_op jit(solution)/shard_map/squeeze | solution.py:320
  21.3 12.6 %dynamic-slice_bitcast_fusion = f32[128,128,256]{2,1,0:T(8,128)} fusion(f32[4,128,128,256]{3,2,1,0:T(8,128)} %refs_0_.9, s32[]{:T(128)S(6)} %select_n.95), kind=kLoop, calls=%fused_computation | loop fusion | bytes 33554436 | tf_op jit(solution)/shard_map/squeeze | solution.py:320
  34.5 16.2 %collective-permute-done.refs_1_ = f32[32,128,256]{2,1,0:T(8,128)S(1)} collective-permute-done((f32[32,128,256]{2,1,0:T(8,128)S(1)}, f32[32,128,256]{2,1,0:T(8,128)S(1)}, u32[]{:S(2)}, u32[]{:S(2)}) %collective-permute-start) | collective-permute-done | bytes 4194336 | tf_op jit(solution)/shard_map/ppermute | solution.py:286
  71.4 8.1 %shard_map.54 = (f32[4,32,32,128]{3,2,1,0:T(8,128)S(1)}, f32[4,32,32,128]{3,2,1,0:T(8,128)}) custom-call(s32[3]{0:T(128)S(1)} %pad_add_fusion.place, f32[4,128,128,256]{3,2,1,0:T(8,128)} %refs_0_.9, f32[32,128,256]{2,1,0:T(8,128)} %collective-permute-done.4.refs_1_, f32[128,256]{1,0:T(8,128)S(1)} %maximum_bitcast_fusion.1.refs_2_), custom_call_target="tpu_custom_call" | custom-call | flops 1610612736 | bytes 12582912 | tf_op jit(solution)/shard_map/pallas_call | solution.py:78
  79.6 30.4 %collective-permute-done.1.recv_ref = f32[4,32,32,128]{3,2,1,0:T(8,128)} collective-permute-done((f32[4,32,32,128]{3,2,1,0:T(8,128)S(1)}, f32[4,32,32,128]{3,2,1,0:T(8,128)}, u32[]{:S(2)}, u32[]{:S(2)}) %collective-permute-start.1) | collective-permute-done | bytes 2097184 | tf_op jit(solution)/shard_map/ppermute | solution.py:286
  118.4 36.4 %collective-permute-done.3.recv_ref = f32[4,32,32,128]{3,2,1,0:T(8,128)} collective-permute-done((f32[4,32,32,128]{3,2,1,0:T(8,128)S(1)}, f32[4,32,32,128]{3,2,1,0:T(8,128)}, u32[]{:S(2)}, u32[]{:S(2)}) %collective-permute-start.3) | collective-permute-done | bytes 2097184 | tf_op jit(solution)/shard_map/ppermute | solution.py:286
  178.0 21.8 %collective-permute-done.5.recv_ref = f32[4,32,32,128]{3,2,1,0:T(8,128)} collective-permute-done((f32[4,32,32,128]{3,2,1,0:T(8,128)}, f32[4,32,32,128]{3,2,1,0:T(8,128)}, u32[]{:S(2)}, u32[]{:S(2)}) %collective-permute-start.5) | collective-permute-done | bytes 2097184 | tf_op jit(solution)/shard_map/ppermute | solution.py:286
  207.0 26.4 %shard_map.59 = (f32[4,8,128,128]{3,2,1,0:T(8,128)S(1)}, f32[4,8,128,128]{3,2,1,0:T(8,128)S(1)}, f32[4,8,128,128]{3,2,1,0:T(8,128)}, f32[4,8,128,128]{3,2,1,0:T(...) custom-call(s32[3]{0:T(128)S(1)} %pad_add_fusion.place, ...), custom_call_target="tpu_custom_call" | custom-call | flops 6442450944 | bytes 50331648 | tf_op jit(solution)/shard_map/pallas_call | solution.py:78
  244.8 14.5 %collective-permute-done.15.refs_11_ = f32[32,32,128]{2,1,0:T(8,128)S(1)} collective-permute-done((f32[32,32,128]{2,1,0:T(8,128)S(1)}, f32[32,32,128]{2,1,0:T(8,128)S(1)}, u32[]{:S(2)}, u32[]{:S(2)}) %collective-permute-start.15) | collective-permute-done | bytes 524320 | tf_op jit(solution)/shard_map/ppermute | solution.py:290
  264.0 10.7 %collective-permute-start.13 = (f32[32,32,128]{2,1,0:T(8,128)S(1)}, f32[32,32,128]{2,1,0:T(8,128)S(1)}, u32[]{:S(2)}, u32[]{:S(2)}) collective-permute-start(f32[32,32,128]{2,1,0:T(8,128)S(1)} %get-tuple-element.84), channel_id=1, source_target_pairs={{0,4},{4,8},{8,12},{12,0},{1,5},{5,9},{9,13},{13,1},{2,6},{6,10},{... | collective-permute-start | bytes 1572872 | tf_op jit(solution)/shard_map/ppermute | solution.py:290
  277.0 12.7 %collective-permute-done.21.recv_ref = f32[4,8,128,128]{3,2,1,0:T(8,128)} collective-permute-done((f32[4,8,128,128]{3,2,1,0:T(8,128)}, f32[4,8,128,128]{3,2,1,0:T(8,128)}, u32[]{:S(2)}, u32[]{:S(2)}) %collective-permute-start.21) | collective-permute-done | bytes 2097184 | tf_op jit(solution)/shard_map/ppermute | solution.py:286
  295.0 15.0 %collective-permute-start.23 = (f32[8,128,128]{2,1,0:T(8,128)S(1)}, f32[8,128,128]{2,1,0:T(8,128)S(1)}, u32[]{:S(2)}, u32[]{:S(2)}) collective-permute-start(f32[8,128,128]{2,1,0:T(8,128)S(1)} %get-tuple-element.97), channel_id=1, source_target_pairs={{0,8},{4,12},{8,0},{12,4},{1,9},{5,13},{9,1},{13,5},{2,10},{6,14},... | collective-permute-start | bytes 1572872 | tf_op jit(solution)/shard_map/ppermute | solution.py:290
  311.9 29.3 %collective-permute-start.24 = (f32[8,128,128]{2,1,0:T(8,128)S(1)}, f32[8,128,128]{2,1,0:T(8,128)S(1)}, u32[]{:S(2)}, u32[]{:S(2)}) collective-permute-start(f32[8,128,128]{2,1,0:T(8,128)S(1)} %get-tuple-element.98), channel_id=1, source_target_pairs={{0,12},{4,0},{8,4},{12,8},{1,13},{5,1},{9,5},{13,9},{2,14},{6,2},{... | collective-permute-start | bytes 1572872 | tf_op jit(solution)/shard_map/ppermute | solution.py:290
  342.1 13.1 %collective-permute-done.23.refs_3_ = f32[8,128,128]{2,1,0:T(8,128)S(1)} collective-permute-done((f32[8,128,128]{2,1,0:T(8,128)S(1)}, f32[8,128,128]{2,1,0:T(8,128)S(1)}, u32[]{:S(2)}, u32[]{:S(2)}) %collective-permute-start.23) | collective-permute-done | bytes 524320 | tf_op jit(solution)/shard_map/ppermute | solution.py:290
  360.1 11.0 %collective-permute-start.26 = (f32[8,128,128]{2,1,0:T(8,128)}, f32[8,128,128]{2,1,0:T(8,128)}, u32[]{:S(2)}, u32[]{:S(2)}) collective-permute-start(f32[8,128,128]{2,1,0:T(8,128)} %get-tuple-element.103), channel_id=1, source_target_pairs={{0,4},{4,8},{8,12},{12,0},{1,5},{5,9},{9,13},{13,1},{2,6},{6,10},{... | collective-permute-start | bytes 1572872 | tf_op jit(solution)/shard_map/ppermute | solution.py:290
  373.5 16.6 %collective-permute-done.29.recv_ref = f32[4,8,128,128]{3,2,1,0:T(8,128)} collective-permute-done((f32[4,8,128,128]{3,2,1,0:T(8,128)}, f32[4,8,128,128]{3,2,1,0:T(8,128)}, u32[]{:S(2)}, u32[]{:S(2)}) %collective-permute-start.29) | collective-permute-done | bytes 2097184 | tf_op jit(solution)/shard_map/ppermute | solution.py:286
  398.9 25.3 %collective-permute-done.33.recv_ref = f32[4,8,128,128]{3,2,1,0:T(8,128)} collective-permute-done((f32[4,8,128,128]{3,2,1,0:T(8,128)}, f32[4,8,128,128]{3,2,1,0:T(8,128)}, u32[]{:S(2)}, u32[]{:S(2)}) %collective-permute-start.33) | collective-permute-done | bytes 2097184 | tf_op jit(solution)/shard_map/ppermute | solution.py:286
  424.2 11.9 %collective-permute-start.31 = (f32[8,128,128]{2,1,0:T(8,128)}, f32[8,128,128]{2,1,0:T(8,128)S(1)}, u32[]{:S(2)}, u32[]{:S(2)}) collective-permute-start(f32[8,128,128]{2,1,0:T(8,128)} %copy-done.56), channel_id=1, source_target_pairs={{0,8},{4,12},{8,0},{12,4},{1,9},{5,13},{9,1},{13,5},{2,10},{6,14},... | collective-permute-start | bytes 1572872 | tf_op jit(solution)/shard_map/ppermute | solution.py:290
  447.1 10.2 %shard_map.58.refs_0_ = f32[768,256]{1,0:T(8,128)} custom-call(s32[3]{0:T(128)S(1)} %pad_add_fusion.place, f32[768,256]{1,0:T(8,128)} %broadcast_in_dim.3.refs_0_, f32[32,32,128]{2,1,0:T(8,128)S(1)} %get-tuple-element.65.refs_1_, f32[32,32,128]{2,1,0:T(8,128)S(1)} %copy-done.6, f32[32,32,128]{2,1,0:T(8,128)S(1)} %copy-done.15, ...), custom_call_target="tpu_custom_call" | custom-call | flops 4831838208 | bytes 8388608 | tf_op jit(solution)/shard_map/pallas_call | solution.py:145
  467.8 7.4 %collective-permute-done.34.refs_2_.refs_14_ = f32[8,128,128]{2,1,0:T(8,128)S(1)} collective-permute-done((f32[8,128,128]{2,1,0:T(8,128)S(1)}, f32[8,128,128]{2,1,0:T(8,128)S(1)}, u32[]{:S(2)}, u32[]{:S(2)}) %collective-permute-start.34) | collective-permute-done | bytes 524320 | tf_op jit(solution)/shard_map/ppermute | solution.py:290
  475.2 30.2 %collective-permute-done.35.refs_3_.refs_15_ = f32[8,128,128]{2,1,0:T(8,128)S(1)} collective-permute-done((f32[8,128,128]{2,1,0:T(8,128)S(1)}, f32[8,128,128]{2,1,0:T(8,128)S(1)}, u32[]{:S(2)}, u32[]{:S(2)}) %collective-permute-start.35) | collective-permute-done | bytes 524320 | tf_op jit(solution)/shard_map/ppermute | solution.py:290
  517.9 13.1 %collective-permute-start.41 = (f32[48,256]{1,0:T(8,128)S(1)}, f32[48,256]{1,0:T(8,128)S(1)}, u32[]{:S(2)}, u32[]{:S(2)}) collective-permute-start(f32[48,256]{1,0:T(8,128)S(1)} %get-tuple-element.139), channel_id=1, source_target_pairs={{0,12},{4,0},{8,4},{12,8},{1,13},{5,1},{9,5},{13,9},{2,14},{6,2},{... | collective-permute-start | bytes 147464 | tf_op jit(solution)/shard_map/ppermute | solution.py:290
  551.3 25.8 %shard_map.68.refs_0_ = f32[512,128]{1,0:T(8,128)S(1)} custom-call(s32[3]{0:T(128)S(1)} %pad_add_fusion.place, f32[16,48,256]{2,1,0:T(8,128)S(1)} %constant_dynamic-update-slice_fusion.5.pieces_ref, f32[512,128]{1,0:T(8,128)S(1)} %copy-done.54), custom_call_target="tpu_custom_call" | custom-call | tf_op jit(solution)/shard_map/pallas_call | solution.py:211
  583.4 7.7 %shard_map.70 = (f32[32,64,128]{2,1,0:T(8,128)}, f32[32,64,128]{2,1,0:T(8,128)}) custom-call(s32[3]{0:T(128)S(1)} %pad_add_fusion.place, f32[512,128]{1,0:T(8,128)S(1)} %shard_map.68.refs_0_, f32[8,128,128]{2,1,0:T(8,128)S(1)} %copy-done.31, f32[8,128,128]{2,1,0:T(8,128)S(1)} %copy-done.34, f32[8,128,128]{2,1,0:T(8,128)S(1)} %copy-done.37, ...), custom_call_target="tpu_custom_call" | custom-call | flops 1610612736 | bytes 10485760 | tf_op jit(solution)/shard_map/pallas_call | solution.py:267
  (258 shorter events, 185.4 us)
Async XLA Ops:
  33.9 173.1 %collective-permute-start.20 = (f32[128,128,256]{2,1,0:T(8,128)}, f32[128,128,256]{2,1,0:T(8,128)}, u32[]{:S(2)}, u32[]{:S(2)}) collective-permute-start(f32[128,128,256]{2,1,0:T(8,128)} %dynamic-slice_bitcast_fusion), channel_id=1, source_target_pairs={{0,1},{1,0},{2,3},{3,2},{4,5},{5,4},{6,7},{7,6},{8,9},{9,8},{10,11... | collective-permute-start | bytes 50331656 | tf_op jit(solution)/shard_map/ppermute | solution.py:286
  60.6 49.3 %collective-permute-start.1 = (f32[4,32,32,128]{3,2,1,0:T(8,128)S(1)}, f32[4,32,32,128]{3,2,1,0:T(8,128)}, u32[]{:S(2)}, u32[]{:S(2)}) collective-permute-start(f32[4,32,32,128]{3,2,1,0:T(8,128)S(1)} %get-tuple-element.64), channel_id=1, source_target_pairs={{0,2},{1,3},{2,0},{3,1},{4,6},{5,7},{6,4},{7,5},{8,10},{9,11},{10,... | collective-permute-start | bytes 6291464 | tf_op jit(solution)/shard_map/ppermute | solution.py:286
  70.7 84.2 %collective-permute-start.3 = (f32[4,32,32,128]{3,2,1,0:T(8,128)S(1)}, f32[4,32,32,128]{3,2,1,0:T(8,128)}, u32[]{:S(2)}, u32[]{:S(2)}) collective-permute-start(f32[4,32,32,128]{3,2,1,0:T(8,128)S(1)} %get-tuple-element.67), channel_id=1, source_target_pairs={{0,2},{1,3},{2,0},{3,1},{4,6},{5,7},{6,4},{7,5},{8,10},{9,11},{10,... | collective-permute-start | bytes 6291464 | tf_op jit(solution)/shard_map/ppermute | solution.py:286
  109.9 89.9 %collective-permute-start.5 = (f32[4,32,32,128]{3,2,1,0:T(8,128)}, f32[4,32,32,128]{3,2,1,0:T(8,128)}, u32[]{:S(2)}, u32[]{:S(2)}) collective-permute-start(f32[4,32,32,128]{3,2,1,0:T(8,128)} %get-tuple-element.72), channel_id=1, source_target_pairs={{0,2},{1,3},{2,0},{3,1},{4,6},{5,7},{6,4},{7,5},{8,10},{9,11},{10,... | collective-permute-start | bytes 6291464 | tf_op jit(solution)/shard_map/ppermute | solution.py:286
  114.2 52.0 %collective-permute-start.7 = (f32[32,32,128]{2,1,0:T(8,128)S(1)}, f32[32,32,128]{2,1,0:T(8,128)S(1)}, u32[]{:S(2)}, u32[]{:S(2)}) collective-permute-start(f32[32,32,128]{2,1,0:T(8,128)S(1)} %get-tuple-element.77), channel_id=1, source_target_pairs={{0,4},{4,8},{8,12},{12,0},{1,5},{5,9},{9,13},{13,1},{2,6},{6,10},{... | collective-permute-start | bytes 1572872 | tf_op jit(solution)/shard_map/ppermute | solution.py:290
  115.8 50.4 %collective-permute-start.8 = (f32[32,32,128]{2,1,0:T(8,128)S(1)}, f32[32,32,128]{2,1,0:T(8,128)S(1)}, u32[]{:S(2)}, u32[]{:S(2)}) collective-permute-start(f32[32,32,128]{2,1,0:T(8,128)S(1)} %get-tuple-element.78), channel_id=1, source_target_pairs={{0,8},{4,12},{8,0},{12,4},{1,9},{5,13},{9,1},{13,5},{2,10},{6,14},... | collective-permute-start | bytes 1572872 | tf_op jit(solution)/shard_map/ppermute | solution.py:290
  169.3 75.4 %collective-permute-start.10 = (f32[4,32,32,128]{3,2,1,0:T(8,128)S(1)}, f32[4,32,32,128]{3,2,1,0:T(8,128)}, u32[]{:S(2)}, u32[]{:S(2)}) collective-permute-start(f32[4,32,32,128]{3,2,1,0:T(8,128)S(1)} %get-tuple-element.80), channel_id=1, source_target_pairs={{0,2},{1,3},{2,0},{3,1},{4,6},{5,7},{6,4},{7,5},{8,10},{9,11},{10,... | collective-permute-start | bytes 6291464 | tf_op jit(solution)/shard_map/ppermute | solution.py:286
  173.1 60.3 %collective-permute-start.11 = (f32[32,32,128]{2,1,0:T(8,128)S(1)}, f32[32,32,128]{2,1,0:T(8,128)S(1)}, u32[]{:S(2)}, u32[]{:S(2)}) collective-permute-start(f32[32,32,128]{2,1,0:T(8,128)S(1)} %get-tuple-element.82), channel_id=1, source_target_pairs={{0,4},{4,8},{8,12},{12,0},{1,5},{5,9},{9,13},{13,1},{2,6},{6,10},{... | collective-permute-start | bytes 1572872 | tf_op jit(solution)/shard_map/ppermute | solution.py:290
  173.6 60.8 %collective-permute-start.14 = (f32[32,32,128]{2,1,0:T(8,128)S(1)}, f32[32,32,128]{2,1,0:T(8,128)S(1)}, u32[]{:S(2)}, u32[]{:S(2)}) collective-permute-start(f32[32,32,128]{2,1,0:T(8,128)S(1)} %get-tuple-element.85), channel_id=1, source_target_pairs={{0,8},{4,12},{8,0},{12,4},{1,9},{5,13},{9,1},{13,5},{2,10},{6,14},... | collective-permute-start | bytes 1572872 | tf_op jit(solution)/shard_map/ppermute | solution.py:290
  234.5 55.2 %collective-permute-start.21 = (f32[4,8,128,128]{3,2,1,0:T(8,128)}, f32[4,8,128,128]{3,2,1,0:T(8,128)}, u32[]{:S(2)}, u32[]{:S(2)}) collective-permute-start(f32[4,8,128,128]{3,2,1,0:T(8,128)} %get-tuple-element.94), channel_id=1, source_target_pairs={{0,2},{1,3},{2,0},{3,1},{4,6},{5,7},{6,4},{7,5},{8,10},{9,11},{10,... | collective-permute-start | bytes 6291464 | tf_op jit(solution)/shard_map/ppermute | solution.py:286
  259.7 82.4 %collective-permute-start.25 = (f32[4,8,128,128]{3,2,1,0:T(8,128)}, f32[4,8,128,128]{3,2,1,0:T(8,128)S(1)}, u32[]{:S(2)}, u32[]{:S(2)}) collective-permute-start(f32[4,8,128,128]{3,2,1,0:T(8,128)} %get-tuple-element.101), channel_id=1, source_target_pairs={{0,2},{1,3},{2,0},{3,1},{4,6},{5,7},{6,4},{7,5},{8,10},{9,11},{10,... | collective-permute-start | bytes 6291464 | tf_op jit(solution)/shard_map/ppermute | solution.py:286
  276.3 64.9 %collective-permute-start.19 = (f32[32,32,128]{2,1,0:T(8,128)S(1)}, f32[32,32,128]{2,1,0:T(8,128)}, u32[]{:S(2)}, u32[]{:S(2)}) collective-permute-start(f32[32,32,128]{2,1,0:T(8,128)S(1)} %get-tuple-element.90), channel_id=1, source_target_pairs={{0,12},{4,0},{8,4},{12,8},{1,13},{5,1},{9,5},{13,9},{2,14},{6,2},{... | collective-permute-start | bytes 1572872 | tf_op jit(solution)/shard_map/ppermute | solution.py:290
  292.9 49.2 %collective-permute-start.22 = (f32[8,128,128]{2,1,0:T(8,128)S(1)}, f32[8,128,128]{2,1,0:T(8,128)S(1)}, u32[]{:S(2)}, u32[]{:S(2)}) collective-permute-start(f32[8,128,128]{2,1,0:T(8,128)S(1)} %get-tuple-element.96), channel_id=1, source_target_pairs={{0,4},{4,8},{8,12},{12,0},{1,5},{5,9},{9,13},{13,1},{2,6},{6,10},{... | collective-permute-start | bytes 1572872 | tf_op jit(solution)/shard_map/ppermute | solution.py:290
  295.0 60.2 %collective-permute-start.23 = (f32[8,128,128]{2,1,0:T(8,128)S(1)}, f32[8,128,128]{2,1,0:T(8,128)S(1)}, u32[]{:S(2)}, u32[]{:S(2)}) collective-permute-start(f32[8,128,128]{2,1,0:T(8,128)S(1)} %get-tuple-element.97), channel_id=1, source_target_pairs={{0,8},{4,12},{8,0},{12,4},{1,9},{5,13},{9,1},{13,5},{2,10},{6,14},... | collective-permute-start | bytes 1572872 | tf_op jit(solution)/shard_map/ppermute | solution.py:290
  311.9 44.8 %collective-permute-start.24 = (f32[8,128,128]{2,1,0:T(8,128)S(1)}, f32[8,128,128]{2,1,0:T(8,128)S(1)}, u32[]{:S(2)}, u32[]{:S(2)}) collective-permute-start(f32[8,128,128]{2,1,0:T(8,128)S(1)} %get-tuple-element.98), channel_id=1, source_target_pairs={{0,12},{4,0},{8,4},{12,8},{1,13},{5,1},{9,5},{13,9},{2,14},{6,2},{... | collective-permute-start | bytes 1572872 | tf_op jit(solution)/shard_map/ppermute | solution.py:290
  341.2 48.9 %collective-permute-start.29 = (f32[4,8,128,128]{3,2,1,0:T(8,128)}, f32[4,8,128,128]{3,2,1,0:T(8,128)}, u32[]{:S(2)}, u32[]{:S(2)}) collective-permute-start(f32[4,8,128,128]{3,2,1,0:T(8,128)} %get-tuple-element.108), channel_id=1, source_target_pairs={{0,2},{1,3},{2,0},{3,1},{4,6},{5,7},{6,4},{7,5},{8,10},{9,11},{10,... | collective-permute-start | bytes 6291464 | tf_op jit(solution)/shard_map/ppermute | solution.py:286
  356.7 67.5 %collective-permute-start.33 = (f32[4,8,128,128]{3,2,1,0:T(8,128)}, f32[4,8,128,128]{3,2,1,0:T(8,128)}, u32[]{:S(2)}, u32[]{:S(2)}) collective-permute-start(f32[4,8,128,128]{3,2,1,0:T(8,128)} %get-tuple-element.115), channel_id=1, source_target_pairs={{0,2},{1,3},{2,0},{3,1},{4,6},{5,7},{6,4},{7,5},{8,10},{9,11},{10,... | collective-permute-start | bytes 6291464 | tf_op jit(solution)/shard_map/ppermute | solution.py:286
  360.1 78.4 %collective-permute-start.26 = (f32[8,128,128]{2,1,0:T(8,128)}, f32[8,128,128]{2,1,0:T(8,128)}, u32[]{:S(2)}, u32[]{:S(2)}) collective-permute-start(f32[8,128,128]{2,1,0:T(8,128)} %get-tuple-element.103), channel_id=1, source_target_pairs={{0,4},{4,8},{8,12},{12,0},{1,5},{5,9},{9,13},{13,1},{2,6},{6,10},{... | collective-permute-start | bytes 1572872 | tf_op jit(solution)/shard_map/ppermute | solution.py:290
  371.1 70.9 %collective-permute-start.27 = (f32[8,128,128]{2,1,0:T(8,128)}, f32[8,128,128]{2,1,0:T(8,128)}, u32[]{:S(2)}, u32[]{:S(2)}) collective-permute-start(f32[8,128,128]{2,1,0:T(8,128)} %get-tuple-element.104), channel_id=1, source_target_pairs={{0,8},{4,12},{8,0},{12,4},{1,9},{5,13},{9,1},{13,5},{2,10},{6,14},... | collective-permute-start | bytes 1572872 | tf_op jit(solution)/shard_map/ppermute | solution.py:290
  371.6 70.5 %collective-permute-start.28 = (f32[8,128,128]{2,1,0:T(8,128)}, f32[8,128,128]{2,1,0:T(8,128)}, u32[]{:S(2)}, u32[]{:S(2)}) collective-permute-start(f32[8,128,128]{2,1,0:T(8,128)} %get-tuple-element.105), channel_id=1, source_target_pairs={{0,12},{4,0},{8,4},{12,8},{1,13},{5,1},{9,5},{13,9},{2,14},{6,2},{... | collective-permute-start | bytes 1572872 | tf_op jit(solution)/shard_map/ppermute | solution.py:290
  395.6 47.2 %collective-permute-start.30 = (f32[8,128,128]{2,1,0:T(8,128)}, f32[8,128,128]{2,1,0:T(8,128)}, u32[]{:S(2)}, u32[]{:S(2)}) collective-permute-start(f32[8,128,128]{2,1,0:T(8,128)} %get-tuple-element.110), channel_id=1, source_target_pairs={{0,4},{4,8},{8,12},{12,0},{1,5},{5,9},{9,13},{13,1},{2,6},{6,10},{... | collective-permute-start | bytes 1572872 | tf_op jit(solution)/shard_map/ppermute | solution.py:290
  424.2 40.2 %collective-permute-start.31 = (f32[8,128,128]{2,1,0:T(8,128)}, f32[8,128,128]{2,1,0:T(8,128)S(1)}, u32[]{:S(2)}, u32[]{:S(2)}) collective-permute-start(f32[8,128,128]{2,1,0:T(8,128)} %copy-done.56), channel_id=1, source_target_pairs={{0,8},{4,12},{8,0},{12,4},{1,9},{5,13},{9,1},{13,5},{2,10},{6,14},... | collective-permute-start | bytes 1572872 | tf_op jit(solution)/shard_map/ppermute | solution.py:290
  442.2 63.2 %collective-permute-start.35 = (f32[8,128,128]{2,1,0:T(8,128)S(1)}, f32[8,128,128]{2,1,0:T(8,128)S(1)}, u32[]{:S(2)}, u32[]{:S(2)}) collective-permute-start(f32[8,128,128]{2,1,0:T(8,128)S(1)} %get-tuple-element.118), channel_id=1, source_target_pairs={{0,8},{4,12},{8,0},{12,4},{1,9},{5,13},{9,1},{13,5},{2,10},{6,14},... | collective-permute-start | bytes 1572872 | tf_op jit(solution)/shard_map/ppermute | solution.py:290
  442.8 62.6 %collective-permute-start.36 = (f32[8,128,128]{2,1,0:T(8,128)S(1)}, f32[8,128,128]{2,1,0:T(8,128)S(1)}, u32[]{:S(2)}, u32[]{:S(2)}) collective-permute-start(f32[8,128,128]{2,1,0:T(8,128)S(1)} %get-tuple-element.119), channel_id=1, source_target_pairs={{0,12},{4,0},{8,4},{12,8},{1,13},{5,1},{9,5},{13,9},{2,14},{6,2},{... | collective-permute-start | bytes 1572872 | tf_op jit(solution)/shard_map/ppermute | solution.py:290
  (94 other events, 2118.6 us)

commit v2 on v1

--- a/solution.py
+++ b/solution.py
@@ -10,8 +10,8 @@
 BF16 = jnp.bfloat16
 HIGHEST = lax.Precision.HIGHEST
 MIB = 1 << 20
-X_PARTS = 4
-R_PARTS = 4
+X_PARTS = (16,) * 8
+R_PARTS = (4,) * 8
 LANES = 128
 PAIRS = ((0, 0), (1, 0), (1, 1))
 
@@ -29,21 +29,22 @@
     return lax.dot_general(left, right, (((0,), (0,)), ((), ())), preferred_element_type=F32)
 
 
-def call(kernel, grid, in_specs, out_specs, out_shape, scratch=(), vmem=48, flops=0, moved=0):
+def call(name, kernel, grid, in_specs, out_specs, out_shape, scratch=(), vmem=16):
     return pl.pallas_call(
         kernel,
+        name=name,
         grid_spec=pltpu.PrefetchScalarGridSpec(
             num_scalar_prefetch=1, grid=grid, in_specs=in_specs, out_specs=out_specs, scratch_shapes=list(scratch)
         ),
         out_shape=out_shape,
         compiler_params=pltpu.CompilerParams(vmem_limit_bytes=vmem * MIB, dimension_semantics=("arbitrary",) * len(grid)),
-        cost_estimate=pl.CostEstimate(flops=flops, bytes_accessed=moved, transcendentals=0),
+        cost_estimate=pl.CostEstimate(flops=0, bytes_accessed=0, transcendentals=0),
     )
 
 
 def project_kernel(parts, place, own_ref, other_ref, basis_ref, *rest):
     outs, basis_split = rest[:-1], rest[-1]
-    keeps, sends = outs[:parts], outs[parts:]
+    keeps, sends = outs[: len(parts)], outs[len(parts) :]
     rank = basis_ref.shape[0]
 
     @pl.when(pl.program_id(0) == 0)
@@ -60,74 +61,81 @@
         out = both[:rank] + (both[rank:] + jnp.dot(stacked[:rank], low, preferred_element_type=F32))
         left, right = out[:, :LANES], out[:, LANES:]
         keep, send = jnp.where(first, left, right), jnp.where(first, right, left)
-        rows = rank // 4 // parts
+        at = 0
         for a in range(4):
-            for part in range(parts):
-                at = (a * parts + part) * rows
+            for part, rows in enumerate(parts):
                 keeps[part][a, :, i, :] = keep[at : at + rows]
                 sends[part][a, :, i, :] = send[at : at + rows]
-
-
-def project(place, field, other, basis, species, x_start, parts):
-    xs, ys, zs = other.shape
+                at += rows
+
+
+def project(place, field, other, basis, job, offset):
+    species, x_start, xs, parts = job
+    _, ys, zs = other.shape
     rank = basis.shape[0]
     block = 8
-    shape = (4, rank // 4 // parts, xs, zs // 2)
-    out = pl.BlockSpec((4, shape[1], block, shape[3]), lambda i, place: (0, 0, i, 0))
-    kernel = lambda place, *refs: project_kernel(parts, place, *refs)
+    steps = xs // block
+    shapes = [(4, rows, xs, zs // 2) for rows in parts] * 2
+    in_specs = [
+        pl.BlockSpec((1, block, ys, zs), lambda i, place: (2 * place[1] + species, x_start // block + i, 0, 0)),
+        pl.BlockSpec((block, ys, zs), lambda i, place: (offset // block + i, 0, 0)),
+        pl.BlockSpec(basis.shape, lambda i, place: (0, 0)),
+    ]
+    out_specs = [pl.BlockSpec((4, s[1], block, s[3]), lambda i, place: (0, 0, i, 0)) for s in shapes]
     result = call(
-        kernel,
-        (xs // block,),
-        [
-            pl.BlockSpec((1, block, ys, zs), lambda i, place: (2 * place[1] + species, x_start // block + i, 0, 0)),
-            pl.BlockSpec((block, ys, zs), lambda i, place: (i, 0, 0)),
-            pl.BlockSpec(basis.shape, lambda i, place: (0, 0)),
-        ],
-        [out] * (2 * parts),
-        [jax.ShapeDtypeStruct(shape, F32)] * (2 * parts),
+        "project_k",
+        lambda place, *refs: project_kernel(parts, place, *refs),
+        (steps,),
+        in_specs,
+        out_specs,
+        [jax.ShapeDtypeStruct(s, F32) for s in shapes],
         [pltpu.VMEM((2 * rank, 2 * ys), BF16)],
-        flops=6 * xs * rank * 2 * ys * zs,
-        moved=4 * xs * zs * (2 * ys + rank),
+        vmem=18,
     )(place, field, other, basis)
-    return result[:parts], result[parts:]
+    count = len(parts)
+    return result[:count], result[count:]
 
 
 def add_kernel(place, keep_ref, recv_ref, *outs):
     for d in range(4):
-        to = lax.rem(place[2] + d, 4)
+        to = lax.bitwise_xor(place[2], d)
         outs[d][...] = keep_ref[to] + recv_ref[to]
 
 
 def add_up(place, keep, recv):
     _, rows, xs, zs = keep.shape
-    block = max(1, 4 * LANES // xs)
+    block = min(rows, max(1, 4 * LANES // xs))
+    while rows % block:
+        block -= 1
     spec = pl.BlockSpec((4, block, xs, zs), lambda i, place: (0, i, 0, 0))
     out = pl.BlockSpec((block, xs, zs), lambda i, place: (i, 0, 0))
     return call(
+        "add_k",
         add_kernel,
         (rows // block,),
         [spec, spec],
         [out] * 4,
         [jax.ShapeDtypeStruct((rows, xs, zs), F32)] * 4,
-        moved=12 * keep.size,
+        vmem=12,
     )(place, keep, recv)
 
 
 def gram_kernel(parts, place, start_ref, *rest):
     lines, (out_ref, high_ref, low_ref) = rest[: 4 * parts], rest[4 * parts :]
-    rows, xs = lines[0].shape[:2]
+    rows = lines[0].shape[0]
+    xs = high_ref.shape[0] // 4
 
     @pl.when(pl.program_id(0) == 0)
     def _():
         out_ref[...] = start_ref[...]
 
     for d in range(4):
-        base = pl.multiple_of(lax.rem(place[2] + 4 - d, 4) * (parts * xs), parts * xs)
+        base = pl.multiple_of(lax.bitwise_xor(place[2], d) * xs, xs)
         for r in range(rows):
             block = jnp.concatenate([lines[d * parts + p][r] for p in range(parts)], axis=0)
             high, low = split(block)
-            high_ref[pl.ds(base, parts * xs), r * LANES : (r + 1) * LANES] = high
-            low_ref[pl.ds(base, parts * xs), r * LANES : (r + 1) * LANES] = low
+            high_ref[pl.ds(base, xs), r * LANES : (r + 1) * LANES] = high
+            low_ref[pl.ds(base, xs), r * LANES : (r + 1) * LANES] = low
     size = out_ref.shape[1]
     for index, (i, j) in enumerate(PAIRS):
         hi, li = high_ref[i * size : (i + 1) * size], low_ref[i * size : (i + 1) * size]
@@ -137,21 +145,21 @@
 
 def add_gram(place, start, lines):
     parts = len(lines[0])
-    rows, xs, zs = lines[0][0].shape
-    block = 8
-    total = 4 * parts * xs
-    line = pl.BlockSpec((block, xs, zs), lambda i, place: (i, 0, 0))
+    rows, _, zs = lines[0][0].shape
+    block = min(8, rows)
+    total = 2 * start.shape[1]
+    flat = [piece for group in lines for piece in group]
     whole = pl.BlockSpec(start.shape, lambda i, place: (0, 0))
     return call(
+        "gram_k",
         lambda place, *refs: gram_kernel(parts, place, *refs),
         (rows // block,),
-        [whole] + [line] * (4 * parts),
+        [whole] + [pl.BlockSpec((block, *piece.shape[1:]), lambda i, place: (i, 0, 0)) for piece in flat],
         whole,
         jax.ShapeDtypeStruct(start.shape, F32),
         [pltpu.VMEM((total, block * zs), BF16)] * 2,
-        flops=6 * start.size * rows * zs,
-        moved=4 * total * rows * zs,
-    )(place, start, *[piece for group in lines for piece in group])
+        vmem=20,
+    )(place, start, *flat)
 
 
 def inverse_factor(small):
@@ -190,7 +198,7 @@
                 at = (
                     lax.rem(place[1] + core, 2) * 8
                     + lax.rem(place[0] + chip, 2) * 4
-                    + lax.rem(place[2] + 4 - d, 4)
+                    + lax.bitwise_xor(place[2], d)
                 )
                 gram_ref[pl.ds(pl.multiple_of(at * size, 8), size), :] = pieces_ref[(core * 2 + chip) * 4 + d]
     half = gram_ref.shape[1]
@@ -209,6 +217,7 @@
 def subspace(place, pieces, start):
     count, size, width = pieces.shape
     return call(
+        "subspace_k",
         basis_kernel,
         (1,),
         [
@@ -218,10 +227,11 @@
         pl.BlockSpec(start.shape, lambda i, place: (0, 0)),
         jax.ShapeDtypeStruct(start.shape, F32),
         [pltpu.VMEM((count * size, width), F32)],
+        vmem=12,
     )(place, pieces, start)
 
 
-def core_kernel(parts, r_parts, place, basis_ref, *rest):
+def core_kernel(counts, steps, place, basis_ref, *rest):
     lines, (keep_ref, send_ref, factor_ref) = rest[:-3], rest[-3:]
     rank = basis_ref.shape[1]
     xs = basis_ref.shape[0] // 4
@@ -229,52 +239,64 @@
     @pl.when(pl.program_id(0) == 0)
     def _():
         for d in range(4):
-            base = pl.multiple_of(lax.rem(place[2] + 4 - d, 4) * xs, xs)
+            base = pl.multiple_of(lax.bitwise_xor(place[2], d) * xs, xs)
             high, low = split(basis_ref[pl.ds(base, xs), :])
             factor_ref[d * xs : (d + 1) * xs, 0:rank] = high
             factor_ref[d * xs : (d + 1) * xs, rank:] = low
 
     factor = factor_ref[...]
 
-    def work(pieces):
-        rows, _, zs = pieces[0].shape
-        lines = [jnp.concatenate([piece[r] for piece in pieces], axis=0) for r in range(rows)]
+    def work(groups):
+        lines = [
+            jnp.concatenate([piece[r] for piece in pieces], axis=0) for pieces in groups for r in range(pieces[0].shape[0])
+        ]
         high, low = split(jnp.concatenate(lines, axis=1))
         both = tn_dot(high, factor)
         out = both[:, :rank] + (both[:, rank:] + tn_dot(low, factor[:, :rank]))
-        out = out.reshape(rows, 2, zs // 2, rank)
+        out = out.reshape(len(lines), 2, LANES // 2, rank)
         first = place[1] == 0
         keep_ref[...] = jnp.where(first, out[:, 0], out[:, 1])
         send_ref[...] = jnp.where(first, out[:, 1], out[:, 0])
 
-    if r_parts == 1:
-        work(lines)
+    groups, at = [], 0
+    for count in counts:
+        groups.append(lines[at : at + count])
+        at += count
+    if steps is None:
+        work(groups)
     else:
-        for part in range(r_parts):
-
-            @pl.when(pl.program_id(0) == part)
-            def _(part=part):
-                work(lines[4 * part : 4 * part + 4])
-
-
-def core_of(place, basis, lines, r_parts):
-    parts = len(lines[0][0])
-    rows, xs, zs = lines[0][0][0].shape
+        for step, members in enumerate(steps):
+
+            @pl.when(pl.program_id(0) == step)
+            def _(members=members):
+                work([groups[member] for member in members])
+
+
+def core_of(place, basis, lines):
     block = 8
     rank = basis.shape[1]
-    flat = [piece for group in lines for d in group for piece in d]
-    total = rows * r_parts
+    groups = [[piece for d in group for piece in d] for group in lines]
+    flat = [piece for group in groups for piece in group]
+    rows = [group[0].shape[0] for group in groups]
+    total, zs = sum(rows), flat[0].shape[2]
+    if len(groups) == 1:
+        steps = None
+        specs = [pl.BlockSpec((block, *piece.shape[1:]), lambda i, place: (i, 0, 0)) for piece in flat]
+    else:
+        steps, at = [[] for _ in range(total // block)], 0
+        for member, count in enumerate(rows):
+            steps[at // block].append(member)
+            at += count
+        specs = [pl.BlockSpec(piece.shape, lambda i, place: (0, 0, 0)) for piece in flat]
     return call(
-        lambda place, *refs: core_kernel(parts, r_parts, place, *refs),
+        "core_k",
+        lambda place, *refs: core_kernel([len(group) for group in groups], steps, place, *refs),
         (total // block,),
-        [pl.BlockSpec(basis.shape, lambda i, place: (0, 0))]
-        + [pl.BlockSpec((block, xs, zs), (lambda i, place: (i, 0, 0)) if r_parts == 1 else (lambda i, place: (0, 0, 0)))]
-        * len(flat),
+        [pl.BlockSpec(basis.shape, lambda i, place: (0, 0))] + specs,
         [pl.BlockSpec((block, zs // 2, rank), lambda i, place: (i, 0, 0))] * 2,
         [jax.ShapeDtypeStruct((total, zs // 2, rank), F32)] * 2,
         [pltpu.VMEM((basis.shape[0], 2 * rank), BF16)],
-        flops=6 * basis.size * total * zs,
-        moved=4 * total * zs * (basis.shape[0] + rank),
+        vmem=36,
     )(place, basis, *flat)
 
 
@@ -286,8 +308,8 @@
     return lax.ppermute(value, "ba", [(i, i ^ distance) for i in range(4)])
 
 
-def z_shift(value, d):
-    return lax.ppermute(value, "aa", [(i, (i + d) % 4) for i in range(4)])
+def z_swap(value, d):
+    return lax.ppermute(value, "aa", [(i, i ^ d) for i in range(4)])
 
 
 def reduce_gram(place, gram):
@@ -299,9 +321,9 @@
     halves = gram.reshape(2, rows // 4, width)
     gram = take(halves, chip) + pair_swap(take(halves, 1 - chip), 2)
     blocks = gram.reshape(4, rows // 16, width)
-    came = [z_shift(take(blocks, (z + d) % 4), d) for d in (1, 2, 3)]
+    came = [z_swap(take(blocks, z ^ d), d) for d in (1, 2, 3)]
     gram = take(blocks, z) + came[0] + came[1] + came[2]
-    gram = jnp.stack([gram] + [z_shift(gram, d) for d in (1, 2, 3)])
+    gram = jnp.stack([gram] + [z_swap(gram, d) for d in (1, 2, 3)])
     gram = jnp.concatenate([gram, pair_swap(gram, 2)])
     return jnp.concatenate([gram, pair_swap(gram, 1)])
 
@@ -315,48 +337,58 @@
     rows = lambda index: lax.dynamic_slice_in_dim(y_basis, index * ys, ys, 0)
     basis_t = jnp.concatenate([rows(ba), rows(ba ^ 1)], axis=0).T
 
-    def swap_field(s, start, size, *earlier):
-        theirs = lax.dynamic_slice(slab_field, (2 * (1 - core) + s, start, 0, 0), (1, size, ys, zs))
-        return pair_swap(after(theirs[0], *earlier), 1)
-
-    def spread(keep, recv):
-        mine = add_up(place, keep, recv)
-        return [mine[0]] + [z_shift(mine[d], d) for d in (1, 2, 3)]
-
-    keeps, sends = [], []
-    step = xs // X_PARTS
-    others = []
-    for i in range(X_PARTS):
-        others.append(swap_field(0, i * step, step, *others[-2:-1]))
-    others.append(swap_field(1, 0, xs, others[-1]))
-    for i in range(X_PARTS):
-        keep, send = project(place, slab_field, others[i], basis_t, 0, i * step, 1)
-        keeps += keep
-        sends += send
-    keep, send = project(place, slab_field, others[-1], basis_t, 1, 0, R_PARTS)
-    keeps += keep
-    sends += send
-
-    came, lines = [], []
-    for i, (keep, send) in enumerate(zip(keeps, sends)):
-        if i >= 2:
-            send = after(send, came[i - 2], *(lines[i - 3][1:] if i >= 3 else ()))
-        came.append(pair_swap(send, 2))
+    share = rank // 4
+    jobs, at = [], 0
+    for size in X_PARTS:
+        jobs.append((0, at, size, (share,)))
+        at += size
+    jobs.append((1, 0, xs, R_PARTS))
+    keeps, sends, came, lines = [], [], [], []
+
+    def spread(i):
+        mine = add_up(place, keeps[i], came[i])
+        line = [mine[0], None, None, None]
+        for d, earlier in ((2, 1), (3, 2), (1, 3)):
+            part = after(mine[d], lines[-1][earlier]) if lines else mine[d]
+            line[d] = z_swap(part, d)
+        lines.append(line)
+
+    def exchange(part):
+        i = len(came)
+        earlier = came[i - 2 : i - 1] + (lines[i - 3][1:] if i >= 3 else []) if i >= 2 else []
+        came.append(pair_swap(after(part, *earlier), 2))
         if i >= 1:
-            lines.append(spread(keeps[i - 1], came[i - 1]))
-    lines.append(spread(keeps[-1], came[-1]))
+            spread(i - 1)
+
+    swaps = [(0, 0, X_PARTS[0]), (0, X_PARTS[0], xs - X_PARTS[0]), (1, 0, xs)]
+    others, theirs = [], []
+    for job in jobs:
+        while swaps and swaps[0][:2] <= job[:2]:
+            s, start, size = swaps.pop(0)
+            earlier = ([], sends[:1], theirs[-1:])[len(theirs)]
+            first = after(2 * (1 - core) + s, *earlier)
+            theirs.append(lax.dynamic_slice(slab_field, (first, start, 0, 0), (1, size, ys, zs))[0])
+            others.append((start, pair_swap(theirs[-1], 1)))
+        base, other = others[-1]
+        keep, send = project(place, slab_field, other, basis_t, job, job[1] - base)
+        for mine, part in zip(keep, send):
+            keeps.append(mine)
+            sends.append(part)
+            exchange(part)
+    spread(len(keeps) - 1)
 
     gram = jnp.zeros((len(PAIRS) * xs * 2, xs * 2), F32)
-    first = [[lines[p][d] for p in range(X_PARTS)] for d in range(4)]
-    second = [[[lines[X_PARTS + p][d]] for d in range(4)] for p in range(R_PARTS)]
+    count = len(X_PARTS)
+    first = [[lines[p][d] for p in range(count)] for d in range(4)]
+    second = [[[line[d]] for d in range(4)] for line in lines[count:]]
     gram = add_gram(place, gram, first)
     for group in second:
         gram = add_gram(place, gram, group)
     basis = subspace(place, reduce_gram(place, gram), x_basis)
 
-    keep0, send0 = core_of(place, basis, [first], 1)
+    keep0, send0 = core_of(place, basis, [first])
     came0 = pair_swap(send0, 1)
-    keep1, send1 = core_of(place, basis, second, R_PARTS)
+    keep1, send1 = core_of(place, basis, second)
     came1 = pair_swap(send1, 1)
     mine, theirs = (keep0, keep1), (came0, came1)
     core_tensor = jnp.stack(

time: 614 us -> 617 us (level)
  waiting for transfers between devices: 267 us -> 209 us
  local copies, waits for them, and re-layouts: 42.8 us -> 82.4 us
  starting transfers between devices: 149 us -> 175 us
  Pallas kernels: 138 us -> 130 us
    ppermute x19 -> x25, waiting for transfers between devices: 188 us -> 52.9 us  [pair_swap(): return lax.ppermute(value, 'ba', [(i, i ^ distance) for i in range(4)])]
    ppermute x30 -> x54, waiting for transfers between devices: 78.9 us -> 156 us  [z_swap(): return lax.ppermute(value, 'aa', [(i, i ^ d) for i in range(4)])]
    unnamed x144 -> x340, local copies, waits for them, and re-layouts: 17.6 us -> 54.8 us
    ppermute x19 -> x25, starting transfers between devices: 14.4 us -> 35.1 us  [pair_swap(): return lax.ppermute(value, 'ba', [(i, i ^ distance) for i in range(4)])]
    pallas_call x21 -> x37, Pallas kernels: 138 us -> 130 us  [the longest x9 59.1 us: project(): call('project_k', lambda place, *refs: project_kernel(parts, place, *refs...]
    ppermute x30 -> x54, starting transfers between devices: 135 us -> 140 us  [z_swap(): return lax.ppermute(value, 'aa', [(i, i ^ d) for i in range(4)])]
    squeeze x2 -> x3, local copies, waits for them, and re-layouts: 23.6 us -> 26.8 us  [fast_body(): lax.dynamic_slice(slab_field, (first, start, 0, 0), (1, size, ys, zs))[0]]
  transfers between devices with their start and end apart: 49 -> 79, of which waited for: 28 -> 35; matrix products, arithmetic and copies ran while one was open for 2% -> 2% of each run, Pallas kernels for 17% -> 15%
where the time goes in v2:
time: 617 us; the launch traced here: 606 us
  waiting for transfers between devices  209 us (34%)
  starting transfers between devices  175 us (28%)
  Pallas kernels  130 us (21%)
  local copies, waits for them, and re-layouts  82.4 us (13%)
  other arithmetic  6.67 us (1%)
    ppermute x54, waiting for transfers between devices, z_swap(): return lax.ppermute(value, 'aa', [(i, i ^ d) for i in range(4)])  156 us
    ppermute x54, starting transfers between devices, z_swap(): return lax.ppermute(value, 'aa', [(i, i ^ d) for i in range(4)])  140 us
    pallas_call x9, Pallas kernels, project(): call('project_k', lambda place, *refs: project_kernel(parts, place, *refs...  59.1 us
    unnamed x340, local copies, waits for them, and re-layouts  54.8 us
    ppermute x25, waiting for transfers between devices, pair_swap(): return lax.ppermute(value, 'ba', [(i, i ^ distance) for i in range(4)])  52.9 us
    ppermute x25, starting transfers between devices, pair_swap(): return lax.ppermute(value, 'ba', [(i, i ^ distance) for i in range(4)])  35.1 us
    squeeze x3, local copies, waits for them, and re-layouts, fast_body(): lax.dynamic_slice(slab_field, (first, start, 0, 0), (1, size, ys, zs))[0]  26.8 us
    pallas_call x1, Pallas kernels, subspace(): call('subspace_k', basis_kernel, (1,), [pl.BlockSpec(pieces.shape, lambda...  26 us
  transfers between devices with their start and end apart: 79, of which 35 were waited for; matrix products, arithmetic and copies ran while one was open for 2% of the time, Pallas kernels for 15%

profile of v2, /device:TPU:0, one launch (start us, length us, event | category | flops | bytes accessed | tf_op | source)
XLA Modules:
  0.0 605.9 jit_solution(3530219012461455900)
XLA Ops:
  13.3 12.1 %dynamic-slice_bitcast_fusion.1 = f32[112,128,256]{2,1,0:T(8,128)} fusion(f32[4,128,128,256]{3,2,1,0:T(8,128)} %refs_0_.17, s32[]{:T(128)S(6)} %select_n.83), kind=kLoop, calls=%fused_computation.1 | loop fusion | bytes 29360132 | tf_op jit(solution)/shard_map/squeeze | solution.py:370
  25.9 11.5 %dynamic-slice_bitcast_fusion = f32[128,128,256]{2,1,0:T(8,128)} fusion(f32[4,128,128,256]{3,2,1,0:T(8,128)} %refs_0_.17, s32[]{:T(128)S(6)} %select_n.84), kind=kLoop, calls=%fused_computation | loop fusion | bytes 33554436 | tf_op jit(solution)/shard_map/squeeze | solution.py:370
  40.4 7.6 %collective-permute-done.2.refs_1_ = f32[112,128,256]{2,1,0:T(8,128)} collective-permute-done((f32[112,128,256]{2,1,0:T(8,128)}, f32[112,128,256]{2,1,0:T(8,128)}, u32[]{:S(2)}, u32[]{:S(2)}) %collective-permute-start.2) | collective-permute-done | bytes 14680096 | tf_op jit(solution)/shard_map/ppermute | solution.py:308
  71.3 7.8 %collective-permute-done.5.refs_9_ = f32[32,16,128]{2,1,0:T(8,128)S(1)} collective-permute-done((f32[32,16,128]{2,1,0:T(8,128)S(1)}, f32[32,16,128]{2,1,0:T(8,128)S(1)}, u32[]{:S(2)}, u32[]{:S(2)}) %collective-permute-start.5) | collective-permute-done | bytes 262176 | tf_op jit(solution)/shard_map/ppermute | solution.py:312
  95.6 13.7 %collective-permute-done.4.recv_ref = f32[4,32,16,128]{3,2,1,0:T(8,128)S(1)} collective-permute-done((f32[4,32,16,128]{3,2,1,0:T(8,128)S(1)}, f32[4,32,16,128]{3,2,1,0:T(8,128)S(1)}, u32[]{:S(2)}, u32[]{:S(2)}) %collective-permute-start.4) | collective-permute-done | bytes 1048608 | tf_op jit(solution)/shard_map/ppermute | solution.py:308
  127.1 8.3 %collective-permute-done.13.refs_11_ = f32[32,16,128]{2,1,0:T(8,128)S(1)} collective-permute-done((f32[32,16,128]{2,1,0:T(8,128)S(1)}, f32[32,16,128]{2,1,0:T(8,128)S(1)}, u32[]{:S(2)}, u32[]{:S(2)}) %collective-permute-start.13) | collective-permute-done | bytes 262176 | tf_op jit(solution)/shard_map/ppermute | solution.py:312
  159.5 11.5 %collective-permute-start.21 = (f32[32,16,128]{2,1,0:T(8,128)S(1)}, f32[32,16,128]{2,1,0:T(8,128)S(1)}, u32[]{:S(2)}, u32[]{:S(2)}) collective-permute-start(f32[32,16,128]{2,1,0:T(8,128)S(1)} %get-tuple-element.214), channel_id=1, source_target_pairs={{0,4},{4,0},{8,12},{12,8},{1,5},{5,1},{9,13},{13,9},{2,6},{6,2},{1... | collective-permute-start | bytes 786440 | tf_op jit(solution)/shard_map/ppermute | solution.py:312
  184.0 9.7 %collective-permute-done.22.refs_21_ = f32[32,16,128]{2,1,0:T(8,128)S(1)} collective-permute-done((f32[32,16,128]{2,1,0:T(8,128)S(1)}, f32[32,16,128]{2,1,0:T(8,128)S(1)}, u32[]{:S(2)}, u32[]{:S(2)}) %collective-permute-start.22) | collective-permute-done | bytes 262176 | tf_op jit(solution)/shard_map/ppermute | solution.py:312
  203.8 24.0 %project_k.17 = (f32[4,4,128,128]{3,2,1,0:T(8,128)S(1)}, f32[4,4,128,128]{3,2,1,0:T(8,128)S(1)}, f32[4,4,128,128]{3,2,1,0:T(8,128)S(1)}, f32[4,4,128,128]{3,2,1,...) custom-call(s32[3]{0:T(128)S(1)} %pad_add_fusion.place, ...), custom_call_target="tpu_custom_call" | custom-call | tf_op jit(solution)/shard_map/project_k/pallas_call | solution.py:85
  235.2 6.8 %collective-permute-done.27.refs_15_ = f32[32,16,128]{2,1,0:T(8,128)S(1)} collective-permute-done((f32[32,16,128]{2,1,0:T(8,128)S(1)}, f32[32,16,128]{2,1,0:T(8,128)S(1)}, u32[]{:S(2)}, u32[]{:S(2)}) %collective-permute-start.27) | collective-permute-done | bytes 262176 | tf_op jit(solution)/shard_map/ppermute | solution.py:312
  247.4 8.6 %collective-permute-done.31.refs_23_ = f32[32,16,128]{2,1,0:T(8,128)S(1)} collective-permute-done((f32[32,16,128]{2,1,0:T(8,128)S(1)}, f32[32,16,128]{2,1,0:T(8,128)S(1)}, u32[]{:S(2)}, u32[]{:S(2)}) %collective-permute-start.31) | collective-permute-done | bytes 262176 | tf_op jit(solution)/shard_map/ppermute | solution.py:312
  262.0 6.5 %collective-permute-done.30.refs_16_ = f32[32,16,128]{2,1,0:T(8,128)S(1)} collective-permute-done((f32[32,16,128]{2,1,0:T(8,128)S(1)}, f32[32,16,128]{2,1,0:T(8,128)S(1)}, u32[]{:S(2)}, u32[]{:S(2)}) %collective-permute-start.30) | collective-permute-done | bytes 262176 | tf_op jit(solution)/shard_map/ppermute | solution.py:312
  268.5 8.8 %collective-permute-done.32.refs_24_ = f32[32,16,128]{2,1,0:T(8,128)S(1)} collective-permute-done((f32[32,16,128]{2,1,0:T(8,128)S(1)}, f32[32,16,128]{2,1,0:T(8,128)S(1)}, u32[]{:S(2)}, u32[]{:S(2)}) %collective-permute-start.32) | collective-permute-done | bytes 262176 | tf_op jit(solution)/shard_map/ppermute | solution.py:312
  290.4 12.9 %collective-permute-done.37.refs_3_ = f32[4,128,128]{2,1,0:T(8,128)S(1)} collective-permute-done((f32[4,128,128]{2,1,0:T(8,128)S(1)}, f32[4,128,128]{2,1,0:T(8,128)S(1)}, u32[]{:S(2)}, u32[]{:S(2)}) %collective-permute-start.37) | collective-permute-done | bytes 262176 | tf_op jit(solution)/shard_map/ppermute | solution.py:312
  315.0 13.0 %collective-permute-done.41.refs_3_.refs_7_ = f32[4,128,128]{2,1,0:T(8,128)S(1)} collective-permute-done((f32[4,128,128]{2,1,0:T(8,128)S(1)}, f32[4,128,128]{2,1,0:T(8,128)S(1)}, u32[]{:S(2)}, u32[]{:S(2)}) %collective-permute-start.41) | collective-permute-done | bytes 262176 | tf_op jit(solution)/shard_map/ppermute | solution.py:312
  340.7 12.9 %collective-permute-done.45.refs_3_.refs_11_ = f32[4,128,128]{2,1,0:T(8,128)S(1)} collective-permute-done((f32[4,128,128]{2,1,0:T(8,128)S(1)}, f32[4,128,128]{2,1,0:T(8,128)S(1)}, u32[]{:S(2)}, u32[]{:S(2)}) %collective-permute-start.45) | collective-permute-done | bytes 262176 | tf_op jit(solution)/shard_map/ppermute | solution.py:312
  364.4 10.3 %collective-permute-start.52 = (f32[4,128,128]{2,1,0:T(8,128)S(1)}, f32[4,128,128]{2,1,0:T(8,128)S(1)}, u32[]{:S(2)}, u32[]{:S(2)}) collective-permute-start(f32[4,128,128]{2,1,0:T(8,128)S(1)} %get-tuple-element.285), channel_id=1, source_target_pairs={{0,4},{4,0},{8,12},{12,8},{1,5},{5,1},{9,13},{13,9},{2,6},{6,2},{1... | collective-permute-start | bytes 786440 | tf_op jit(solution)/shard_map/ppermute | solution.py:312
  377.1 12.5 %collective-permute-done.49.refs_3_.refs_15_ = f32[4,128,128]{2,1,0:T(8,128)S(1)} collective-permute-done((f32[4,128,128]{2,1,0:T(8,128)S(1)}, f32[4,128,128]{2,1,0:T(8,128)S(1)}, u32[]{:S(2)}, u32[]{:S(2)}) %collective-permute-start.49) | collective-permute-done | bytes 262176 | tf_op jit(solution)/shard_map/ppermute | solution.py:312
  408.3 10.1 %collective-permute-done.59.recv_ref = f32[4,4,128,128]{3,2,1,0:T(8,128)S(1)} collective-permute-done((f32[4,4,128,128]{3,2,1,0:T(8,128)S(1)}, f32[4,4,128,128]{3,2,1,0:T(8,128)S(1)}, u32[]{:S(2)}, u32[]{:S(2)}) %collective-permute-start.59) | collective-permute-done | bytes 1048608 | tf_op jit(solution)/shard_map/ppermute | solution.py:308
  425.5 10.9 %collective-permute-start.60 = (f32[4,128,128]{2,1,0:T(8,128)S(1)}, f32[4,128,128]{2,1,0:T(8,128)S(1)}, u32[]{:S(2)}, u32[]{:S(2)}) collective-permute-start(f32[4,128,128]{2,1,0:T(8,128)S(1)} %get-tuple-element.305), channel_id=1, source_target_pairs={{0,4},{4,0},{8,12},{12,8},{1,5},{5,1},{9,13},{13,9},{2,6},{6,2},{1... | collective-permute-start | bytes 786440 | tf_op jit(solution)/shard_map/ppermute | solution.py:312
  445.8 6.9 %collective-permute-done.61.refs_3_.refs_27_ = f32[4,128,128]{2,1,0:T(8,128)S(1)} collective-permute-done((f32[4,128,128]{2,1,0:T(8,128)S(1)}, f32[4,128,128]{2,1,0:T(8,128)S(1)}, u32[]{:S(2)}, u32[]{:S(2)}) %collective-permute-start.61) | collective-permute-done | bytes 262176 | tf_op jit(solution)/shard_map/ppermute | solution.py:312
  475.6 9.2 %gram_k.9.refs_0_ = f32[768,256]{1,0:T(8,128)S(1)} custom-call(s32[3]{0:T(128)S(1)} %pad_add_fusion.place, f32[768,256]{1,0:T(8,128)S(1)} %broadcast_in_dim.3.refs_0_, f32[32,16,128]{2,1,0:T(8,128)S(1)} %get-tuple-element.165.refs_1_, f32[32,16,128]{2,1,0:T(8,128)S(1)} %get-tuple-element.169.refs_2_, f32[32,16,128]{2,1,0:T(8,128)S(1)} %get-tuple-element.173.refs_3_, ...), custom_call_target="tpu_custom_call" | custom-call | tf_op jit(solution)/shard_map/gram_k/pallas_call | solution.py:153
  501.9 7.3 %collective-permute-start.68 = (f32[192,256]{1,0:T(8,128)S(1)}, f32[192,256]{1,0:T(8,128)S(1)}, u32[]{:S(2)}, u32[]{:S(2)}) collective-permute-start(f32[192,256]{1,0:T(8,128)S(1)} %dynamic-slice_bitcast_fusion.4), channel_id=1, source_target_pairs={{0,2},{1,3},{2,0},{3,1},{4,6},{5,7},{6,4},{7,5},{8,10},{9,11},{10,... | collective-permute-start | bytes 589832 | tf_op jit(solution)/shard_map/ppermute | solution.py:308
  537.5 26.0 %subspace_k.1.refs_0_ = f32[512,128]{1,0:T(8,128)S(1)} custom-call(s32[3]{0:T(128)S(1)} %pad_add_fusion.place, f32[16,48,256]{2,1,0:T(8,128)S(1)} %constant_dynamic-update-slice_fusion.5.pieces_ref, f32[512,128]{1,0:T(8,128)S(1)} %copy-done.165), custom_call_target="tpu_custom_call" | custom-call | tf_op jit(solution)/shard_map/subspace_k/pallas_call | solution.py:219
  (531 shorter events, 334.1 us)
Async XLA Ops:
  37.4 166.4 %collective-permute-start.34 = (f32[128,128,256]{2,1,0:T(8,128)}, f32[128,128,256]{2,1,0:T(8,128)}, u32[]{:S(2)}, u32[]{:S(2)}) collective-permute-start(f32[128,128,256]{2,1,0:T(8,128)} %dynamic-slice_bitcast_fusion), channel_id=1, source_target_pairs={{0,1},{1,0},{2,3},{3,2},{4,5},{5,4},{6,7},{7,6},{8,9},{9,8},{10,11... | collective-permute-start | bytes 50331656 | tf_op jit(solution)/shard_map/ppermute | solution.py:308
  37.5 26.8 %collective-permute-start.1 = (f32[4,32,16,128]{3,2,1,0:T(8,128)S(1)}, f32[4,32,16,128]{3,2,1,0:T(8,128)S(1)}, u32[]{:S(2)}, u32[]{:S(2)}) collective-permute-start(f32[4,32,16,128]{3,2,1,0:T(8,128)S(1)} %get-tuple-element.164), channel_id=1, source_target_pairs={{0,2},{1,3},{2,0},{3,1},{4,6},{5,7},{6,4},{7,5},{8,10},{9,11},{10,... | collective-permute-start | bytes 3145736 | tf_op jit(solution)/shard_map/ppermute | solution.py:308
  52.4 34.9 %collective-permute-start.3 = (f32[4,32,16,128]{3,2,1,0:T(8,128)S(1)}, f32[4,32,16,128]{3,2,1,0:T(8,128)S(1)}, u32[]{:S(2)}, u32[]{:S(2)}) collective-permute-start(f32[4,32,16,128]{3,2,1,0:T(8,128)S(1)} %get-tuple-element.168), channel_id=1, source_target_pairs={{0,2},{1,3},{2,0},{3,1},{4,6},{5,7},{6,4},{7,5},{8,10},{9,11},{10,... | collective-permute-start | bytes 3145736 | tf_op jit(solution)/shard_map/ppermute | solution.py:308
  64.3 44.9 %collective-permute-start.4 = (f32[4,32,16,128]{3,2,1,0:T(8,128)S(1)}, f32[4,32,16,128]{3,2,1,0:T(8,128)S(1)}, u32[]{:S(2)}, u32[]{:S(2)}) collective-permute-start(f32[4,32,16,128]{3,2,1,0:T(8,128)S(1)} %get-tuple-element.172), channel_id=1, source_target_pairs={{0,2},{1,3},{2,0},{3,1},{4,6},{5,7},{6,4},{7,5},{8,10},{9,11},{10,... | collective-permute-start | bytes 3145736 | tf_op jit(solution)/shard_map/ppermute | solution.py:308
  87.3 59.4 %collective-permute-start.8 = (f32[4,32,16,128]{3,2,1,0:T(8,128)S(1)}, f32[4,32,16,128]{3,2,1,0:T(8,128)S(1)}, u32[]{:S(2)}, u32[]{:S(2)}) collective-permute-start(f32[4,32,16,128]{3,2,1,0:T(8,128)S(1)} %get-tuple-element.179), channel_id=1, source_target_pairs={{0,2},{1,3},{2,0},{3,1},{4,6},{5,7},{6,4},{7,5},{8,10},{9,11},{10,... | collective-permute-start | bytes 3145736 | tf_op jit(solution)/shard_map/ppermute | solution.py:308
  89.5 28.3 %collective-permute-start.9 = (f32[32,16,128]{2,1,0:T(8,128)S(1)}, f32[32,16,128]{2,1,0:T(8,128)S(1)}, u32[]{:S(2)}, u32[]{:S(2)}) collective-permute-start(f32[32,16,128]{2,1,0:T(8,128)S(1)} %get-tuple-element.184), channel_id=1, source_target_pairs={{0,4},{4,0},{8,12},{12,8},{1,5},{5,1},{9,13},{13,9},{2,6},{6,2},{1... | collective-permute-start | bytes 786440 | tf_op jit(solution)/shard_map/ppermute | solution.py:312
  118.5 38.3 %collective-permute-start.12 = (f32[4,32,16,128]{3,2,1,0:T(8,128)S(1)}, f32[4,32,16,128]{3,2,1,0:T(8,128)S(1)}, u32[]{:S(2)}, u32[]{:S(2)}) collective-permute-start(f32[4,32,16,128]{3,2,1,0:T(8,128)S(1)} %get-tuple-element.189), channel_id=1, source_target_pairs={{0,2},{1,3},{2,0},{3,1},{4,6},{5,7},{6,4},{7,5},{8,10},{9,11},{10,... | collective-permute-start | bytes 3145736 | tf_op jit(solution)/shard_map/ppermute | solution.py:308
  146.7 48.4 %collective-permute-start.16 = (f32[4,32,16,128]{3,2,1,0:T(8,128)S(1)}, f32[4,32,16,128]{3,2,1,0:T(8,128)S(1)}, u32[]{:S(2)}, u32[]{:S(2)}) collective-permute-start(f32[4,32,16,128]{3,2,1,0:T(8,128)S(1)} %get-tuple-element.199), channel_id=1, source_target_pairs={{0,2},{1,3},{2,0},{3,1},{4,6},{5,7},{6,4},{7,5},{8,10},{9,11},{10,... | collective-permute-start | bytes 3145736 | tf_op jit(solution)/shard_map/ppermute | solution.py:308
  175.4 52.4 %collective-permute-start.20 = (f32[4,32,16,128]{3,2,1,0:T(8,128)S(1)}, f32[4,32,16,128]{3,2,1,0:T(8,128)S(1)}, u32[]{:S(2)}, u32[]{:S(2)}) collective-permute-start(f32[4,32,16,128]{3,2,1,0:T(8,128)S(1)} %get-tuple-element.209), channel_id=1, source_target_pairs={{0,2},{1,3},{2,0},{3,1},{4,6},{5,7},{6,4},{7,5},{8,10},{9,11},{10,... | collective-permute-start | bytes 3145736 | tf_op jit(solution)/shard_map/ppermute | solution.py:308
  195.1 60.8 %collective-permute-start.24 = (f32[4,32,16,128]{3,2,1,0:T(8,128)S(1)}, f32[4,32,16,128]{3,2,1,0:T(8,128)S(1)}, u32[]{:S(2)}, u32[]{:S(2)}) collective-permute-start(f32[4,32,16,128]{3,2,1,0:T(8,128)S(1)} %get-tuple-element.219), channel_id=1, source_target_pairs={{0,2},{1,3},{2,0},{3,1},{4,6},{5,7},{6,4},{7,5},{8,10},{9,11},{10,... | collective-permute-start | bytes 3145736 | tf_op jit(solution)/shard_map/ppermute | solution.py:308
  197.9 29.9 %collective-permute-start.25 = (f32[32,16,128]{2,1,0:T(8,128)S(1)}, f32[32,16,128]{2,1,0:T(8,128)S(1)}, u32[]{:S(2)}, u32[]{:S(2)}) collective-permute-start(f32[32,16,128]{2,1,0:T(8,128)S(1)} %get-tuple-element.222), channel_id=1, source_target_pairs={{0,4},{4,0},{8,12},{12,8},{1,5},{5,1},{9,13},{13,9},{2,6},{6,2},{1... | collective-permute-start | bytes 786440 | tf_op jit(solution)/shard_map/ppermute | solution.py:312
  227.9 49.5 %collective-permute-start.35 = (f32[4,4,128,128]{3,2,1,0:T(8,128)S(1)}, f32[4,4,128,128]{3,2,1,0:T(8,128)S(1)}, u32[]{:S(2)}, u32[]{:S(2)}) collective-permute-start(f32[4,4,128,128]{3,2,1,0:T(8,128)S(1)} %get-tuple-element.242), channel_id=1, source_target_pairs={{0,2},{1,3},{2,0},{3,1},{4,6},{5,7},{6,4},{7,5},{8,10},{9,11},{10,... | collective-permute-start | bytes 3145736 | tf_op jit(solution)/shard_map/ppermute | solution.py:308
  256.0 47.4 %collective-permute-start.39 = (f32[4,4,128,128]{3,2,1,0:T(8,128)S(1)}, f32[4,4,128,128]{3,2,1,0:T(8,128)S(1)}, u32[]{:S(2)}, u32[]{:S(2)}) collective-permute-start(f32[4,4,128,128]{3,2,1,0:T(8,128)S(1)} %get-tuple-element.252), channel_id=1, source_target_pairs={{0,2},{1,3},{2,0},{3,1},{4,6},{5,7},{6,4},{7,5},{8,10},{9,11},{10,... | collective-permute-start | bytes 3145736 | tf_op jit(solution)/shard_map/ppermute | solution.py:308
  277.4 50.6 %collective-permute-start.43 = (f32[4,4,128,128]{3,2,1,0:T(8,128)S(1)}, f32[4,4,128,128]{3,2,1,0:T(8,128)S(1)}, u32[]{:S(2)}, u32[]{:S(2)}) collective-permute-start(f32[4,4,128,128]{3,2,1,0:T(8,128)S(1)} %get-tuple-element.262), channel_id=1, source_target_pairs={{0,2},{1,3},{2,0},{3,1},{4,6},{5,7},{6,4},{7,5},{8,10},{9,11},{10,... | collective-permute-start | bytes 3145736 | tf_op jit(solution)/shard_map/ppermute | solution.py:308
  303.3 50.2 %collective-permute-start.47 = (f32[4,4,128,128]{3,2,1,0:T(8,128)S(1)}, f32[4,4,128,128]{3,2,1,0:T(8,128)S(1)}, u32[]{:S(2)}, u32[]{:S(2)}) collective-permute-start(f32[4,4,128,128]{3,2,1,0:T(8,128)S(1)} %get-tuple-element.272), channel_id=1, source_target_pairs={{0,2},{1,3},{2,0},{3,1},{4,6},{5,7},{6,4},{7,5},{8,10},{9,11},{10,... | collective-permute-start | bytes 3145736 | tf_op jit(solution)/shard_map/ppermute | solution.py:308
  328.0 35.0 %collective-permute-start.51 = (f32[4,4,128,128]{3,2,1,0:T(8,128)S(1)}, f32[4,4,128,128]{3,2,1,0:T(8,128)S(1)}, u32[]{:S(2)}, u32[]{:S(2)}) collective-permute-start(f32[4,4,128,128]{3,2,1,0:T(8,128)S(1)} %get-tuple-element.282), channel_id=1, source_target_pairs={{0,2},{1,3},{2,0},{3,1},{4,6},{5,7},{6,4},{7,5},{8,10},{9,11},{10,... | collective-permute-start | bytes 3145736 | tf_op jit(solution)/shard_map/ppermute | solution.py:308
  353.6 44.4 %collective-permute-start.55 = (f32[4,4,128,128]{3,2,1,0:T(8,128)S(1)}, f32[4,4,128,128]{3,2,1,0:T(8,128)S(1)}, u32[]{:S(2)}, u32[]{:S(2)}) collective-permute-start(f32[4,4,128,128]{3,2,1,0:T(8,128)S(1)} %get-tuple-element.292), channel_id=1, source_target_pairs={{0,2},{1,3},{2,0},{3,1},{4,6},{5,7},{6,4},{7,5},{8,10},{9,11},{10,... | collective-permute-start | bytes 3145736 | tf_op jit(solution)/shard_map/ppermute | solution.py:308
  363.0 26.6 %collective-permute-start.49 = (f32[4,128,128]{2,1,0:T(8,128)S(1)}, f32[4,128,128]{2,1,0:T(8,128)S(1)}, u32[]{:S(2)}, u32[]{:S(2)}) collective-permute-start(f32[4,128,128]{2,1,0:T(8,128)S(1)} %get-tuple-element.277), channel_id=1, source_target_pairs={{0,8},{4,12},{8,0},{12,4},{1,9},{5,13},{9,1},{13,5},{2,10},{6,14},... | collective-permute-start | bytes 786440 | tf_op jit(solution)/shard_map/ppermute | solution.py:312
  364.4 29.7 %collective-permute-start.52 = (f32[4,128,128]{2,1,0:T(8,128)S(1)}, f32[4,128,128]{2,1,0:T(8,128)S(1)}, u32[]{:S(2)}, u32[]{:S(2)}) collective-permute-start(f32[4,128,128]{2,1,0:T(8,128)S(1)} %get-tuple-element.285), channel_id=1, source_target_pairs={{0,4},{4,0},{8,12},{12,8},{1,5},{5,1},{9,13},{13,9},{2,6},{6,2},{1... | collective-permute-start | bytes 786440 | tf_op jit(solution)/shard_map/ppermute | solution.py:312
  398.0 38.4 %collective-permute-start.63 = (f32[4,4,128,128]{3,2,1,0:T(8,128)S(1)}, f32[4,4,128,128]{3,2,1,0:T(8,128)S(1)}, u32[]{:S(2)}, u32[]{:S(2)}) collective-permute-start(f32[4,4,128,128]{3,2,1,0:T(8,128)S(1)} %get-tuple-element.312), channel_id=1, source_target_pairs={{0,2},{1,3},{2,0},{3,1},{4,6},{5,7},{6,4},{7,5},{8,10},{9,11},{10,... | collective-permute-start | bytes 3145736 | tf_op jit(solution)/shard_map/ppermute | solution.py:308
  408.3 28.1 %collective-permute-start.56 = (f32[4,128,128]{2,1,0:T(8,128)S(1)}, f32[4,128,128]{2,1,0:T(8,128)S(1)}, u32[]{:S(2)}, u32[]{:S(2)}) collective-permute-start(f32[4,128,128]{2,1,0:T(8,128)S(1)} %get-tuple-element.295), channel_id=1, source_target_pairs={{0,4},{4,0},{8,12},{12,8},{1,5},{5,1},{9,13},{13,9},{2,6},{6,2},{1... | collective-permute-start | bytes 786440 | tf_op jit(solution)/shard_map/ppermute | solution.py:312
  439.4 56.7 %collective-permute-start.64 = (f32[4,128,128]{2,1,0:T(8,128)}, f32[4,128,128]{2,1,0:T(8,128)}, u32[]{:S(2)}, u32[]{:S(2)}) collective-permute-start(f32[4,128,128]{2,1,0:T(8,128)} %get-tuple-element.315), channel_id=1, source_target_pairs={{0,4},{4,0},{8,12},{12,8},{1,5},{5,1},{9,13},{13,9},{2,6},{6,2},{1... | collective-permute-start | bytes 786440 | tf_op jit(solution)/shard_map/ppermute | solution.py:312
  445.4 50.7 %collective-permute-start.65 = (f32[4,128,128]{2,1,0:T(8,128)}, f32[4,128,128]{2,1,0:T(8,128)}, u32[]{:S(2)}, u32[]{:S(2)}) collective-permute-start(f32[4,128,128]{2,1,0:T(8,128)} %get-tuple-element.317), channel_id=1, source_target_pairs={{0,8},{4,12},{8,0},{12,4},{1,9},{5,13},{9,1},{13,5},{2,10},{6,14},... | collective-permute-start | bytes 786440 | tf_op jit(solution)/shard_map/ppermute | solution.py:312
  453.4 42.7 %collective-permute-start.66 = (f32[4,128,128]{2,1,0:T(8,128)}, f32[4,128,128]{2,1,0:T(8,128)}, u32[]{:S(2)}, u32[]{:S(2)}) collective-permute-start(f32[4,128,128]{2,1,0:T(8,128)} %get-tuple-element.319), channel_id=1, source_target_pairs={{0,12},{4,8},{8,4},{12,0},{1,13},{5,9},{9,5},{13,1},{2,14},{6,10},... | collective-permute-start | bytes 786440 | tf_op jit(solution)/shard_map/ppermute | solution.py:312
  (222 other events, 5949.5 us)

commit v3 on v2

--- a/solution.py
+++ b/solution.py
@@ -27,6 +27,10 @@
 
 def tn_dot(left, right):
     return lax.dot_general(left, right, (((0,), (0,)), ((), ())), preferred_element_type=F32)
+
+
+def in_hbm(*values):
+    return [pltpu.with_memory_space_constraint(value, pltpu.HBM) for value in values]
 
 
 def call(name, kernel, grid, in_specs, out_specs, out_shape, scratch=(), vmem=16):
@@ -88,10 +92,10 @@
         (steps,),
         in_specs,
         out_specs,
-        [jax.ShapeDtypeStruct(s, F32) for s in shapes],
+        [pltpu.HBM(s, F32) for s in shapes],
         [pltpu.VMEM((2 * rank, 2 * ys), BF16)],
-        vmem=18,
-    )(place, field, other, basis)
+        vmem=60,
+    )(place, *in_hbm(field, other), basis)
     count = len(parts)
     return result[:count], result[count:]
 
@@ -115,9 +119,9 @@
         (rows // block,),
         [spec, spec],
         [out] * 4,
-        [jax.ShapeDtypeStruct((rows, xs, zs), F32)] * 4,
-        vmem=12,
-    )(place, keep, recv)
+        [pltpu.HBM((rows, xs, zs), F32)] * 4,
+        vmem=60,
+    )(place, *in_hbm(keep, recv))
 
 
 def gram_kernel(parts, place, start_ref, *rest):
@@ -158,8 +162,8 @@
         whole,
         jax.ShapeDtypeStruct(start.shape, F32),
         [pltpu.VMEM((total, block * zs), BF16)] * 2,
-        vmem=20,
-    )(place, start, *flat)
+        vmem=60,
+    )(place, start, *in_hbm(*flat))
 
 
 def inverse_factor(small):
@@ -227,7 +231,7 @@
         pl.BlockSpec(start.shape, lambda i, place: (0, 0)),
         jax.ShapeDtypeStruct(start.shape, F32),
         [pltpu.VMEM((count * size, width), F32)],
-        vmem=12,
+        vmem=60,
     )(place, pieces, start)
 
 
@@ -294,10 +298,10 @@
         (total // block,),
         [pl.BlockSpec(basis.shape, lambda i, place: (0, 0))] + specs,
         [pl.BlockSpec((block, zs // 2, rank), lambda i, place: (i, 0, 0))] * 2,
-        [jax.ShapeDtypeStruct((total, zs // 2, rank), F32)] * 2,
+        [pltpu.HBM((total, zs // 2, rank), F32)] * 2,
         [pltpu.VMEM((basis.shape[0], 2 * rank), BF16)],
-        vmem=36,
-    )(place, basis, *flat)
+        vmem=60,
+    )(place, basis, *in_hbm(*flat))
 
 
 def after(value, *earlier):
@@ -344,6 +348,8 @@
         at += size
     jobs.append((1, 0, xs, R_PARTS))
     keeps, sends, came, lines = [], [], [], []
+    grams = [jnp.zeros((len(PAIRS) * xs * 2, xs * 2), F32)]
+    count = len(X_PARTS)
 
     def spread(i):
         mine = add_up(place, keeps[i], came[i])
@@ -352,10 +358,17 @@
             part = after(mine[d], lines[-1][earlier]) if lines else mine[d]
             line[d] = z_swap(part, d)
         lines.append(line)
+        if i >= count - 1:
+            group = [[old[d] for old in lines[:count]] for d in range(4)] if i == count - 1 else [[part] for part in line]
+            grams.append(add_gram(place, grams[-1], group))
 
     def exchange(part):
         i = len(came)
-        earlier = came[i - 2 : i - 1] + (lines[i - 3][1:] if i >= 3 else []) if i >= 2 else []
+        earlier = []
+        if i >= 2:
+            earlier = [came[i - 2]] + (lines[i - 3][1:] if i >= 3 else [])
+        if i >= count + 3:
+            earlier.append(grams[i - count - 2])
         came.append(pair_swap(after(part, *earlier), 2))
         if i >= 1:
             spread(i - 1)
@@ -377,14 +390,9 @@
             exchange(part)
     spread(len(keeps) - 1)
 
-    gram = jnp.zeros((len(PAIRS) * xs * 2, xs * 2), F32)
-    count = len(X_PARTS)
-    first = [[lines[p][d] for p in range(count)] for d in range(4)]
+    first = [[line[d] for line in lines[:count]] for d in range(4)]
     second = [[[line[d]] for d in range(4)] for line in lines[count:]]
-    gram = add_gram(place, gram, first)
-    for group in second:
-        gram = add_gram(place, gram, group)
-    basis = subspace(place, reduce_gram(place, gram), x_basis)
+    basis = subspace(place, reduce_gram(place, grams[-1]), x_basis)
 
     keep0, send0 = core_of(place, basis, [first])
     came0 = pair_swap(send0, 1)

time: 617 us -> 609 us (0.987)
  Pallas kernels: 130 us -> 210 us
  local copies, waits for them, and re-layouts: 82.4 us -> 39.8 us
  starting transfers between devices: 175 us -> 150 us
  waiting for transfers between devices: 209 us -> 191 us
    unnamed x340 -> x136, local copies, waits for them, and re-layouts: 54.8 us -> 10.4 us
    pallas_call x16, Pallas kernels: 11.3 us -> 52.6 us  [add_up(): call('add_k', add_kernel, (rows // block,), [spec, spec], [out] * 4, [plt...]
    pallas_call x9, Pallas kernels: 22.6 us -> 43.4 us  [add_gram(): call('gram_k', lambda place, *refs: gram_kernel(parts, place, *refs), (ro...]
    ppermute x54, starting transfers between devices: 140 us -> 126 us  [z_swap(): return lax.ppermute(value, 'aa', [(i, i ^ d) for i in range(4)])]
    ppermute x25, starting transfers between devices: 35.1 us -> 24.4 us  [pair_swap(): return lax.ppermute(value, 'ba', [(i, i ^ distance) for i in range(4)])]
    pallas_call x9, Pallas kernels: 59.1 us -> 69.7 us  [project(): call('project_k', lambda place, *refs: project_kernel(parts, place, *refs...]
    ppermute x25, waiting for transfers between devices: 52.9 us -> 42.9 us  [pair_swap(): return lax.ppermute(value, 'ba', [(i, i ^ distance) for i in range(4)])]
    ppermute x54, waiting for transfers between devices: 156 us -> 148 us  [z_swap(): return lax.ppermute(value, 'aa', [(i, i ^ d) for i in range(4)])]
  transfers between devices with their start and end apart: 79 -> 79, of which waited for: 35 -> 35; matrix products, arithmetic and copies ran while one was open for 2% -> 3% of each run, Pallas kernels for 15% -> 27%
where the time goes in v3:
time: 609 us; the launch traced here: 599 us
  Pallas kernels  210 us (34%)
  waiting for transfers between devices  191 us (31%)
  starting transfers between devices  150 us (25%)
  local copies, waits for them, and re-layouts  39.8 us (7%)
  other arithmetic  6.4 us (1%)
    ppermute x54, waiting for transfers between devices, z_swap(): return lax.ppermute(value, 'aa', [(i, i ^ d) for i in range(4)])  148 us
    ppermute x54, starting transfers between devices, z_swap(): return lax.ppermute(value, 'aa', [(i, i ^ d) for i in range(4)])  126 us
    pallas_call x9, Pallas kernels, project(): call('project_k', lambda place, *refs: project_kernel(parts, place, *refs...  69.7 us
    pallas_call x16, Pallas kernels, add_up(): call('add_k', add_kernel, (rows // block,), [spec, spec], [out] * 4, [plt...  52.6 us
    pallas_call x9, Pallas kernels, add_gram(): call('gram_k', lambda place, *refs: gram_kernel(parts, place, *refs), (ro...  43.4 us
    ppermute x25, waiting for transfers between devices, pair_swap(): return lax.ppermute(value, 'ba', [(i, i ^ distance) for i in range(4)])  42.9 us
    pallas_call x1, Pallas kernels, subspace(): call('subspace_k', basis_kernel, (1,), [pl.BlockSpec(pieces.shape, lambda...  28 us
    squeeze x3, local copies, waits for them, and re-layouts, fast_body(): lax.dynamic_slice(slab_field, (first, start, 0, 0), (1, size, ys, zs))[0]  25.8 us
  transfers between devices with their start and end apart: 79, of which 35 were waited for; matrix products, arithmetic and copies ran while one was open for 3% of the time, Pallas kernels for 27%

profile of v3, /device:TPU:0, one launch (start us, length us, event | category | flops | bytes accessed | tf_op | source)
XLA Modules:
  0.0 598.5 jit_solution(7553809234536497642)
XLA Ops:
  12.3 12.3 %dynamic-slice_bitcast_fusion.1 = f32[112,128,256]{2,1,0:T(8,128)} fusion(f32[4,128,128,256]{3,2,1,0:T(8,128)} %refs_0_.17, s32[]{:T(128)S(6)} %select_n.83), kind=kLoop, calls=%fused_computation.1 | loop fusion | bytes 29360132 | tf_op jit(solution)/shard_map/squeeze | solution.py:383
  24.9 11.7 %dynamic-slice_bitcast_fusion = f32[128,128,256]{2,1,0:T(8,128)} fusion(f32[4,128,128,256]{3,2,1,0:T(8,128)} %refs_0_.17, s32[]{:T(128)S(6)} %select_n.84), kind=kLoop, calls=%fused_computation | loop fusion | bytes 33554436 | tf_op jit(solution)/shard_map/squeeze | solution.py:383
  39.7 7.4 %collective-permute-done.2.refs_1_ = f32[112,128,256]{2,1,0:T(8,128)} collective-permute-done((f32[112,128,256]{2,1,0:T(8,128)}, f32[112,128,256]{2,1,0:T(8,128)}, u32[]{:S(2)}, u32[]{:S(2)}) %collective-permute-start.2) | collective-permute-done | bytes 14680096 | tf_op jit(solution)/shard_map/ppermute | solution.py:312
  73.1 8.0 %collective-permute-done.5.refs_9_ = f32[32,16,128]{2,1,0:T(8,128)S(1)} collective-permute-done((f32[32,16,128]{2,1,0:T(8,128)}, f32[32,16,128]{2,1,0:T(8,128)S(1)}, u32[]{:S(2)}, u32[]{:S(2)}) %collective-permute-start.5) | collective-permute-done | bytes 262176 | tf_op jit(solution)/shard_map/ppermute | solution.py:316
  101.8 6.8 %collective-permute-done.4.recv_ref = f32[4,32,16,128]{3,2,1,0:T(8,128)S(1)} collective-permute-done((f32[4,32,16,128]{3,2,1,0:T(8,128)}, f32[4,32,16,128]{3,2,1,0:T(8,128)S(1)}, u32[]{:S(2)}, u32[]{:S(2)}) %collective-permute-start.4) | collective-permute-done | bytes 1048608 | tf_op jit(solution)/shard_map/ppermute | solution.py:312
  131.1 10.8 %collective-permute-done.13.refs_11_ = f32[32,16,128]{2,1,0:T(8,128)S(1)} collective-permute-done((f32[32,16,128]{2,1,0:T(8,128)}, f32[32,16,128]{2,1,0:T(8,128)S(1)}, u32[]{:S(2)}, u32[]{:S(2)}) %collective-permute-start.13) | collective-permute-done | bytes 262176 | tf_op jit(solution)/shard_map/ppermute | solution.py:316
  166.7 8.6 %collective-permute-start.21 = (f32[32,16,128]{2,1,0:T(8,128)}, f32[32,16,128]{2,1,0:T(8,128)S(1)}, u32[]{:S(2)}, u32[]{:S(2)}) collective-permute-start(f32[32,16,128]{2,1,0:T(8,128)} %get-tuple-element.214), channel_id=1, source_target_pairs={{0,4},{4,0},{8,12},{12,8},{1,5},{5,1},{9,13},{13,9},{2,6},{6,2},{1... | collective-permute-start | bytes 786440 | tf_op jit(solution)/shard_map/ppermute | solution.py:316
  192.9 9.7 %collective-permute-done.22.refs_21_ = f32[32,16,128]{2,1,0:T(8,128)S(1)} collective-permute-done((f32[32,16,128]{2,1,0:T(8,128)}, f32[32,16,128]{2,1,0:T(8,128)S(1)}, u32[]{:S(2)}, u32[]{:S(2)}) %collective-permute-start.22) | collective-permute-done | bytes 262176 | tf_op jit(solution)/shard_map/ppermute | solution.py:316
  214.8 26.6 %project_k.17 = (f32[4,4,128,128]{3,2,1,0:T(8,128)}, f32[4,4,128,128]{3,2,1,0:T(8,128)}, f32[4,4,128,128]{3,2,1,0:T(8,128)}, f32[4,4,128,128]{3,2,1,0:T(8,128)},...) custom-call(s32[3]{0:T(128)} %pad_add_fusion.place, ...), custom_call_target="tpu_custom_call" | custom-call | tf_op jit(solution)/shard_map/project_k/pallas_call | solution.py:89
  250.1 7.9 %collective-permute-done.27.refs_15_ = f32[32,16,128]{2,1,0:T(8,128)S(1)} collective-permute-done((f32[32,16,128]{2,1,0:T(8,128)}, f32[32,16,128]{2,1,0:T(8,128)S(1)}, u32[]{:S(2)}, u32[]{:S(2)}) %collective-permute-start.27) | collective-permute-done | bytes 262176 | tf_op jit(solution)/shard_map/ppermute | solution.py:316
  263.0 8.3 %collective-permute-done.31.refs_23_ = f32[32,16,128]{2,1,0:T(8,128)S(1)} collective-permute-done((f32[32,16,128]{2,1,0:T(8,128)}, f32[32,16,128]{2,1,0:T(8,128)S(1)}, u32[]{:S(2)}, u32[]{:S(2)}) %collective-permute-start.31) | collective-permute-done | bytes 262176 | tf_op jit(solution)/shard_map/ppermute | solution.py:316
  279.9 5.7 collective-permute-done.30.refs_16_
  285.7 10.1 %collective-permute-done.32.refs_24_ = f32[32,16,128]{2,1,0:T(8,128)S(1)} collective-permute-done((f32[32,16,128]{2,1,0:T(8,128)}, f32[32,16,128]{2,1,0:T(8,128)S(1)}, u32[]{:S(2)}, u32[]{:S(2)}) %collective-permute-start.32) | collective-permute-done | bytes 262176 | tf_op jit(solution)/shard_map/ppermute | solution.py:316
  306.7 11.8 %gram_k.9.refs_0_ = f32[768,256]{1,0:T(8,128)} custom-call(s32[3]{0:T(128)} %pad_add_fusion.place, f32[768,256]{1,0:T(8,128)} %broadcast_in_dim.3.refs_0_, f32[32,16,128]{2,1,0:T(8,128)} %get-tuple-element.165.refs_1_, f32[32,16,128]{2,1,0:T(8,128)} %get-tuple-element.169.refs_2_, f32[32,16,128]{2,1,0:T(8,128)} %get-tuple-element.173.refs_3_, ...), custom_call_target="tpu_custom_call" | custom-call | tf_op jit(solution)/shard_map/gram_k/pallas_call | solution.py:157
  340.2 12.5 %collective-permute-done.41.refs_3_.refs_7_ = f32[4,128,128]{2,1,0:T(8,128)S(1)} collective-permute-done((f32[4,128,128]{2,1,0:T(8,128)}, f32[4,128,128]{2,1,0:T(8,128)S(1)}, u32[]{:S(2)}, u32[]{:S(2)}) %collective-permute-start.41) | collective-permute-done | bytes 262176 | tf_op jit(solution)/shard_map/ppermute | solution.py:316
  369.4 12.5 %collective-permute-done.45.refs_3_.refs_11_ = f32[4,128,128]{2,1,0:T(8,128)S(1)} collective-permute-done((f32[4,128,128]{2,1,0:T(8,128)}, f32[4,128,128]{2,1,0:T(8,128)S(1)}, u32[]{:S(2)}, u32[]{:S(2)}) %collective-permute-start.45) | collective-permute-done | bytes 262176 | tf_op jit(solution)/shard_map/ppermute | solution.py:316
  407.2 14.1 %collective-permute-done.49.refs_3_.refs_15_ = f32[4,128,128]{2,1,0:T(8,128)S(1)} collective-permute-done((f32[4,128,128]{2,1,0:T(8,128)}, f32[4,128,128]{2,1,0:T(8,128)S(1)}, u32[]{:S(2)}, u32[]{:S(2)}) %collective-permute-start.49) | collective-permute-done | bytes 262176 | tf_op jit(solution)/shard_map/ppermute | solution.py:316
  441.3 7.8 %collective-permute-done.59.recv_ref = f32[4,4,128,128]{3,2,1,0:T(8,128)S(1)} collective-permute-done((f32[4,4,128,128]{3,2,1,0:T(8,128)}, f32[4,4,128,128]{3,2,1,0:T(8,128)S(1)}, u32[]{:S(2)}, u32[]{:S(2)}) %collective-permute-start.59) | collective-permute-done | bytes 1048608 | tf_op jit(solution)/shard_map/ppermute | solution.py:312
  460.0 9.0 %collective-permute-start.60 = (f32[4,128,128]{2,1,0:T(8,128)}, f32[4,128,128]{2,1,0:T(8,128)S(1)}, u32[]{:S(2)}, u32[]{:S(2)}) collective-permute-start(f32[4,128,128]{2,1,0:T(8,128)} %get-tuple-element.305), channel_id=1, source_target_pairs={{0,4},{4,0},{8,12},{12,8},{1,5},{5,1},{9,13},{13,9},{2,6},{6,2},{1... | collective-permute-start | bytes 786440 | tf_op jit(solution)/shard_map/ppermute | solution.py:316
  478.3 15.4 %collective-permute-done.61.refs_3_.refs_27_ = f32[4,128,128]{2,1,0:T(8,128)S(1)} collective-permute-done((f32[4,128,128]{2,1,0:T(8,128)}, f32[4,128,128]{2,1,0:T(8,128)S(1)}, u32[]{:S(2)}, u32[]{:S(2)}) %collective-permute-start.61) | collective-permute-done | bytes 262176 | tf_op jit(solution)/shard_map/ppermute | solution.py:316
  515.2 6.2 %collective-permute-done.68 = f32[192,256]{1,0:T(8,128)S(1)} collective-permute-done((f32[192,256]{1,0:T(8,128)S(1)}, f32[192,256]{1,0:T(8,128)S(1)}, u32[]{:S(2)}, u32[]{:S(2)}) %collective-permute-start.68) | collective-permute-done | bytes 196640 | tf_op jit(solution)/shard_map/ppermute | solution.py:312
  547.0 28.0 %subspace_k.1.refs_0_ = f32[512,128]{1,0:T(8,128)} custom-call(s32[3]{0:T(128)} %pad_add_fusion.place, f32[16,48,256]{2,1,0:T(8,128)} %copy-done.62, f32[512,128]{1,0:T(8,128)} %start_ref.1), custom_call_target="tpu_custom_call" | custom-call | tf_op jit(solution)/shard_map/subspace_k/pallas_call | solution.py:223
  575.0 8.6 %core_k.3 = (f32[32,64,128]{2,1,0:T(8,128)}, f32[32,64,128]{2,1,0:T(8,128)}) custom-call(s32[3]{0:T(128)} %pad_add_fusion.place, f32[512,128]{1,0:T(8,128)} %subspace_k.1.refs_0_, f32[4,128,128]{2,1,0:T(8,128)} %get-tuple-element.243.refs_1_, f32[4,128,128]{2,1,0:T(8,128)} %copy-done.39, f32[4,128,128]{2,1,0:T(8,128)} %copy-done.40, ...), custom_call_target="tpu_custom_call" | custom-call | tf_op jit(solution)/shard_map/core_k/pallas_call | solution.py:295
  583.8 7.6 %core_k.2 = (f32[32,64,128]{2,1,0:T(8,128)}, f32[32,64,128]{2,1,0:T(8,128)}) custom-call(s32[3]{0:T(128)} %pad_add_fusion.place, f32[512,128]{1,0:T(8,128)} %subspace_k.1.refs_0_, f32[32,16,128]{2,1,0:T(8,128)} %get-tuple-element.165.refs_1_, f32[32,16,128]{2,1,0:T(8,128)} %get-tuple-element.169.refs_2_, f32[32,16,128]{2,1,0:T(8,128)} %get-tuple-element.173.refs_3_, ...), custom_call_target="tpu_custom_call" | custom-call | tf_op jit(solution)/shard_map/core_k/pallas_call | solution.py:295
  (327 shorter events, 329.5 us)
Async XLA Ops:
  36.7 177.8 %collective-permute-start.34 = (f32[128,128,256]{2,1,0:T(8,128)}, f32[128,128,256]{2,1,0:T(8,128)}, u32[]{:S(2)}, u32[]{:S(2)}) collective-permute-start(f32[128,128,256]{2,1,0:T(8,128)} %dynamic-slice_bitcast_fusion), channel_id=1, source_target_pairs={{0,1},{1,0},{2,3},{3,2},{4,5},{5,4},{6,7},{7,6},{8,9},{9,8},{10,11... | collective-permute-start | bytes 50331656 | tf_op jit(solution)/shard_map/ppermute | solution.py:312
  36.8 26.8 %collective-permute-start.1 = (f32[4,32,16,128]{3,2,1,0:T(8,128)S(1)}, f32[4,32,16,128]{3,2,1,0:T(8,128)S(1)}, u32[]{:S(2)}, u32[]{:S(2)}) collective-permute-start(f32[4,32,16,128]{3,2,1,0:T(8,128)S(1)} %copy-done.64), channel_id=1, source_target_pairs={{0,2},{1,3},{2,0},{3,1},{4,6},{5,7},{6,4},{7,5},{8,10},{9,11},{10,... | collective-permute-start | bytes 3145736 | tf_op jit(solution)/shard_map/ppermute | solution.py:312
  52.4 37.1 %collective-permute-start.3 = (f32[4,32,16,128]{3,2,1,0:T(8,128)}, f32[4,32,16,128]{3,2,1,0:T(8,128)S(1)}, u32[]{:S(2)}, u32[]{:S(2)}) collective-permute-start(f32[4,32,16,128]{3,2,1,0:T(8,128)} %get-tuple-element.168), channel_id=1, source_target_pairs={{0,2},{1,3},{2,0},{3,1},{4,6},{5,7},{6,4},{7,5},{8,10},{9,11},{10,... | collective-permute-start | bytes 3145736 | tf_op jit(solution)/shard_map/ppermute | solution.py:312
  63.6 44.9 %collective-permute-start.4 = (f32[4,32,16,128]{3,2,1,0:T(8,128)}, f32[4,32,16,128]{3,2,1,0:T(8,128)S(1)}, u32[]{:S(2)}, u32[]{:S(2)}) collective-permute-start(f32[4,32,16,128]{3,2,1,0:T(8,128)} %get-tuple-element.172), channel_id=1, source_target_pairs={{0,2},{1,3},{2,0},{3,1},{4,6},{5,7},{6,4},{7,5},{8,10},{9,11},{10,... | collective-permute-start | bytes 3145736 | tf_op jit(solution)/shard_map/ppermute | solution.py:312
  90.6 59.8 %collective-permute-start.8 = (f32[4,32,16,128]{3,2,1,0:T(8,128)}, f32[4,32,16,128]{3,2,1,0:T(8,128)S(1)}, u32[]{:S(2)}, u32[]{:S(2)}) collective-permute-start(f32[4,32,16,128]{3,2,1,0:T(8,128)} %get-tuple-element.179), channel_id=1, source_target_pairs={{0,2},{1,3},{2,0},{3,1},{4,6},{5,7},{6,4},{7,5},{8,10},{9,11},{10,... | collective-permute-start | bytes 3145736 | tf_op jit(solution)/shard_map/ppermute | solution.py:312
  121.9 41.4 %collective-permute-start.12 = (f32[4,32,16,128]{3,2,1,0:T(8,128)}, f32[4,32,16,128]{3,2,1,0:T(8,128)}, u32[]{:S(2)}, u32[]{:S(2)}) collective-permute-start(f32[4,32,16,128]{3,2,1,0:T(8,128)} %get-tuple-element.189), channel_id=1, source_target_pairs={{0,2},{1,3},{2,0},{3,1},{4,6},{5,7},{6,4},{7,5},{8,10},{9,11},{10,... | collective-permute-start | bytes 3145736 | tf_op jit(solution)/shard_map/ppermute | solution.py:312
  151.4 51.2 %collective-permute-start.16 = (f32[4,32,16,128]{3,2,1,0:T(8,128)}, f32[4,32,16,128]{3,2,1,0:T(8,128)S(1)}, u32[]{:S(2)}, u32[]{:S(2)}) collective-permute-start(f32[4,32,16,128]{3,2,1,0:T(8,128)} %get-tuple-element.199), channel_id=1, source_target_pairs={{0,2},{1,3},{2,0},{3,1},{4,6},{5,7},{6,4},{7,5},{8,10},{9,11},{10,... | collective-permute-start | bytes 3145736 | tf_op jit(solution)/shard_map/ppermute | solution.py:312
  181.3 60.1 %collective-permute-start.20 = (f32[4,32,16,128]{3,2,1,0:T(8,128)}, f32[4,32,16,128]{3,2,1,0:T(8,128)S(1)}, u32[]{:S(2)}, u32[]{:S(2)}) collective-permute-start(f32[4,32,16,128]{3,2,1,0:T(8,128)} %get-tuple-element.209), channel_id=1, source_target_pairs={{0,2},{1,3},{2,0},{3,1},{4,6},{5,7},{6,4},{7,5},{8,10},{9,11},{10,... | collective-permute-start | bytes 3145736 | tf_op jit(solution)/shard_map/ppermute | solution.py:312
  203.7 67.6 %collective-permute-start.24 = (f32[4,32,16,128]{3,2,1,0:T(8,128)}, f32[4,32,16,128]{3,2,1,0:T(8,128)S(1)}, u32[]{:S(2)}, u32[]{:S(2)}) collective-permute-start(f32[4,32,16,128]{3,2,1,0:T(8,128)} %get-tuple-element.219), channel_id=1, source_target_pairs={{0,2},{1,3},{2,0},{3,1},{4,6},{5,7},{6,4},{7,5},{8,10},{9,11},{10,... | collective-permute-start | bytes 3145736 | tf_op jit(solution)/shard_map/ppermute | solution.py:312
  208.2 33.3 %collective-permute-start.25 = (f32[32,16,128]{2,1,0:T(8,128)}, f32[32,16,128]{2,1,0:T(8,128)S(1)}, u32[]{:S(2)}, u32[]{:S(2)}) collective-permute-start(f32[32,16,128]{2,1,0:T(8,128)} %get-tuple-element.222), channel_id=1, source_target_pairs={{0,4},{4,0},{8,12},{12,8},{1,5},{5,1},{9,13},{13,9},{2,6},{6,2},{1... | collective-permute-start | bytes 786440 | tf_op jit(solution)/shard_map/ppermute | solution.py:316
  213.3 28.2 %collective-permute-start.26 = (f32[32,16,128]{2,1,0:T(8,128)}, f32[32,16,128]{2,1,0:T(8,128)S(1)}, u32[]{:S(2)}, u32[]{:S(2)}) collective-permute-start(f32[32,16,128]{2,1,0:T(8,128)} %get-tuple-element.225), channel_id=1, source_target_pairs={{0,12},{4,8},{8,4},{12,0},{1,13},{5,9},{9,5},{13,1},{2,14},{6,10},... | collective-permute-start | bytes 786440 | tf_op jit(solution)/shard_map/ppermute | solution.py:316
  214.5 27.0 %collective-permute-start.28 = (f32[32,16,128]{2,1,0:T(8,128)}, f32[32,16,128]{2,1,0:T(8,128)S(1)}, u32[]{:S(2)}, u32[]{:S(2)}) collective-permute-start(f32[32,16,128]{2,1,0:T(8,128)} %get-tuple-element.230), channel_id=1, source_target_pairs={{0,8},{4,12},{8,0},{12,4},{1,9},{5,13},{9,1},{13,5},{2,10},{6,14},... | collective-permute-start | bytes 786440 | tf_op jit(solution)/shard_map/ppermute | solution.py:316
  241.5 54.3 %collective-permute-start.35 = (f32[4,4,128,128]{3,2,1,0:T(8,128)}, f32[4,4,128,128]{3,2,1,0:T(8,128)}, u32[]{:S(2)}, u32[]{:S(2)}) collective-permute-start(f32[4,4,128,128]{3,2,1,0:T(8,128)} %get-tuple-element.242), channel_id=1, source_target_pairs={{0,2},{1,3},{2,0},{3,1},{4,6},{5,7},{6,4},{7,5},{8,10},{9,11},{10,... | collective-permute-start | bytes 3145736 | tf_op jit(solution)/shard_map/ppermute | solution.py:312
  271.3 52.1 %collective-permute-start.39 = (f32[4,4,128,128]{3,2,1,0:T(8,128)}, f32[4,4,128,128]{3,2,1,0:T(8,128)}, u32[]{:S(2)}, u32[]{:S(2)}) collective-permute-start(f32[4,4,128,128]{3,2,1,0:T(8,128)} %get-tuple-element.252), channel_id=1, source_target_pairs={{0,2},{1,3},{2,0},{3,1},{4,6},{5,7},{6,4},{7,5},{8,10},{9,11},{10,... | collective-permute-start | bytes 3145736 | tf_op jit(solution)/shard_map/ppermute | solution.py:312
  295.8 56.8 %collective-permute-start.43 = (f32[4,4,128,128]{3,2,1,0:T(8,128)}, f32[4,4,128,128]{3,2,1,0:T(8,128)S(1)}, u32[]{:S(2)}, u32[]{:S(2)}) collective-permute-start(f32[4,4,128,128]{3,2,1,0:T(8,128)} %get-tuple-element.262), channel_id=1, source_target_pairs={{0,2},{1,3},{2,0},{3,1},{4,6},{5,7},{6,4},{7,5},{8,10},{9,11},{10,... | collective-permute-start | bytes 3145736 | tf_op jit(solution)/shard_map/ppermute | solution.py:312
  324.1 57.8 %collective-permute-start.47 = (f32[4,4,128,128]{3,2,1,0:T(8,128)}, f32[4,4,128,128]{3,2,1,0:T(8,128)S(1)}, u32[]{:S(2)}, u32[]{:S(2)}) collective-permute-start(f32[4,4,128,128]{3,2,1,0:T(8,128)} %get-tuple-element.272), channel_id=1, source_target_pairs={{0,2},{1,3},{2,0},{3,1},{4,6},{5,7},{6,4},{7,5},{8,10},{9,11},{10,... | collective-permute-start | bytes 3145736 | tf_op jit(solution)/shard_map/ppermute | solution.py:312
  352.7 43.8 %collective-permute-start.51 = (f32[4,4,128,128]{3,2,1,0:T(8,128)}, f32[4,4,128,128]{3,2,1,0:T(8,128)S(1)}, u32[]{:S(2)}, u32[]{:S(2)}) collective-permute-start(f32[4,4,128,128]{3,2,1,0:T(8,128)} %get-tuple-element.282), channel_id=1, source_target_pairs={{0,2},{1,3},{2,0},{3,1},{4,6},{5,7},{6,4},{7,5},{8,10},{9,11},{10,... | collective-permute-start | bytes 3145736 | tf_op jit(solution)/shard_map/ppermute | solution.py:312
  382.6 47.1 %collective-permute-start.55 = (f32[4,4,128,128]{3,2,1,0:T(8,128)}, f32[4,4,128,128]{3,2,1,0:T(8,128)S(1)}, u32[]{:S(2)}, u32[]{:S(2)}) collective-permute-start(f32[4,4,128,128]{3,2,1,0:T(8,128)} %get-tuple-element.292), channel_id=1, source_target_pairs={{0,2},{1,3},{2,0},{3,1},{4,6},{5,7},{6,4},{7,5},{8,10},{9,11},{10,... | collective-permute-start | bytes 3145736 | tf_op jit(solution)/shard_map/ppermute | solution.py:312
  392.5 28.7 %collective-permute-start.49 = (f32[4,128,128]{2,1,0:T(8,128)}, f32[4,128,128]{2,1,0:T(8,128)S(1)}, u32[]{:S(2)}, u32[]{:S(2)}) collective-permute-start(f32[4,128,128]{2,1,0:T(8,128)} %get-tuple-element.277), channel_id=1, source_target_pairs={{0,8},{4,12},{8,0},{12,4},{1,9},{5,13},{9,1},{13,5},{2,10},{6,14},... | collective-permute-start | bytes 786440 | tf_op jit(solution)/shard_map/ppermute | solution.py:316
  400.8 28.2 %collective-permute-start.52 = (f32[4,128,128]{2,1,0:T(8,128)}, f32[4,128,128]{2,1,0:T(8,128)S(1)}, u32[]{:S(2)}, u32[]{:S(2)}) collective-permute-start(f32[4,128,128]{2,1,0:T(8,128)} %get-tuple-element.285), channel_id=1, source_target_pairs={{0,4},{4,0},{8,12},{12,8},{1,5},{5,1},{9,13},{13,9},{2,6},{6,2},{1... | collective-permute-start | bytes 786440 | tf_op jit(solution)/shard_map/ppermute | solution.py:316
  430.5 39.9 %collective-permute-start.63 = (f32[4,4,128,128]{3,2,1,0:T(8,128)}, f32[4,4,128,128]{3,2,1,0:T(8,128)S(1)}, u32[]{:S(2)}, u32[]{:S(2)}) collective-permute-start(f32[4,4,128,128]{3,2,1,0:T(8,128)} %get-tuple-element.312), channel_id=1, source_target_pairs={{0,2},{1,3},{2,0},{3,1},{4,6},{5,7},{6,4},{7,5},{8,10},{9,11},{10,... | collective-permute-start | bytes 3145736 | tf_op jit(solution)/shard_map/ppermute | solution.py:312
  441.3 27.7 %collective-permute-start.56 = (f32[4,128,128]{2,1,0:T(8,128)}, f32[4,128,128]{2,1,0:T(8,128)S(1)}, u32[]{:S(2)}, u32[]{:S(2)}) collective-permute-start(f32[4,128,128]{2,1,0:T(8,128)} %get-tuple-element.295), channel_id=1, source_target_pairs={{0,4},{4,0},{8,12},{12,8},{1,5},{5,1},{9,13},{13,9},{2,6},{6,2},{1... | collective-permute-start | bytes 786440 | tf_op jit(solution)/shard_map/ppermute | solution.py:316
  474.7 31.0 %collective-permute-start.64 = (f32[4,128,128]{2,1,0:T(8,128)}, f32[4,128,128]{2,1,0:T(8,128)S(1)}, u32[]{:S(2)}, u32[]{:S(2)}) collective-permute-start(f32[4,128,128]{2,1,0:T(8,128)} %get-tuple-element.315), channel_id=1, source_target_pairs={{0,4},{4,0},{8,12},{12,8},{1,5},{5,1},{9,13},{13,9},{2,6},{6,2},{1... | collective-permute-start | bytes 786440 | tf_op jit(solution)/shard_map/ppermute | solution.py:316
  477.5 28.2 %collective-permute-start.65 = (f32[4,128,128]{2,1,0:T(8,128)}, f32[4,128,128]{2,1,0:T(8,128)S(1)}, u32[]{:S(2)}, u32[]{:S(2)}) collective-permute-start(f32[4,128,128]{2,1,0:T(8,128)} %get-tuple-element.317), channel_id=1, source_target_pairs={{0,8},{4,12},{8,0},{12,4},{1,9},{5,13},{9,1},{13,5},{2,10},{6,14},... | collective-permute-start | bytes 786440 | tf_op jit(solution)/shard_map/ppermute | solution.py:316
  (120 other events, 1835.8 us)

commit v4 on v3

--- a/solution.py
+++ b/solution.py
@@ -92,10 +92,10 @@
         (steps,),
         in_specs,
         out_specs,
-        [pltpu.HBM(s, F32) for s in shapes],
+        [jax.ShapeDtypeStruct(s, F32) for s in shapes],
         [pltpu.VMEM((2 * rank, 2 * ys), BF16)],
-        vmem=60,
-    )(place, *in_hbm(field, other), basis)
+        vmem=18,
+    )(place, field, other, basis)
     count = len(parts)
     return result[:count], result[count:]
 
@@ -119,9 +119,9 @@
         (rows // block,),
         [spec, spec],
         [out] * 4,
-        [pltpu.HBM((rows, xs, zs), F32)] * 4,
-        vmem=60,
-    )(place, *in_hbm(keep, recv))
+        [jax.ShapeDtypeStruct((rows, xs, zs), F32)] * 4,
+        vmem=12,
+    )(place, keep, recv)
 
 
 def gram_kernel(parts, place, start_ref, *rest):
@@ -162,35 +162,48 @@
         whole,
         jax.ShapeDtypeStruct(start.shape, F32),
         [pltpu.VMEM((total, block * zs), BF16)] * 2,
-        vmem=60,
+        vmem=20,
     )(place, start, *in_hbm(*flat))
 
 
 def inverse_factor(small):
     n = small.shape[0]
+    shape = (8, n)
     rows = lax.broadcasted_iota(jnp.int32, (n, n), 0)
     cols = lax.broadcasted_iota(jnp.int32, (n, n), 1)
     unit = jnp.where(rows == cols, 1.0, 0.0).astype(F32)
-    tiles = [small[8 * t : 8 * t + 8] for t in range(n // 8)]
-    units = [unit[8 * t : 8 * t + 8] for t in range(n // 8)]
-    sub = lax.broadcasted_iota(jnp.int32, (8, n), 0)
-    done = [None] * (n // 8)
-    for j in range(n):
-        at, r = divmod(j, 8)
-        row, unit_row = tiles[at][r : r + 1], units[at][r : r + 1]
-        pivot = row[:, j : j + 1]
-        inverse = 1.0 / pivot
-        scale = lax.rsqrt(pivot)
-        scaled = row * inverse
-        for t in range(at, n // 8):
-            column = tiles[t][:, j : j + 1]
-            if t == at:
-                column = jnp.where(sub[:, 0:1] > r, column, 0.0)
-            factor = column * inverse
-            tiles[t] = tiles[t] - factor * row
-            units[t] = units[t] - factor * unit_row
-        piece = jnp.where(sub == r, unit_row * scale, 0.0)
-        done[at] = piece if r == 0 else done[at] + piece
+    tiles = [small[t : t + 8] for t in range(0, n, 8)]
+    units = [unit[t : t + 8] for t in range(0, n, 8)]
+    sub = lax.broadcasted_iota(jnp.int32, shape, 0)
+    along_row = lambda tile, j: jnp.broadcast_to(tile[:, j : j + 1], shape)
+    spread = lambda tile, i: jnp.broadcast_to(tile[i : i + 1], shape)
+    done = []
+    for b in range(n // 8):
+        columns = [along_row(tiles[b], 8 * b + k) for k in range(8)]
+        entry = [[spread(columns[k], i) if i >= k else None for k in range(8)] for i in range(8)]
+        row = [spread(tiles[b], i) for i in range(8)]
+        unit_row = [spread(units[b], i) for i in range(8)]
+        inverse, factor = [None] * 8, [[None] * 8 for _ in range(8)]
+        for k in range(8):
+            inverse[k] = 1.0 / entry[k][k]
+            for i in range(k + 1, 8):
+                factor[i][k] = entry[i][k] * inverse[k]
+                for j in range(k + 1, i + 1):
+                    entry[i][j] = entry[i][j] - factor[i][k] * entry[j][k]
+                row[i] = row[i] - factor[i][k] * row[k]
+                unit_row[i] = unit_row[i] - factor[i][k] * unit_row[k]
+        result = jnp.zeros(shape, F32)
+        for k in range(8):
+            result = jnp.where(sub == k, unit_row[k] * lax.rsqrt(entry[k][k]), result)
+        done.append(result)
+        for t in range(b + 1, n // 8):
+            column = [along_row(tiles[t], 8 * b + k) for k in range(8)]
+            for k in range(8):
+                for m in range(k):
+                    column[k] = column[k] - factor[k][m] * column[m]
+                scaled = column[k] * inverse[k]
+                tiles[t] = tiles[t] - scaled * row[k]
+                units[t] = units[t] - scaled * unit_row[k]
     return jnp.concatenate(done, axis=0)
 
 
@@ -208,14 +221,17 @@
     half = gram_ref.shape[1]
     g00, g10, g11 = (gram_ref[i * half : (i + 1) * half, :] for i in range(3))
     g01 = g10.T
-    basis = start_ref[...]
-    for _ in range(ITERS):
-        top, low = basis[:half], basis[half:]
-        dot = lambda a, b: jnp.dot(a, b, precision=HIGHEST, preferred_element_type=F32)
+    dot = lambda a, b: jnp.dot(a, b, precision=HIGHEST, preferred_element_type=F32)
+    out_ref[...] = start_ref[...]
+
+    def iterate(_, carry):
+        top, low = out_ref[:half], out_ref[half:]
         images = jnp.concatenate([dot(g00, top) + dot(g01, low), dot(g10, top) + dot(g11, low)], axis=0)
         small = dot(images.T, images)
-        basis = dot(images, inverse_factor(small).T)
-    out_ref[...] = basis
+        out_ref[...] = dot(images, inverse_factor(small).T)
+        return carry
+
+    lax.fori_loop(0, ITERS, iterate, 0)
 
 
 def subspace(place, pieces, start):
@@ -231,7 +247,7 @@
         pl.BlockSpec(start.shape, lambda i, place: (0, 0)),
         jax.ShapeDtypeStruct(start.shape, F32),
         [pltpu.VMEM((count * size, width), F32)],
-        vmem=60,
+        vmem=12,
     )(place, pieces, start)
 
 
@@ -300,7 +316,7 @@
         [pl.BlockSpec((block, zs // 2, rank), lambda i, place: (i, 0, 0))] * 2,
         [pltpu.HBM((total, zs // 2, rank), F32)] * 2,
         [pltpu.VMEM((basis.shape[0], 2 * rank), BF16)],
-        vmem=60,
+        vmem=36,
     )(place, basis, *in_hbm(*flat))
 
 

time: 609 us -> 557 us (0.915)
  Pallas kernels: 210 us -> 132 us
  starting transfers between devices: 150 us -> 171 us
  waiting for transfers between devices: 191 us -> 199 us
    pallas_call x16, Pallas kernels: 52.6 us -> 10.4 us  [add_up(): call('add_k', add_kernel, (rows // block,), [spec, spec], [out] * 4, [jax...]
    ppermute x54, starting transfers between devices: 126 us -> 146 us  [z_swap(): return lax.ppermute(value, 'aa', [(i, i ^ d) for i in range(4)])]
    pallas_call x1, Pallas kernels: 28 us -> 14.8 us  [subspace(): call('subspace_k', basis_kernel, (1,), [pl.BlockSpec(pieces.shape, lambda...]
    pallas_call x9, Pallas kernels: 43.4 us -> 32.4 us  [add_gram(): call('gram_k', lambda place, *refs: gram_kernel(parts, place, *refs), (ro...]
    pallas_call x9, Pallas kernels: 69.7 us -> 59.2 us  [project(): call('project_k', lambda place, *refs: project_kernel(parts, place, *refs...]
    ppermute x54, waiting for transfers between devices: 148 us -> 155 us  [z_swap(): return lax.ppermute(value, 'aa', [(i, i ^ d) for i in range(4)])]
  transfers between devices with their start and end apart: 79 -> 79, of which waited for: 35 -> 36; matrix products, arithmetic and copies ran while one was open for 3% -> 3% of each run, Pallas kernels for 27% -> 19%
where the time goes in v4:
time: 557 us; the launch traced here: 548 us
  waiting for transfers between devices  199 us (36%)
  starting transfers between devices  171 us (31%)
  Pallas kernels  132 us (24%)
  local copies, waits for them, and re-layouts  38.4 us (7%)
  other arithmetic  5.67 us (1%)
    ppermute x54, waiting for transfers between devices, z_swap(): return lax.ppermute(value, 'aa', [(i, i ^ d) for i in range(4)])  155 us
    ppermute x54, starting transfers between devices, z_swap(): return lax.ppermute(value, 'aa', [(i, i ^ d) for i in range(4)])  146 us
    pallas_call x9, Pallas kernels, project(): call('project_k', lambda place, *refs: project_kernel(parts, place, *refs...  59.2 us
    ppermute x25, waiting for transfers between devices, pair_swap(): return lax.ppermute(value, 'ba', [(i, i ^ distance) for i in range(4)])  43.7 us
    pallas_call x9, Pallas kernels, add_gram(): call('gram_k', lambda place, *refs: gram_kernel(parts, place, *refs), (ro...  32.4 us
    squeeze x3, local copies, waits for them, and re-layouts, fast_body(): lax.dynamic_slice(slab_field, (first, start, 0, 0), (1, size, ys, zs))[0]  27.2 us
    ppermute x25, starting transfers between devices, pair_swap(): return lax.ppermute(value, 'ba', [(i, i ^ distance) for i in range(4)])  24.9 us
    pallas_call x2, Pallas kernels, core_of(): call('core_k', lambda place, *refs: core_kernel([len(group) for group in...  15.4 us
  transfers between devices with their start and end apart: 79, of which 36 were waited for; matrix products, arithmetic and copies ran while one was open for 3% of the time, Pallas kernels for 19%

profile of v4, /device:TPU:0, one launch (start us, length us, event | category | flops | bytes accessed | tf_op | source)
XLA Modules:
  0.0 547.9 jit_solution(2474842684423545940)
XLA Ops:
  13.3 12.3 %dynamic-slice_bitcast_fusion.1 = f32[112,128,256]{2,1,0:T(8,128)} fusion(f32[4,128,128,256]{3,2,1,0:T(8,128)} %refs_0_.17, s32[]{:T(128)S(6)} %select_n.83), kind=kLoop, calls=%fused_computation.1 | loop fusion | bytes 29360132 | tf_op jit(solution)/shard_map/squeeze | solution.py:399
  26.0 11.8 %dynamic-slice_bitcast_fusion = f32[128,128,256]{2,1,0:T(8,128)} fusion(f32[4,128,128,256]{3,2,1,0:T(8,128)} %refs_0_.17, s32[]{:T(128)S(6)} %select_n.84), kind=kLoop, calls=%fused_computation | loop fusion | bytes 33554436 | tf_op jit(solution)/shard_map/squeeze | solution.py:399
  40.8 7.4 %collective-permute-done.2.refs_1_ = f32[112,128,256]{2,1,0:T(8,128)} collective-permute-done((f32[112,128,256]{2,1,0:T(8,128)}, f32[112,128,256]{2,1,0:T(8,128)}, u32[]{:S(2)}, u32[]{:S(2)}) %collective-permute-start.2) | collective-permute-done | bytes 14680096 | tf_op jit(solution)/shard_map/ppermute | solution.py:328
  72.3 7.8 %collective-permute-done.5.refs_9_ = f32[32,16,128]{2,1,0:T(8,128)S(1)} collective-permute-done((f32[32,16,128]{2,1,0:T(8,128)S(1)}, f32[32,16,128]{2,1,0:T(8,128)S(1)}, u32[]{:S(2)}, u32[]{:S(2)}) %collective-permute-start.5) | collective-permute-done | bytes 262176 | tf_op jit(solution)/shard_map/ppermute | solution.py:332
  97.2 12.5 %collective-permute-done.4.recv_ref = f32[4,32,16,128]{3,2,1,0:T(8,128)S(1)} collective-permute-done((f32[4,32,16,128]{3,2,1,0:T(8,128)S(1)}, f32[4,32,16,128]{3,2,1,0:T(8,128)S(1)}, u32[]{:S(2)}, u32[]{:S(2)}) %collective-permute-start.4) | collective-permute-done | bytes 1048608 | tf_op jit(solution)/shard_map/ppermute | solution.py:328
  128.0 8.4 %collective-permute-done.13.refs_11_ = f32[32,16,128]{2,1,0:T(8,128)S(1)} collective-permute-done((f32[32,16,128]{2,1,0:T(8,128)S(1)}, f32[32,16,128]{2,1,0:T(8,128)S(1)}, u32[]{:S(2)}, u32[]{:S(2)}) %collective-permute-start.13) | collective-permute-done | bytes 262176 | tf_op jit(solution)/shard_map/ppermute | solution.py:332
  159.6 11.0 %collective-permute-start.21 = (f32[32,16,128]{2,1,0:T(8,128)S(1)}, f32[32,16,128]{2,1,0:T(8,128)S(1)}, u32[]{:S(2)}, u32[]{:S(2)}) collective-permute-start(f32[32,16,128]{2,1,0:T(8,128)S(1)} %get-tuple-element.214), channel_id=1, source_target_pairs={{0,4},{4,0},{8,12},{12,8},{1,5},{5,1},{9,13},{13,9},{2,6},{6,2},{1... | collective-permute-start | bytes 786440 | tf_op jit(solution)/shard_map/ppermute | solution.py:332
  183.9 10.1 %collective-permute-done.22.refs_21_ = f32[32,16,128]{2,1,0:T(8,128)S(1)} collective-permute-done((f32[32,16,128]{2,1,0:T(8,128)S(1)}, f32[32,16,128]{2,1,0:T(8,128)S(1)}, u32[]{:S(2)}, u32[]{:S(2)}) %collective-permute-start.22) | collective-permute-done | bytes 262176 | tf_op jit(solution)/shard_map/ppermute | solution.py:332
  204.2 24.0 %project_k.17 = (f32[4,4,128,128]{3,2,1,0:T(8,128)S(1)}, f32[4,4,128,128]{3,2,1,0:T(8,128)S(1)}, f32[4,4,128,128]{3,2,1,0:T(8,128)S(1)}, f32[4,4,128,128]{3,2,1,...) custom-call(s32[3]{0:T(128)S(1)} %pad_add_fusion.place, ...), custom_call_target="tpu_custom_call" | custom-call | tf_op jit(solution)/shard_map/project_k/pallas_call | solution.py:89
  248.1 8.5 %collective-permute-done.31.refs_23_ = f32[32,16,128]{2,1,0:T(8,128)S(1)} collective-permute-done((f32[32,16,128]{2,1,0:T(8,128)S(1)}, f32[32,16,128]{2,1,0:T(8,128)S(1)}, u32[]{:S(2)}, u32[]{:S(2)}) %collective-permute-start.31) | collective-permute-done | bytes 262176 | tf_op jit(solution)/shard_map/ppermute | solution.py:332
  269.9 8.8 %collective-permute-done.32.refs_24_ = f32[32,16,128]{2,1,0:T(8,128)S(1)} collective-permute-done((f32[32,16,128]{2,1,0:T(8,128)S(1)}, f32[32,16,128]{2,1,0:T(8,128)S(1)}, u32[]{:S(2)}, u32[]{:S(2)}) %collective-permute-start.32) | collective-permute-done | bytes 262176 | tf_op jit(solution)/shard_map/ppermute | solution.py:332
  287.8 10.6 %gram_k.9.refs_0_ = f32[768,256]{1,0:T(8,128)S(1)} custom-call(s32[3]{0:T(128)S(1)} %pad_add_fusion.place, f32[768,256]{1,0:T(8,128)S(1)} %broadcast_in_dim.3.refs_0_, f32[32,16,128]{2,1,0:T(8,128)} %copy-done, f32[32,16,128]{2,1,0:T(8,128)} %copy-done.1, f32[32,16,128]{2,1,0:T(8,128)} %copy-done.2, f32[32,16,128]{2,1,0:T(8,128)} %copy-done.3, ...), custom_call_target="tpu_custom_call" | custom-call | tf_op jit(solution)/shard_map/gram_k/pallas_call | solution.py:157
  320.2 10.4 %collective-permute-done.41.refs_3_.refs_7_ = f32[4,128,128]{2,1,0:T(8,128)S(1)} collective-permute-done((f32[4,128,128]{2,1,0:T(8,128)S(1)}, f32[4,128,128]{2,1,0:T(8,128)S(1)}, u32[]{:S(2)}, u32[]{:S(2)}) %collective-permute-start.41) | collective-permute-done | bytes 262176 | tf_op jit(solution)/shard_map/ppermute | solution.py:332
  345.7 11.3 %collective-permute-done.45.refs_3_.refs_11_ = f32[4,128,128]{2,1,0:T(8,128)S(1)} collective-permute-done((f32[4,128,128]{2,1,0:T(8,128)S(1)}, f32[4,128,128]{2,1,0:T(8,128)S(1)}, u32[]{:S(2)}, u32[]{:S(2)}) %collective-permute-start.45) | collective-permute-done | bytes 262176 | tf_op jit(solution)/shard_map/ppermute | solution.py:332
  372.0 8.3 %collective-permute-start.52 = (f32[4,128,128]{2,1,0:T(8,128)S(1)}, f32[4,128,128]{2,1,0:T(8,128)S(1)}, u32[]{:S(2)}, u32[]{:S(2)}) collective-permute-start(f32[4,128,128]{2,1,0:T(8,128)S(1)} %get-tuple-element.285), channel_id=1, source_target_pairs={{0,4},{4,0},{8,12},{12,8},{1,5},{5,1},{9,13},{13,9},{2,6},{6,2},{1... | collective-permute-start | bytes 786440 | tf_op jit(solution)/shard_map/ppermute | solution.py:332
  380.3 14.7 %collective-permute-done.49.refs_3_.refs_15_ = f32[4,128,128]{2,1,0:T(8,128)S(1)} collective-permute-done((f32[4,128,128]{2,1,0:T(8,128)S(1)}, f32[4,128,128]{2,1,0:T(8,128)S(1)}, u32[]{:S(2)}, u32[]{:S(2)}) %collective-permute-start.49) | collective-permute-done | bytes 262176 | tf_op jit(solution)/shard_map/ppermute | solution.py:332
  404.8 10.6 %collective-permute-start.57 = (f32[4,128,128]{2,1,0:T(8,128)S(1)}, f32[4,128,128]{2,1,0:T(8,128)S(1)}, u32[]{:S(2)}, u32[]{:S(2)}) collective-permute-start(f32[4,128,128]{2,1,0:T(8,128)S(1)} %get-tuple-element.297), channel_id=1, source_target_pairs={{0,8},{4,12},{8,0},{12,4},{1,9},{5,13},{9,1},{13,5},{2,10},{6,14},... | collective-permute-start | bytes 786440 | tf_op jit(solution)/shard_map/ppermute | solution.py:332
  420.1 13.9 %collective-permute-done.57.refs_3_.refs_23_ = f32[4,128,128]{2,1,0:T(8,128)S(1)} collective-permute-done((f32[4,128,128]{2,1,0:T(8,128)S(1)}, f32[4,128,128]{2,1,0:T(8,128)S(1)}, u32[]{:S(2)}, u32[]{:S(2)}) %collective-permute-start.57) | collective-permute-done | bytes 262176 | tf_op jit(solution)/shard_map/ppermute | solution.py:332
  436.4 9.3 %collective-permute-start.60 = (f32[4,128,128]{2,1,0:T(8,128)S(1)}, f32[4,128,128]{2,1,0:T(8,128)S(1)}, u32[]{:S(2)}, u32[]{:S(2)}) collective-permute-start(f32[4,128,128]{2,1,0:T(8,128)S(1)} %get-tuple-element.305), channel_id=1, source_target_pairs={{0,4},{4,0},{8,12},{12,8},{1,5},{5,1},{9,13},{13,9},{2,6},{6,2},{1... | collective-permute-start | bytes 786440 | tf_op jit(solution)/shard_map/ppermute | solution.py:332
  447.1 9.8 %collective-permute-start.64 = (f32[4,128,128]{2,1,0:T(8,128)S(1)}, f32[4,128,128]{2,1,0:T(8,128)}, u32[]{:S(2)}, u32[]{:S(2)}) collective-permute-start(f32[4,128,128]{2,1,0:T(8,128)S(1)} %get-tuple-element.315), channel_id=1, source_target_pairs={{0,4},{4,0},{8,12},{12,8},{1,5},{5,1},{9,13},{13,9},{2,6},{6,2},{1... | collective-permute-start | bytes 786440 | tf_op jit(solution)/shard_map/ppermute | solution.py:332
  457.0 7.8 %collective-permute-done.61.refs_3_.refs_27_ = f32[4,128,128]{2,1,0:T(8,128)S(1)} collective-permute-done((f32[4,128,128]{2,1,0:T(8,128)S(1)}, f32[4,128,128]{2,1,0:T(8,128)S(1)}, u32[]{:S(2)}, u32[]{:S(2)}) %collective-permute-start.61) | collective-permute-done | bytes 262176 | tf_op jit(solution)/shard_map/ppermute | solution.py:332
  510.2 14.8 %subspace_k.1.refs_0_ = f32[512,128]{1,0:T(8,128)S(1)} custom-call(s32[3]{0:T(128)S(1)} %pad_add_fusion.place, f32[16,48,256]{2,1,0:T(8,128)S(1)} %constant_dynamic-update-slice_fusion.5.pieces_ref, f32[512,128]{1,0:T(8,128)S(1)} %copy-done.16), custom_call_target="tpu_custom_call" | custom-call | tf_op jit(solution)/shard_map/subspace_k/pallas_call | solution.py:239
  525.1 8.2 %core_k.3 = (f32[32,64,128]{2,1,0:T(8,128)}, f32[32,64,128]{2,1,0:T(8,128)}) custom-call(s32[3]{0:T(128)S(1)} %pad_add_fusion.place, f32[512,128]{1,0:T(8,128)S(1)} %subspace_k.1.refs_0_, f32[4,128,128]{2,1,0:T(8,128)} %copy-done.8, f32[4,128,128]{2,1,0:T(8,128)} %copy-done.45, f32[4,128,128]{2,1,0:T(8,128)} %copy-done.46, f32[4,128,128]{2,1,0:T(8,128)} %copy-done.47, ...), custom_call_target="tpu_custom_call" | custom-call | tf_op jit(solution)/shard_map/core_k/pallas_call | solution.py:311
  533.5 7.2 %core_k.2 = (f32[32,64,128]{2,1,0:T(8,128)}, f32[32,64,128]{2,1,0:T(8,128)}) custom-call(s32[3]{0:T(128)S(1)} %pad_add_fusion.place, f32[512,128]{1,0:T(8,128)S(1)} %subspace_k.1.refs_0_, f32[32,16,128]{2,1,0:T(8,128)} %copy-done, f32[32,16,128]{2,1,0:T(8,128)} %copy-done.1, f32[32,16,128]{2,1,0:T(8,128)} %copy-done.2, f32[32,16,128]{2,1,0:T(8,128)} %copy-done.3, ...), custom_call_target="tpu_custom_call" | custom-call | tf_op jit(solution)/shard_map/core_k/pallas_call | solution.py:311
  (331 shorter events, 286.4 us)
Async XLA Ops:
  37.8 166.4 %collective-permute-start.34 = (f32[128,128,256]{2,1,0:T(8,128)}, f32[128,128,256]{2,1,0:T(8,128)}, u32[]{:S(2)}, u32[]{:S(2)}) collective-permute-start(f32[128,128,256]{2,1,0:T(8,128)} %dynamic-slice_bitcast_fusion), channel_id=1, source_target_pairs={{0,1},{1,0},{2,3},{3,2},{4,5},{5,4},{6,7},{7,6},{8,9},{9,8},{10,11... | collective-permute-start | bytes 50331656 | tf_op jit(solution)/shard_map/ppermute | solution.py:328
  37.9 26.8 %collective-permute-start.1 = (f32[4,32,16,128]{3,2,1,0:T(8,128)S(1)}, f32[4,32,16,128]{3,2,1,0:T(8,128)S(1)}, u32[]{:S(2)}, u32[]{:S(2)}) collective-permute-start(f32[4,32,16,128]{3,2,1,0:T(8,128)S(1)} %copy-done.18), channel_id=1, source_target_pairs={{0,2},{1,3},{2,0},{3,1},{4,6},{5,7},{6,4},{7,5},{8,10},{9,11},{10,... | collective-permute-start | bytes 3145736 | tf_op jit(solution)/shard_map/ppermute | solution.py:328
  52.5 35.8 %collective-permute-start.3 = (f32[4,32,16,128]{3,2,1,0:T(8,128)S(1)}, f32[4,32,16,128]{3,2,1,0:T(8,128)S(1)}, u32[]{:S(2)}, u32[]{:S(2)}) collective-permute-start(f32[4,32,16,128]{3,2,1,0:T(8,128)S(1)} %get-tuple-element.168), channel_id=1, source_target_pairs={{0,2},{1,3},{2,0},{3,1},{4,6},{5,7},{6,4},{7,5},{8,10},{9,11},{10,... | collective-permute-start | bytes 3145736 | tf_op jit(solution)/shard_map/ppermute | solution.py:328
  64.7 44.9 %collective-permute-start.4 = (f32[4,32,16,128]{3,2,1,0:T(8,128)S(1)}, f32[4,32,16,128]{3,2,1,0:T(8,128)S(1)}, u32[]{:S(2)}, u32[]{:S(2)}) collective-permute-start(f32[4,32,16,128]{3,2,1,0:T(8,128)S(1)} %get-tuple-element.172), channel_id=1, source_target_pairs={{0,2},{1,3},{2,0},{3,1},{4,6},{5,7},{6,4},{7,5},{8,10},{9,11},{10,... | collective-permute-start | bytes 3145736 | tf_op jit(solution)/shard_map/ppermute | solution.py:328
  88.3 59.4 %collective-permute-start.8 = (f32[4,32,16,128]{3,2,1,0:T(8,128)S(1)}, f32[4,32,16,128]{3,2,1,0:T(8,128)S(1)}, u32[]{:S(2)}, u32[]{:S(2)}) collective-permute-start(f32[4,32,16,128]{3,2,1,0:T(8,128)S(1)} %get-tuple-element.179), channel_id=1, source_target_pairs={{0,2},{1,3},{2,0},{3,1},{4,6},{5,7},{6,4},{7,5},{8,10},{9,11},{10,... | collective-permute-start | bytes 3145736 | tf_op jit(solution)/shard_map/ppermute | solution.py:328
  90.6 27.6 %collective-permute-start.9 = (f32[32,16,128]{2,1,0:T(8,128)S(1)}, f32[32,16,128]{2,1,0:T(8,128)S(1)}, u32[]{:S(2)}, u32[]{:S(2)}) collective-permute-start(f32[32,16,128]{2,1,0:T(8,128)S(1)} %get-tuple-element.184), channel_id=1, source_target_pairs={{0,4},{4,0},{8,12},{12,8},{1,5},{5,1},{9,13},{13,9},{2,6},{6,2},{1... | collective-permute-start | bytes 786440 | tf_op jit(solution)/shard_map/ppermute | solution.py:332
  118.9 38.9 %collective-permute-start.12 = (f32[4,32,16,128]{3,2,1,0:T(8,128)S(1)}, f32[4,32,16,128]{3,2,1,0:T(8,128)S(1)}, u32[]{:S(2)}, u32[]{:S(2)}) collective-permute-start(f32[4,32,16,128]{3,2,1,0:T(8,128)S(1)} %get-tuple-element.189), channel_id=1, source_target_pairs={{0,2},{1,3},{2,0},{3,1},{4,6},{5,7},{6,4},{7,5},{8,10},{9,11},{10,... | collective-permute-start | bytes 3145736 | tf_op jit(solution)/shard_map/ppermute | solution.py:328
  147.7 46.3 %collective-permute-start.16 = (f32[4,32,16,128]{3,2,1,0:T(8,128)S(1)}, f32[4,32,16,128]{3,2,1,0:T(8,128)S(1)}, u32[]{:S(2)}, u32[]{:S(2)}) collective-permute-start(f32[4,32,16,128]{3,2,1,0:T(8,128)S(1)} %get-tuple-element.199), channel_id=1, source_target_pairs={{0,2},{1,3},{2,0},{3,1},{4,6},{5,7},{6,4},{7,5},{8,10},{9,11},{10,... | collective-permute-start | bytes 3145736 | tf_op jit(solution)/shard_map/ppermute | solution.py:328
  175.1 53.1 %collective-permute-start.20 = (f32[4,32,16,128]{3,2,1,0:T(8,128)S(1)}, f32[4,32,16,128]{3,2,1,0:T(8,128)S(1)}, u32[]{:S(2)}, u32[]{:S(2)}) collective-permute-start(f32[4,32,16,128]{3,2,1,0:T(8,128)S(1)} %get-tuple-element.209), channel_id=1, source_target_pairs={{0,2},{1,3},{2,0},{3,1},{4,6},{5,7},{6,4},{7,5},{8,10},{9,11},{10,... | collective-permute-start | bytes 3145736 | tf_op jit(solution)/shard_map/ppermute | solution.py:328
  194.0 62.5 %collective-permute-start.24 = (f32[4,32,16,128]{3,2,1,0:T(8,128)S(1)}, f32[4,32,16,128]{3,2,1,0:T(8,128)S(1)}, u32[]{:S(2)}, u32[]{:S(2)}) collective-permute-start(f32[4,32,16,128]{3,2,1,0:T(8,128)S(1)} %get-tuple-element.219), channel_id=1, source_target_pairs={{0,2},{1,3},{2,0},{3,1},{4,6},{5,7},{6,4},{7,5},{8,10},{9,11},{10,... | collective-permute-start | bytes 3145736 | tf_op jit(solution)/shard_map/ppermute | solution.py:328
  196.3 31.9 %collective-permute-start.25 = (f32[32,16,128]{2,1,0:T(8,128)S(1)}, f32[32,16,128]{2,1,0:T(8,128)S(1)}, u32[]{:S(2)}, u32[]{:S(2)}) collective-permute-start(f32[32,16,128]{2,1,0:T(8,128)S(1)} %get-tuple-element.222), channel_id=1, source_target_pairs={{0,4},{4,0},{8,12},{12,8},{1,5},{5,1},{9,13},{13,9},{2,6},{6,2},{1... | collective-permute-start | bytes 786440 | tf_op jit(solution)/shard_map/ppermute | solution.py:332
  202.2 26.0 %collective-permute-start.26 = (f32[32,16,128]{2,1,0:T(8,128)S(1)}, f32[32,16,128]{2,1,0:T(8,128)S(1)}, u32[]{:S(2)}, u32[]{:S(2)}) collective-permute-start(f32[32,16,128]{2,1,0:T(8,128)S(1)} %get-tuple-element.225), channel_id=1, source_target_pairs={{0,12},{4,8},{8,4},{12,0},{1,13},{5,9},{9,5},{13,1},{2,14},{6,10},... | collective-permute-start | bytes 786440 | tf_op jit(solution)/shard_map/ppermute | solution.py:332
  228.3 50.4 %collective-permute-start.35 = (f32[4,4,128,128]{3,2,1,0:T(8,128)S(1)}, f32[4,4,128,128]{3,2,1,0:T(8,128)S(1)}, u32[]{:S(2)}, u32[]{:S(2)}) collective-permute-start(f32[4,4,128,128]{3,2,1,0:T(8,128)S(1)} %get-tuple-element.242), channel_id=1, source_target_pairs={{0,2},{1,3},{2,0},{3,1},{4,6},{5,7},{6,4},{7,5},{8,10},{9,11},{10,... | collective-permute-start | bytes 3145736 | tf_op jit(solution)/shard_map/ppermute | solution.py:328
  256.5 48.6 %collective-permute-start.39 = (f32[4,4,128,128]{3,2,1,0:T(8,128)S(1)}, f32[4,4,128,128]{3,2,1,0:T(8,128)S(1)}, u32[]{:S(2)}, u32[]{:S(2)}) collective-permute-start(f32[4,4,128,128]{3,2,1,0:T(8,128)S(1)} %get-tuple-element.252), channel_id=1, source_target_pairs={{0,2},{1,3},{2,0},{3,1},{4,6},{5,7},{6,4},{7,5},{8,10},{9,11},{10,... | collective-permute-start | bytes 3145736 | tf_op jit(solution)/shard_map/ppermute | solution.py:328
  278.7 51.9 %collective-permute-start.43 = (f32[4,4,128,128]{3,2,1,0:T(8,128)S(1)}, f32[4,4,128,128]{3,2,1,0:T(8,128)S(1)}, u32[]{:S(2)}, u32[]{:S(2)}) collective-permute-start(f32[4,4,128,128]{3,2,1,0:T(8,128)S(1)} %get-tuple-element.262), channel_id=1, source_target_pairs={{0,2},{1,3},{2,0},{3,1},{4,6},{5,7},{6,4},{7,5},{8,10},{9,11},{10,... | collective-permute-start | bytes 3145736 | tf_op jit(solution)/shard_map/ppermute | solution.py:328
  305.1 51.9 %collective-permute-start.47 = (f32[4,4,128,128]{3,2,1,0:T(8,128)S(1)}, f32[4,4,128,128]{3,2,1,0:T(8,128)S(1)}, u32[]{:S(2)}, u32[]{:S(2)}) collective-permute-start(f32[4,4,128,128]{3,2,1,0:T(8,128)S(1)} %get-tuple-element.272), channel_id=1, source_target_pairs={{0,2},{1,3},{2,0},{3,1},{4,6},{5,7},{6,4},{7,5},{8,10},{9,11},{10,... | collective-permute-start | bytes 3145736 | tf_op jit(solution)/shard_map/ppermute | solution.py:328
  330.6 40.0 %collective-permute-start.51 = (f32[4,4,128,128]{3,2,1,0:T(8,128)S(1)}, f32[4,4,128,128]{3,2,1,0:T(8,128)S(1)}, u32[]{:S(2)}, u32[]{:S(2)}) collective-permute-start(f32[4,4,128,128]{3,2,1,0:T(8,128)S(1)} %get-tuple-element.282), channel_id=1, source_target_pairs={{0,2},{1,3},{2,0},{3,1},{4,6},{5,7},{6,4},{7,5},{8,10},{9,11},{10,... | collective-permute-start | bytes 3145736 | tf_op jit(solution)/shard_map/ppermute | solution.py:328
  357.0 46.3 %collective-permute-start.55 = (f32[4,4,128,128]{3,2,1,0:T(8,128)S(1)}, f32[4,4,128,128]{3,2,1,0:T(8,128)S(1)}, u32[]{:S(2)}, u32[]{:S(2)}) collective-permute-start(f32[4,4,128,128]{3,2,1,0:T(8,128)S(1)} %get-tuple-element.292), channel_id=1, source_target_pairs={{0,2},{1,3},{2,0},{3,1},{4,6},{5,7},{6,4},{7,5},{8,10},{9,11},{10,... | collective-permute-start | bytes 3145736 | tf_op jit(solution)/shard_map/ppermute | solution.py:328
  366.5 28.6 %collective-permute-start.49 = (f32[4,128,128]{2,1,0:T(8,128)S(1)}, f32[4,128,128]{2,1,0:T(8,128)S(1)}, u32[]{:S(2)}, u32[]{:S(2)}) collective-permute-start(f32[4,128,128]{2,1,0:T(8,128)S(1)} %get-tuple-element.277), channel_id=1, source_target_pairs={{0,8},{4,12},{8,0},{12,4},{1,9},{5,13},{9,1},{13,5},{2,10},{6,14},... | collective-permute-start | bytes 786440 | tf_op jit(solution)/shard_map/ppermute | solution.py:332
  372.0 28.0 %collective-permute-start.52 = (f32[4,128,128]{2,1,0:T(8,128)S(1)}, f32[4,128,128]{2,1,0:T(8,128)S(1)}, u32[]{:S(2)}, u32[]{:S(2)}) collective-permute-start(f32[4,128,128]{2,1,0:T(8,128)S(1)} %get-tuple-element.285), channel_id=1, source_target_pairs={{0,4},{4,0},{8,12},{12,8},{1,5},{5,1},{9,13},{13,9},{2,6},{6,2},{1... | collective-permute-start | bytes 786440 | tf_op jit(solution)/shard_map/ppermute | solution.py:332
  403.3 42.4 %collective-permute-start.63 = (f32[4,4,128,128]{3,2,1,0:T(8,128)S(1)}, f32[4,4,128,128]{3,2,1,0:T(8,128)S(1)}, u32[]{:S(2)}, u32[]{:S(2)}) collective-permute-start(f32[4,4,128,128]{3,2,1,0:T(8,128)S(1)} %get-tuple-element.312), channel_id=1, source_target_pairs={{0,2},{1,3},{2,0},{3,1},{4,6},{5,7},{6,4},{7,5},{8,10},{9,11},{10,... | collective-permute-start | bytes 3145736 | tf_op jit(solution)/shard_map/ppermute | solution.py:328
  404.8 29.1 %collective-permute-start.57 = (f32[4,128,128]{2,1,0:T(8,128)S(1)}, f32[4,128,128]{2,1,0:T(8,128)S(1)}, u32[]{:S(2)}, u32[]{:S(2)}) collective-permute-start(f32[4,128,128]{2,1,0:T(8,128)S(1)} %get-tuple-element.297), channel_id=1, source_target_pairs={{0,8},{4,12},{8,0},{12,4},{1,9},{5,13},{9,1},{13,5},{2,10},{6,14},... | collective-permute-start | bytes 786440 | tf_op jit(solution)/shard_map/ppermute | solution.py:332
  418.9 26.9 %collective-permute-start.56 = (f32[4,128,128]{2,1,0:T(8,128)S(1)}, f32[4,128,128]{2,1,0:T(8,128)S(1)}, u32[]{:S(2)}, u32[]{:S(2)}) collective-permute-start(f32[4,128,128]{2,1,0:T(8,128)S(1)} %get-tuple-element.295), channel_id=1, source_target_pairs={{0,4},{4,0},{8,12},{12,8},{1,5},{5,1},{9,13},{13,9},{2,6},{6,2},{1... | collective-permute-start | bytes 786440 | tf_op jit(solution)/shard_map/ppermute | solution.py:332
  447.1 26.6 %collective-permute-start.64 = (f32[4,128,128]{2,1,0:T(8,128)S(1)}, f32[4,128,128]{2,1,0:T(8,128)}, u32[]{:S(2)}, u32[]{:S(2)}) collective-permute-start(f32[4,128,128]{2,1,0:T(8,128)S(1)} %get-tuple-element.315), channel_id=1, source_target_pairs={{0,4},{4,0},{8,12},{12,8},{1,5},{5,1},{9,13},{13,9},{2,6},{6,2},{1... | collective-permute-start | bytes 786440 | tf_op jit(solution)/shard_map/ppermute | solution.py:332
  (122 other events, 2095.1 us)

commit v5 on v4

--- a/solution.py
+++ b/solution.py
@@ -33,7 +33,7 @@
     return [pltpu.with_memory_space_constraint(value, pltpu.HBM) for value in values]
 
 
-def call(name, kernel, grid, in_specs, out_specs, out_shape, scratch=(), vmem=16):
+def call(name, kernel, grid, in_specs, out_specs, out_shape, scratch=(), vmem=16, aliases={}):
     return pl.pallas_call(
         kernel,
         name=name,
@@ -41,13 +41,14 @@
             num_scalar_prefetch=1, grid=grid, in_specs=in_specs, out_specs=out_specs, scratch_shapes=list(scratch)
         ),
         out_shape=out_shape,
+        input_output_aliases=aliases,
         compiler_params=pltpu.CompilerParams(vmem_limit_bytes=vmem * MIB, dimension_semantics=("arbitrary",) * len(grid)),
         cost_estimate=pl.CostEstimate(flops=0, bytes_accessed=0, transcendentals=0),
     )
 
 
-def project_kernel(parts, place, own_ref, other_ref, basis_ref, *rest):
-    outs, basis_split = rest[:-1], rest[-1]
+def project_kernel(parts, skip, place, own_ref, other_ref, basis_ref, *rest):
+    outs, basis_split = rest[skip:-1], rest[-1]
     keeps, sends = outs[: len(parts)], outs[len(parts) :]
     rank = basis_ref.shape[0]
 
@@ -73,29 +74,32 @@
                 at += rows
 
 
-def project(place, field, other, basis, job, offset):
+def project(place, field, other, basis, job, offset, total, before):
     species, x_start, xs, parts = job
     _, ys, zs = other.shape
     rank = basis.shape[0]
     block = 8
     steps = xs // block
-    shapes = [(4, rows, xs, zs // 2) for rows in parts] * 2
+    shapes = [(4, rows, total, zs // 2) for rows in parts] * 2
+    first = x_start // block if total > xs else 0
+    array = pltpu.HBM if total > xs else jax.ShapeDtypeStruct
     in_specs = [
         pl.BlockSpec((1, block, ys, zs), lambda i, place: (2 * place[1] + species, x_start // block + i, 0, 0)),
         pl.BlockSpec((block, ys, zs), lambda i, place: (offset // block + i, 0, 0)),
         pl.BlockSpec(basis.shape, lambda i, place: (0, 0)),
-    ]
-    out_specs = [pl.BlockSpec((4, s[1], block, s[3]), lambda i, place: (0, 0, i, 0)) for s in shapes]
+    ] + [pl.BlockSpec(memory_space=pl.ANY)] * len(before)
+    out_specs = [pl.BlockSpec((4, s[1], block, s[3]), lambda i, place: (0, 0, first + i, 0)) for s in shapes]
     result = call(
         "project_k",
-        lambda place, *refs: project_kernel(parts, place, *refs),
+        lambda place, *refs: project_kernel(parts, len(before), place, *refs),
         (steps,),
         in_specs,
         out_specs,
-        [jax.ShapeDtypeStruct(s, F32) for s in shapes],
+        [array(s, F32) for s in shapes],
         [pltpu.VMEM((2 * rank, 2 * ys), BF16)],
         vmem=18,
-    )(place, field, other, basis)
+        aliases={4 + index: index for index in range(len(before))},
+    )(place, field, other, basis, *in_hbm(*before))
     count = len(parts)
     return result[:count], result[count:]
 
@@ -252,7 +256,7 @@
 
 
 def core_kernel(counts, steps, place, basis_ref, *rest):
-    lines, (keep_ref, send_ref, factor_ref) = rest[:-3], rest[-3:]
+    lines, (keep_ref, send_ref, factor_ref) = rest[: sum(counts)], rest[-3:]
     rank = basis_ref.shape[1]
     xs = basis_ref.shape[0] // 4
 
@@ -275,7 +279,7 @@
         out = both[:, :rank] + (both[:, rank:] + tn_dot(low, factor[:, :rank]))
         out = out.reshape(len(lines), 2, LANES // 2, rank)
         first = place[1] == 0
-        keep_ref[...] = jnp.where(first, out[:, 0], out[:, 1])
+        keep_ref[0] = jnp.where(first, out[:, 0], out[:, 1])
         send_ref[...] = jnp.where(first, out[:, 1], out[:, 0])
 
     groups, at = [], 0
@@ -292,13 +296,14 @@
                 work([groups[member] for member in members])
 
 
-def core_of(place, basis, lines):
+def core_of(place, basis, lines, species, whole):
     block = 8
     rank = basis.shape[1]
     groups = [[piece for d in group for piece in d] for group in lines]
     flat = [piece for group in groups for piece in group]
     rows = [group[0].shape[0] for group in groups]
     total, zs = sum(rows), flat[0].shape[2]
+    before = [] if whole is None else [whole]
     if len(groups) == 1:
         steps = None
         specs = [pl.BlockSpec((block, *piece.shape[1:]), lambda i, place: (i, 0, 0)) for piece in flat]
@@ -312,12 +317,36 @@
         "core_k",
         lambda place, *refs: core_kernel([len(group) for group in groups], steps, place, *refs),
         (total // block,),
-        [pl.BlockSpec(basis.shape, lambda i, place: (0, 0))] + specs,
-        [pl.BlockSpec((block, zs // 2, rank), lambda i, place: (i, 0, 0))] * 2,
-        [pltpu.HBM((total, zs // 2, rank), F32)] * 2,
+        [pl.BlockSpec(basis.shape, lambda i, place: (0, 0))] + specs + [pl.BlockSpec(memory_space=pl.ANY)] * len(before),
+        [
+            pl.BlockSpec((1, block, zs // 2, rank), lambda i, place: (2 * place[1] + species, i, 0, 0)),
+            pl.BlockSpec((block, zs // 2, rank), lambda i, place: (i, 0, 0)),
+        ],
+        [pltpu.HBM((4, total, zs // 2, rank), F32), pltpu.HBM((total, zs // 2, rank), F32)],
         [pltpu.VMEM((basis.shape[0], 2 * rank), BF16)],
         vmem=36,
-    )(place, basis, *in_hbm(*flat))
+        aliases={2 + len(flat): 0} if before else {},
+    )(place, basis, *in_hbm(*flat, *before))
+
+
+def finish_kernel(place, whole_ref, *refs):
+    out_ref = refs[-1]
+    for species, ref in enumerate(refs[:-1]):
+        out_ref[species] = ref[...]
+
+
+def finish(place, whole, came):
+    rows, zs, rank = came[0].shape
+    block = 8
+    return call(
+        "finish_k",
+        finish_kernel,
+        (rows // block,),
+        [pl.BlockSpec(memory_space=pl.ANY)] + [pl.BlockSpec((block, zs, rank), lambda i, place: (i, 0, 0))] * 2,
+        pl.BlockSpec((2, block, zs, rank), lambda i, place: (1 - place[1], i, 0, 0)),
+        pltpu.HBM(whole.shape, F32),
+        aliases={1: 0},
+    )(place, *in_hbm(whole, *came))
 
 
 def after(value, *earlier):
@@ -362,8 +391,10 @@
     for size in X_PARTS:
         jobs.append((0, at, size, (share,)))
         at += size
-    jobs.append((1, 0, xs, R_PARTS))
+    late = [(1, start, xs // 2, R_PARTS) for start in (0, xs // 2)]
+    jobs[3:3] = late
     keeps, sends, came, lines = [], [], [], []
+    halves = []
     grams = [jnp.zeros((len(PAIRS) * xs * 2, xs * 2), F32)]
     count = len(X_PARTS)
 
@@ -383,6 +414,8 @@
         earlier = []
         if i >= 2:
             earlier = [came[i - 2]] + (lines[i - 3][1:] if i >= 3 else [])
+        if i in (6, 7):
+            earlier.append(halves[i - 6])
         if i >= count + 3:
             earlier.append(grams[i - count - 2])
         came.append(pair_swap(after(part, *earlier), 2))
@@ -390,34 +423,40 @@
             spread(i - 1)
 
     swaps = [(0, 0, X_PARTS[0]), (0, X_PARTS[0], xs - X_PARTS[0]), (1, 0, xs)]
-    others, theirs = [], []
+    others, theirs, second = [], [], []
     for job in jobs:
-        while swaps and swaps[0][:2] <= job[:2]:
+        while swaps and swaps[0][0] <= job[0] and swaps[0][1] <= job[1]:
             s, start, size = swaps.pop(0)
-            earlier = ([], sends[:1], theirs[-1:])[len(theirs)]
+            earlier = ([], sends[:1], lines[0][:1] if lines else [])[len(theirs)]
             first = after(2 * (1 - core) + s, *earlier)
             theirs.append(lax.dynamic_slice(slab_field, (first, start, 0, 0), (1, size, ys, zs))[0])
-            others.append((start, pair_swap(theirs[-1], 1)))
-        base, other = others[-1]
-        keep, send = project(place, slab_field, other, basis_t, job, job[1] - base)
+            others.append((s, start, pair_swap(theirs[-1], 1)))
+        base, other = [(start, array) for s, start, array in others if s == job[0] and start <= job[1]][-1]
+        if job[0] == 0:
+            keep, send = project(place, slab_field, other, basis_t, job, job[1] - base, job[2], [])
+        else:
+            keep, send = project(place, slab_field, other, basis_t, job, job[1] - base, xs, second)
+            second = [*keep, *send]
+            halves.append(send[0])
+            continue
         for mine, part in zip(keep, send):
             keeps.append(mine)
             sends.append(part)
             exchange(part)
+    for mine, part in zip(second[: len(R_PARTS)], second[len(R_PARTS) :]):
+        keeps.append(mine)
+        sends.append(part)
+        exchange(part)
     spread(len(keeps) - 1)
 
     first = [[line[d] for line in lines[:count]] for d in range(4)]
     second = [[[line[d]] for d in range(4)] for line in lines[count:]]
     basis = subspace(place, reduce_gram(place, grams[-1]), x_basis)
 
-    keep0, send0 = core_of(place, basis, [first])
+    whole, send0 = core_of(place, basis, [first], 0, None)
     came0 = pair_swap(send0, 1)
-    keep1, send1 = core_of(place, basis, second)
-    came1 = pair_swap(send1, 1)
-    mine, theirs = (keep0, keep1), (came0, came1)
-    core_tensor = jnp.stack(
-        [jnp.where(core == i // 2, mine[i % 2], theirs[i % 2]) for i in range(species)]
-    ).transpose(0, 3, 1, 2)
+    whole, send1 = core_of(place, basis, second, 1, whole)
+    core_tensor = finish(place, whole, [came0, pair_swap(send1, 1)]).transpose(0, 3, 1, 2)
     new_basis = lax.dynamic_slice_in_dim(basis, z * xs, xs, 0)
     return new_basis, core_tensor
 

time: 557 us -> 554 us (level)
  starting transfers between devices: 171 us -> 160 us
  Pallas kernels: 132 us -> 141 us
    ppermute x54, starting transfers between devices: 146 us -> 135 us  [z_swap(): return lax.ppermute(value, 'aa', [(i, i ^ d) for i in range(4)])]
    pallas_call x9 -> x11, Pallas kernels: 59.2 us -> 66.1 us  [the longest x10 61.8 us: project(): call('project_k', lambda place, *refs: project_kernel(parts, len(before),...]
    unnamed x140 -> x160, local copies, waits for them, and re-layouts: 10.4 us -> 11.7 us
  transfers between devices with their start and end apart: 79 -> 79, of which waited for: 36 -> 37; matrix products, arithmetic and copies ran while one was open for 3% -> 5% of each run, Pallas kernels for 19% -> 20%
where the time goes in v5:
time: 554 us; the launch traced here: 545 us
  waiting for transfers between devices  201 us (36%)
  starting transfers between devices  160 us (29%)
  Pallas kernels  141 us (25%)
  local copies, waits for them, and re-layouts  40.4 us (7%)
    ppermute x54, waiting for transfers between devices, z_swap(): return lax.ppermute(value, 'aa', [(i, i ^ d) for i in range(4)])  161 us
    ppermute x54, starting transfers between devices, z_swap(): return lax.ppermute(value, 'aa', [(i, i ^ d) for i in range(4)])  135 us
    pallas_call x10, Pallas kernels, project(): call('project_k', lambda place, *refs: project_kernel(parts, len(before),...  61.8 us
    ppermute x25, waiting for transfers between devices, pair_swap(): return lax.ppermute(value, 'ba', [(i, i ^ distance) for i in range(4)])  40.3 us
    pallas_call x9, Pallas kernels, add_gram(): call('gram_k', lambda place, *refs: gram_kernel(parts, place, *refs), (ro...  33 us
    squeeze x3, local copies, waits for them, and re-layouts, fast_body(): lax.dynamic_slice(slab_field, (first, start, 0, 0), (1, size, ys, zs))[0]  27 us
    ppermute x25, starting transfers between devices, pair_swap(): return lax.ppermute(value, 'ba', [(i, i ^ distance) for i in range(4)])  24.9 us
    pallas_call x2, Pallas kernels, core_of(): call('core_k', lambda place, *refs: core_kernel([len(group) for group in...  15.5 us
  transfers between devices with their start and end apart: 79, of which 37 were waited for; matrix products, arithmetic and copies ran while one was open for 5% of the time, Pallas kernels for 20%

profile of v5, /device:TPU:0, one launch (start us, length us, event | category | flops | bytes accessed | tf_op | source)
XLA Modules:
  0.0 544.8 jit_solution(7190675085185927715)
XLA Ops:
  15.9 12.2 %dynamic-slice_bitcast_fusion.1 = f32[112,128,256]{2,1,0:T(8,128)} fusion(f32[4,128,128,256]{3,2,1,0:T(8,128)} %refs_0_.19, s32[]{:T(128)S(6)} %select_n.61), kind=kLoop, calls=%fused_computation.1 | loop fusion | bytes 29360132 | tf_op jit(solution)/shard_map/squeeze | solution.py:432
  28.1 11.4 %collective-permute-done.1.recv_ref = f32[4,32,16,128]{3,2,1,0:T(8,128)S(1)} collective-permute-done((f32[4,32,16,128]{3,2,1,0:T(8,128)}, f32[4,32,16,128]{3,2,1,0:T(8,128)S(1)}, u32[]{:S(2)}, u32[]{:S(2)}) %collective-permute-start.1) | collective-permute-done | bytes 1048608 | tf_op jit(solution)/shard_map/ppermute | solution.py:357
  41.6 11.6 %dynamic-slice_bitcast_fusion = f32[128,128,256]{2,1,0:T(8,128)} fusion(f32[4,128,128,256]{3,2,1,0:T(8,128)} %refs_0_.19, s32[]{:T(128)S(6)} %select_n.62), kind=kLoop, calls=%fused_computation | loop fusion | bytes 33554436 | tf_op jit(solution)/shard_map/squeeze | solution.py:432
  68.6 9.1 %collective-permute-done.5.refs_9_ = f32[32,16,128]{2,1,0:T(8,128)S(1)} collective-permute-done((f32[32,16,128]{2,1,0:T(8,128)S(1)}, f32[32,16,128]{2,1,0:T(8,128)S(1)}, u32[]{:S(2)}, u32[]{:S(2)}) %collective-permute-start.5) | collective-permute-done | bytes 262176 | tf_op jit(solution)/shard_map/ppermute | solution.py:361
  96.3 9.8 %collective-permute-done.4.recv_ref = f32[4,32,16,128]{3,2,1,0:T(8,128)S(1)} collective-permute-done((f32[4,32,16,128]{3,2,1,0:T(8,128)S(1)}, f32[4,32,16,128]{3,2,1,0:T(8,128)S(1)}, u32[]{:S(2)}, u32[]{:S(2)}) %collective-permute-start.4) | collective-permute-done | bytes 1048608 | tf_op jit(solution)/shard_map/ppermute | solution.py:357
  125.0 8.5 %collective-permute-done.13.refs_11_ = f32[32,16,128]{2,1,0:T(8,128)S(1)} collective-permute-done((f32[32,16,128]{2,1,0:T(8,128)S(1)}, f32[32,16,128]{2,1,0:T(8,128)S(1)}, u32[]{:S(2)}, u32[]{:S(2)}) %collective-permute-start.13) | collective-permute-done | bytes 262176 | tf_op jit(solution)/shard_map/ppermute | solution.py:361
  160.7 13.2 %project_k.17 = (f32[4,4,128,128]{3,2,1,0:T(8,128)}, f32[4,4,128,128]{3,2,1,0:T(8,128)}, f32[4,4,128,128]{3,2,1,0:T(8,128)}, f32[4,4,128,128]{3,2,1,0:T(8,128)},...) custom-call(s32[3]{0:T(128)S(1)} %pad_add_fusion.place, ...), custom_call_target="tpu_custom_call" | custom-call | tf_op jit(solution)/shard_map/project_k/pallas_call | solution.py:92
  184.3 13.1 %project_k.19 = (f32[4,4,128,128]{3,2,1,0:T(8,128)}, f32[4,4,128,128]{3,2,1,0:T(8,128)}, f32[4,4,128,128]{3,2,1,0:T(8,128)}, f32[4,4,128,128]{3,2,1,0:T(8,128)},...) custom-call(s32[3]{0:T(128)S(1)} %pad_add_fusion.place, ...), custom_call_target="tpu_custom_call", output_to_operand_aliasing={{0}: (4, {}), {1}: (5, {}), {2}: (6, {}), {3}: (7, {}), {4}... | custom-call | tf_op jit(solution)/shard_map/project_k/pallas_call | solution.py:92
  215.9 9.1 %collective-permute-done.29.refs_22_ = f32[32,16,128]{2,1,0:T(8,128)S(1)} collective-permute-done((f32[32,16,128]{2,1,0:T(8,128)S(1)}, f32[32,16,128]{2,1,0:T(8,128)S(1)}, u32[]{:S(2)}, u32[]{:S(2)}) %collective-permute-start.29) | collective-permute-done | bytes 262176 | tf_op jit(solution)/shard_map/ppermute | solution.py:361
  241.3 10.3 %collective-permute-done.32.refs_23_ = f32[32,16,128]{2,1,0:T(8,128)S(1)} collective-permute-done((f32[32,16,128]{2,1,0:T(8,128)S(1)}, f32[32,16,128]{2,1,0:T(8,128)S(1)}, u32[]{:S(2)}, u32[]{:S(2)}) %collective-permute-start.32) | collective-permute-done | bytes 262176 | tf_op jit(solution)/shard_map/ppermute | solution.py:361
  257.9 7.3 %collective-permute-done.31.refs_16_ = f32[32,16,128]{2,1,0:T(8,128)S(1)} collective-permute-done((f32[32,16,128]{2,1,0:T(8,128)S(1)}, f32[32,16,128]{2,1,0:T(8,128)S(1)}, u32[]{:S(2)}, u32[]{:S(2)}) %collective-permute-start.31) | collective-permute-done | bytes 262176 | tf_op jit(solution)/shard_map/ppermute | solution.py:361
  265.3 8.8 %collective-permute-done.33.refs_24_ = f32[32,16,128]{2,1,0:T(8,128)S(1)} collective-permute-done((f32[32,16,128]{2,1,0:T(8,128)S(1)}, f32[32,16,128]{2,1,0:T(8,128)S(1)}, u32[]{:S(2)}, u32[]{:S(2)}) %collective-permute-start.33) | collective-permute-done | bytes 262176 | tf_op jit(solution)/shard_map/ppermute | solution.py:361
  284.9 11.2 %gram_k.9.refs_0_ = f32[768,256]{1,0:T(8,128)S(1)} custom-call(s32[3]{0:T(128)S(1)} %pad_add_fusion.place, f32[768,256]{1,0:T(8,128)S(1)} %broadcast_in_dim.3.refs_0_, f32[32,16,128]{2,1,0:T(8,128)} %copy-done.8, f32[32,16,128]{2,1,0:T(8,128)} %copy-done.9, f32[32,16,128]{2,1,0:T(8,128)} %copy-done.10, f32[32,16,128]{2,1,0:T(8,128)} %copy-done.11, ...), custom_call_target="tpu_custom_call" | custom-call | tf_op jit(solution)/shard_map/gram_k/pallas_call | solution.py:161
  317.1 11.6 %collective-permute-done.41.refs_3_.refs_7_ = f32[4,128,128]{2,1,0:T(8,128)S(1)} collective-permute-done((f32[4,128,128]{2,1,0:T(8,128)S(1)}, f32[4,128,128]{2,1,0:T(8,128)S(1)}, u32[]{:S(2)}, u32[]{:S(2)}) %collective-permute-start.41) | collective-permute-done | bytes 262176 | tf_op jit(solution)/shard_map/ppermute | solution.py:361
  343.9 11.4 %collective-permute-done.45.refs_3_.refs_11_ = f32[4,128,128]{2,1,0:T(8,128)S(1)} collective-permute-done((f32[4,128,128]{2,1,0:T(8,128)S(1)}, f32[4,128,128]{2,1,0:T(8,128)S(1)}, u32[]{:S(2)}, u32[]{:S(2)}) %collective-permute-start.45) | collective-permute-done | bytes 262176 | tf_op jit(solution)/shard_map/ppermute | solution.py:361
  358.1 7.0 %collective-permute-start.48 = (f32[4,128,128]{2,1,0:T(8,128)S(1)}, f32[4,128,128]{2,1,0:T(8,128)S(1)}, u32[]{:S(2)}, u32[]{:S(2)}) collective-permute-start(f32[4,128,128]{2,1,0:T(8,128)S(1)} %get-tuple-element.307), channel_id=1, source_target_pairs={{0,4},{4,0},{8,12},{12,8},{1,5},{5,1},{9,13},{13,9},{2,6},{6,2},{1... | collective-permute-start | bytes 786440 | tf_op jit(solution)/shard_map/ppermute | solution.py:361
  369.9 7.7 %collective-permute-start.52 = (f32[4,128,128]{2,1,0:T(8,128)S(1)}, f32[4,128,128]{2,1,0:T(8,128)S(1)}, u32[]{:S(2)}, u32[]{:S(2)}) collective-permute-start(f32[4,128,128]{2,1,0:T(8,128)S(1)} %get-tuple-element.317), channel_id=1, source_target_pairs={{0,4},{4,0},{8,12},{12,8},{1,5},{5,1},{9,13},{13,9},{2,6},{6,2},{1... | collective-permute-start | bytes 786440 | tf_op jit(solution)/shard_map/ppermute | solution.py:361
  377.9 15.1 %collective-permute-done.49.refs_3_.refs_15_ = f32[4,128,128]{2,1,0:T(8,128)S(1)} collective-permute-done((f32[4,128,128]{2,1,0:T(8,128)S(1)}, f32[4,128,128]{2,1,0:T(8,128)S(1)}, u32[]{:S(2)}, u32[]{:S(2)}) %collective-permute-start.49) | collective-permute-done | bytes 262176 | tf_op jit(solution)/shard_map/ppermute | solution.py:361
  403.5 9.3 %collective-permute-start.57 = (f32[4,128,128]{2,1,0:T(8,128)S(1)}, f32[4,128,128]{2,1,0:T(8,128)S(1)}, u32[]{:S(2)}, u32[]{:S(2)}) collective-permute-start(f32[4,128,128]{2,1,0:T(8,128)S(1)} %get-tuple-element.329), channel_id=1, source_target_pairs={{0,8},{4,12},{8,0},{12,4},{1,9},{5,13},{9,1},{13,5},{2,10},{6,14},... | collective-permute-start | bytes 786440 | tf_op jit(solution)/shard_map/ppermute | solution.py:361
  418.6 11.1 %collective-permute-done.57.refs_3_.refs_23_ = f32[4,128,128]{2,1,0:T(8,128)S(1)} collective-permute-done((f32[4,128,128]{2,1,0:T(8,128)S(1)}, f32[4,128,128]{2,1,0:T(8,128)S(1)}, u32[]{:S(2)}, u32[]{:S(2)}) %collective-permute-start.57) | collective-permute-done | bytes 262176 | tf_op jit(solution)/shard_map/ppermute | solution.py:361
  441.5 12.8 %collective-permute-start.64 = (f32[4,128,128]{2,1,0:T(8,128)S(1)}, f32[4,128,128]{2,1,0:T(8,128)}, u32[]{:S(2)}, u32[]{:S(2)}) collective-permute-start(f32[4,128,128]{2,1,0:T(8,128)S(1)} %get-tuple-element.347), channel_id=1, source_target_pairs={{0,4},{4,0},{8,12},{12,8},{1,5},{5,1},{9,13},{13,9},{2,6},{6,2},{1... | collective-permute-start | bytes 786440 | tf_op jit(solution)/shard_map/ppermute | solution.py:361
  505.4 14.9 %subspace_k.1.refs_0_ = f32[512,128]{1,0:T(8,128)S(1)} custom-call(s32[3]{0:T(128)S(1)} %pad_add_fusion.place, f32[16,48,256]{2,1,0:T(8,128)S(1)} %constant_dynamic-update-slice_fusion.5.pieces_ref, f32[512,128]{1,0:T(8,128)S(1)} %copy-done.24), custom_call_target="tpu_custom_call" | custom-call | tf_op jit(solution)/shard_map/subspace_k/pallas_call | solution.py:243
  520.4 7.3 %core_k.2 = (f32[4,32,64,128]{3,2,1,0:T(8,128)}, f32[32,64,128]{2,1,0:T(8,128)}) custom-call(s32[3]{0:T(128)S(1)} %pad_add_fusion.place, f32[512,128]{1,0:T(8,128)S(1)} %subspace_k.1.refs_0_, f32[32,16,128]{2,1,0:T(8,128)} %copy-done.8, f32[32,16,128]{2,1,0:T(8,128)} %copy-done.9, f32[32,16,128]{2,1,0:T(8,128)} %copy-done.10, f32[32,16,128]{2,1,0:T(8,128)} %copy-done.11, ...), custom_call_target="tpu_custom_call" | custom-call | tf_op jit(solution)/shard_map/core_k/pallas_call | solution.py:316
  527.9 8.2 %core_k.3 = (f32[4,32,64,128]{3,2,1,0:T(8,128)}, f32[32,64,128]{2,1,0:T(8,128)}) custom-call(s32[3]{0:T(128)S(1)} %pad_add_fusion.place, f32[512,128]{1,0:T(8,128)S(1)} %subspace_k.1.refs_0_, f32[4,128,128]{2,1,0:T(8,128)} %copy-done.16, f32[4,128,128]{2,1,0:T(8,128)} %copy-done.54, f32[4,128,128]{2,1,0:T(8,128)} %copy-done.55, ...), custom_call_target="tpu_custom_call", output_to_operand_aliasing={{0}: (34, {})} | custom-call | tf_op jit(solution)/shard_map/core_k/pallas_call | solution.py:316
  (350 shorter events, 290.3 us)
Async XLA Ops:
  13.0 26.5 %collective-permute-start.1 = (f32[4,32,16,128]{3,2,1,0:T(8,128)}, f32[4,32,16,128]{3,2,1,0:T(8,128)S(1)}, u32[]{:S(2)}, u32[]{:S(2)}) collective-permute-start(f32[4,32,16,128]{3,2,1,0:T(8,128)} %get-tuple-element.180), channel_id=1, source_target_pairs={{0,2},{1,3},{2,0},{3,1},{4,6},{5,7},{6,4},{7,5},{8,10},{9,11},{10,... | collective-permute-start | bytes 3145736 | tf_op jit(solution)/shard_map/ppermute | solution.py:357
  28.1 25.1 %collective-permute-start.2 = (f32[112,128,256]{2,1,0:T(8,128)}, f32[112,128,256]{2,1,0:T(8,128)}, u32[]{:S(2)}, u32[]{:S(2)}) collective-permute-start(f32[112,128,256]{2,1,0:T(8,128)} %dynamic-slice_bitcast_fusion.1), channel_id=1, source_target_pairs={{0,1},{1,0},{2,3},{3,2},{4,5},{5,4},{6,7},{7,6},{8,9},{9,8},{10,11... | collective-permute-start | bytes 44040200 | tf_op jit(solution)/shard_map/ppermute | solution.py:357
  53.2 107.5 %collective-permute-start.20 = (f32[128,128,256]{2,1,0:T(8,128)}, f32[128,128,256]{2,1,0:T(8,128)S(1)}, u32[]{:S(2)}, u32[]{:S(2)}) collective-permute-start(f32[128,128,256]{2,1,0:T(8,128)} %dynamic-slice_bitcast_fusion), channel_id=1, source_target_pairs={{0,1},{1,0},{2,3},{3,2},{4,5},{5,4},{6,7},{7,6},{8,9},{9,8},{10,11... | collective-permute-start | bytes 50331656 | tf_op jit(solution)/shard_map/ppermute | solution.py:357
  57.6 30.1 %collective-permute-start.3 = (f32[4,32,16,128]{3,2,1,0:T(8,128)S(1)}, f32[4,32,16,128]{3,2,1,0:T(8,128)S(1)}, u32[]{:S(2)}, u32[]{:S(2)}) collective-permute-start(f32[4,32,16,128]{3,2,1,0:T(8,128)S(1)} %get-tuple-element.184), channel_id=1, source_target_pairs={{0,2},{1,3},{2,0},{3,1},{4,6},{5,7},{6,4},{7,5},{8,10},{9,11},{10,... | collective-permute-start | bytes 3145736 | tf_op jit(solution)/shard_map/ppermute | solution.py:357
  63.8 42.3 %collective-permute-start.4 = (f32[4,32,16,128]{3,2,1,0:T(8,128)S(1)}, f32[4,32,16,128]{3,2,1,0:T(8,128)S(1)}, u32[]{:S(2)}, u32[]{:S(2)}) collective-permute-start(f32[4,32,16,128]{3,2,1,0:T(8,128)S(1)} %get-tuple-element.188), channel_id=1, source_target_pairs={{0,2},{1,3},{2,0},{3,1},{4,6},{5,7},{6,4},{7,5},{8,10},{9,11},{10,... | collective-permute-start | bytes 3145736 | tf_op jit(solution)/shard_map/ppermute | solution.py:357
  87.7 57.1 %collective-permute-start.8 = (f32[4,32,16,128]{3,2,1,0:T(8,128)S(1)}, f32[4,32,16,128]{3,2,1,0:T(8,128)S(1)}, u32[]{:S(2)}, u32[]{:S(2)}) collective-permute-start(f32[4,32,16,128]{3,2,1,0:T(8,128)S(1)} %get-tuple-element.195), channel_id=1, source_target_pairs={{0,2},{1,3},{2,0},{3,1},{4,6},{5,7},{6,4},{7,5},{8,10},{9,11},{10,... | collective-permute-start | bytes 3145736 | tf_op jit(solution)/shard_map/ppermute | solution.py:357
  90.6 23.8 %collective-permute-start.9 = (f32[32,16,128]{2,1,0:T(8,128)S(1)}, f32[32,16,128]{2,1,0:T(8,128)S(1)}, u32[]{:S(2)}, u32[]{:S(2)}) collective-permute-start(f32[32,16,128]{2,1,0:T(8,128)S(1)} %get-tuple-element.200), channel_id=1, source_target_pairs={{0,4},{4,0},{8,12},{12,8},{1,5},{5,1},{9,13},{13,9},{2,6},{6,2},{1... | collective-permute-start | bytes 786440 | tf_op jit(solution)/shard_map/ppermute | solution.py:361
  115.9 35.5 %collective-permute-start.12 = (f32[4,32,16,128]{3,2,1,0:T(8,128)S(1)}, f32[4,32,16,128]{3,2,1,0:T(8,128)S(1)}, u32[]{:S(2)}, u32[]{:S(2)}) collective-permute-start(f32[4,32,16,128]{3,2,1,0:T(8,128)S(1)} %get-tuple-element.205), channel_id=1, source_target_pairs={{0,2},{1,3},{2,0},{3,1},{4,6},{5,7},{6,4},{7,5},{8,10},{9,11},{10,... | collective-permute-start | bytes 3145736 | tf_op jit(solution)/shard_map/ppermute | solution.py:357
  144.8 52.8 %collective-permute-start.16 = (f32[4,32,16,128]{3,2,1,0:T(8,128)S(1)}, f32[4,32,16,128]{3,2,1,0:T(8,128)S(1)}, u32[]{:S(2)}, u32[]{:S(2)}) collective-permute-start(f32[4,32,16,128]{3,2,1,0:T(8,128)S(1)} %get-tuple-element.215), channel_id=1, source_target_pairs={{0,2},{1,3},{2,0},{3,1},{4,6},{5,7},{6,4},{7,5},{8,10},{9,11},{10,... | collective-permute-start | bytes 3145736 | tf_op jit(solution)/shard_map/ppermute | solution.py:357
  146.7 27.2 %collective-permute-start.17 = (f32[32,16,128]{2,1,0:T(8,128)S(1)}, f32[32,16,128]{2,1,0:T(8,128)S(1)}, u32[]{:S(2)}, u32[]{:S(2)}) collective-permute-start(f32[32,16,128]{2,1,0:T(8,128)S(1)} %get-tuple-element.220), channel_id=1, source_target_pairs={{0,4},{4,0},{8,12},{12,8},{1,5},{5,1},{9,13},{13,9},{2,6},{6,2},{1... | collective-permute-start | bytes 786440 | tf_op jit(solution)/shard_map/ppermute | solution.py:361
  174.0 51.0 %collective-permute-start.21 = (f32[4,32,16,128]{3,2,1,0:T(8,128)S(1)}, f32[4,32,16,128]{3,2,1,0:T(8,128)S(1)}, u32[]{:S(2)}, u32[]{:S(2)}) collective-permute-start(f32[4,32,16,128]{3,2,1,0:T(8,128)S(1)} %get-tuple-element.227), channel_id=1, source_target_pairs={{0,2},{1,3},{2,0},{3,1},{4,6},{5,7},{6,4},{7,5},{8,10},{9,11},{10,... | collective-permute-start | bytes 3145736 | tf_op jit(solution)/shard_map/ppermute | solution.py:357
  197.5 33.8 %collective-permute-start.25 = (f32[4,32,16,128]{3,2,1,0:T(8,128)S(1)}, f32[4,32,16,128]{3,2,1,0:T(8,128)S(1)}, u32[]{:S(2)}, u32[]{:S(2)}) collective-permute-start(f32[4,32,16,128]{3,2,1,0:T(8,128)S(1)} %get-tuple-element.253), channel_id=1, source_target_pairs={{0,2},{1,3},{2,0},{3,1},{4,6},{5,7},{6,4},{7,5},{8,10},{9,11},{10,... | collective-permute-start | bytes 3145736 | tf_op jit(solution)/shard_map/ppermute | solution.py:357
  225.0 49.1 %collective-permute-start.35 = (f32[4,4,128,128]{3,2,1,0:T(8,128)}, f32[4,4,128,128]{3,2,1,0:T(8,128)S(1)}, u32[]{:S(2)}, u32[]{:S(2)}) collective-permute-start(f32[4,4,128,128]{3,2,1,0:T(8,128)} %get-tuple-element.274), channel_id=1, source_target_pairs={{0,2},{1,3},{2,0},{3,1},{4,6},{5,7},{6,4},{7,5},{8,10},{9,11},{10,... | collective-permute-start | bytes 3145736 | tf_op jit(solution)/shard_map/ppermute | solution.py:357
  251.6 50.1 %collective-permute-start.39 = (f32[4,4,128,128]{3,2,1,0:T(8,128)}, f32[4,4,128,128]{3,2,1,0:T(8,128)S(1)}, u32[]{:S(2)}, u32[]{:S(2)}) collective-permute-start(f32[4,4,128,128]{3,2,1,0:T(8,128)} %get-tuple-element.284), channel_id=1, source_target_pairs={{0,2},{1,3},{2,0},{3,1},{4,6},{5,7},{6,4},{7,5},{8,10},{9,11},{10,... | collective-permute-start | bytes 3145736 | tf_op jit(solution)/shard_map/ppermute | solution.py:357
  274.1 54.6 %collective-permute-start.43 = (f32[4,4,128,128]{3,2,1,0:T(8,128)}, f32[4,4,128,128]{3,2,1,0:T(8,128)S(1)}, u32[]{:S(2)}, u32[]{:S(2)}) collective-permute-start(f32[4,4,128,128]{3,2,1,0:T(8,128)} %get-tuple-element.294), channel_id=1, source_target_pairs={{0,2},{1,3},{2,0},{3,1},{4,6},{5,7},{6,4},{7,5},{8,10},{9,11},{10,... | collective-permute-start | bytes 3145736 | tf_op jit(solution)/shard_map/ppermute | solution.py:357
  301.8 53.5 %collective-permute-start.47 = (f32[4,4,128,128]{3,2,1,0:T(8,128)S(1)}, f32[4,4,128,128]{3,2,1,0:T(8,128)S(1)}, u32[]{:S(2)}, u32[]{:S(2)}) collective-permute-start(f32[4,4,128,128]{3,2,1,0:T(8,128)S(1)} %copy-done.25), channel_id=1, source_target_pairs={{0,2},{1,3},{2,0},{3,1},{4,6},{5,7},{6,4},{7,5},{8,10},{9,11},{10,... | collective-permute-start | bytes 3145736 | tf_op jit(solution)/shard_map/ppermute | solution.py:357
  328.7 40.5 %collective-permute-start.51 = (f32[4,4,128,128]{3,2,1,0:T(8,128)S(1)}, f32[4,4,128,128]{3,2,1,0:T(8,128)S(1)}, u32[]{:S(2)}, u32[]{:S(2)}) collective-permute-start(f32[4,4,128,128]{3,2,1,0:T(8,128)S(1)} %copy-done.26), channel_id=1, source_target_pairs={{0,2},{1,3},{2,0},{3,1},{4,6},{5,7},{6,4},{7,5},{8,10},{9,11},{10,... | collective-permute-start | bytes 3145736 | tf_op jit(solution)/shard_map/ppermute | solution.py:357
  355.3 46.0 %collective-permute-start.55 = (f32[4,4,128,128]{3,2,1,0:T(8,128)S(1)}, f32[4,4,128,128]{3,2,1,0:T(8,128)S(1)}, u32[]{:S(2)}, u32[]{:S(2)}) collective-permute-start(f32[4,4,128,128]{3,2,1,0:T(8,128)S(1)} %copy-done.27), channel_id=1, source_target_pairs={{0,2},{1,3},{2,0},{3,1},{4,6},{5,7},{6,4},{7,5},{8,10},{9,11},{10,... | collective-permute-start | bytes 3145736 | tf_op jit(solution)/shard_map/ppermute | solution.py:357
  365.0 28.0 %collective-permute-start.49 = (f32[4,128,128]{2,1,0:T(8,128)S(1)}, f32[4,128,128]{2,1,0:T(8,128)S(1)}, u32[]{:S(2)}, u32[]{:S(2)}) collective-permute-start(f32[4,128,128]{2,1,0:T(8,128)S(1)} %get-tuple-element.309), channel_id=1, source_target_pairs={{0,8},{4,12},{8,0},{12,4},{1,9},{5,13},{9,1},{13,5},{2,10},{6,14},... | collective-permute-start | bytes 786440 | tf_op jit(solution)/shard_map/ppermute | solution.py:361
  369.9 28.8 %collective-permute-start.52 = (f32[4,128,128]{2,1,0:T(8,128)S(1)}, f32[4,128,128]{2,1,0:T(8,128)S(1)}, u32[]{:S(2)}, u32[]{:S(2)}) collective-permute-start(f32[4,128,128]{2,1,0:T(8,128)S(1)} %get-tuple-element.317), channel_id=1, source_target_pairs={{0,4},{4,0},{8,12},{12,8},{1,5},{5,1},{9,13},{13,9},{2,6},{6,2},{1... | collective-permute-start | bytes 786440 | tf_op jit(solution)/shard_map/ppermute | solution.py:361
  394.3 23.6 %collective-permute-start.59 = (f32[4,4,128,128]{3,2,1,0:T(8,128)S(1)}, f32[4,4,128,128]{3,2,1,0:T(8,128)S(1)}, u32[]{:S(2)}, u32[]{:S(2)}) collective-permute-start(f32[4,4,128,128]{3,2,1,0:T(8,128)S(1)} %copy-done.28), channel_id=1, source_target_pairs={{0,2},{1,3},{2,0},{3,1},{4,6},{5,7},{6,4},{7,5},{8,10},{9,11},{10,... | collective-permute-start | bytes 3145736 | tf_op jit(solution)/shard_map/ppermute | solution.py:357
  401.3 37.2 %collective-permute-start.63 = (f32[4,4,128,128]{3,2,1,0:T(8,128)S(1)}, f32[4,4,128,128]{3,2,1,0:T(8,128)S(1)}, u32[]{:S(2)}, u32[]{:S(2)}) collective-permute-start(f32[4,4,128,128]{3,2,1,0:T(8,128)S(1)} %copy-done.29), channel_id=1, source_target_pairs={{0,2},{1,3},{2,0},{3,1},{4,6},{5,7},{6,4},{7,5},{8,10},{9,11},{10,... | collective-permute-start | bytes 3145736 | tf_op jit(solution)/shard_map/ppermute | solution.py:357
  403.5 26.3 %collective-permute-start.57 = (f32[4,128,128]{2,1,0:T(8,128)S(1)}, f32[4,128,128]{2,1,0:T(8,128)S(1)}, u32[]{:S(2)}, u32[]{:S(2)}) collective-permute-start(f32[4,128,128]{2,1,0:T(8,128)S(1)} %get-tuple-element.329), channel_id=1, source_target_pairs={{0,8},{4,12},{8,0},{12,4},{1,9},{5,13},{9,1},{13,5},{2,10},{6,14},... | collective-permute-start | bytes 786440 | tf_op jit(solution)/shard_map/ppermute | solution.py:361
  441.5 28.3 %collective-permute-start.64 = (f32[4,128,128]{2,1,0:T(8,128)S(1)}, f32[4,128,128]{2,1,0:T(8,128)}, u32[]{:S(2)}, u32[]{:S(2)}) collective-permute-start(f32[4,128,128]{2,1,0:T(8,128)S(1)} %get-tuple-element.347), channel_id=1, source_target_pairs={{0,4},{4,0},{8,12},{12,8},{1,5},{5,1},{9,13},{13,9},{2,6},{6,2},{1... | collective-permute-start | bytes 786440 | tf_op jit(solution)/shard_map/ppermute | solution.py:361
  (132 other events, 3918.6 us)

commit v6 on v5

--- a/solution.py
+++ b/solution.py
@@ -346,7 +346,7 @@
         pl.BlockSpec((2, block, zs, rank), lambda i, place: (1 - place[1], i, 0, 0)),
         pltpu.HBM(whole.shape, F32),
         aliases={1: 0},
-    )(place, *in_hbm(whole, *came))
+    )(place, *in_hbm(whole), *came)
 
 
 def after(value, *earlier):
@@ -402,7 +402,10 @@
         mine = add_up(place, keeps[i], came[i])
         line = [mine[0], None, None, None]
         for d, earlier in ((2, 1), (3, 2), (1, 3)):
-            part = after(mine[d], lines[-1][earlier]) if lines else mine[d]
+            ready = [lines[-1][earlier]] if lines else []
+            if i + 1 == len(X_PARTS) + len(R_PARTS) and d == 1:
+                ready.append(grams[-2])
+            part = after(mine[d], *ready)
             line[d] = z_swap(part, d)
         lines.append(line)
         if i >= count - 1:

time: 554 us -> 550 us (level)
    unnamed x160 -> x162, local copies, waits for them, and re-layouts: 11.7 us -> 10.2 us
  transfers between devices with their start and end apart: 79 -> 79, of which waited for: 37 -> 38; matrix products, arithmetic and copies ran while one was open for 5% -> 5% of each run, Pallas kernels for 20% -> 20%
where the time goes in v6:
time: 550 us; the launch traced here: 541 us
  waiting for transfers between devices  204 us (37%)
  starting transfers between devices  157 us (29%)
  Pallas kernels  138 us (25%)
  local copies, waits for them, and re-layouts  38.8 us (7%)
    ppermute x54, waiting for transfers between devices, z_swap(): return lax.ppermute(value, 'aa', [(i, i ^ d) for i in range(4)])  164 us
    ppermute x54, starting transfers between devices, z_swap(): return lax.ppermute(value, 'aa', [(i, i ^ d) for i in range(4)])  132 us
    pallas_call x10, Pallas kernels, project(): call('project_k', lambda place, *refs: project_kernel(parts, len(before),...  61.8 us
    ppermute x25, waiting for transfers between devices, pair_swap(): return lax.ppermute(value, 'ba', [(i, i ^ distance) for i in range(4)])  40.6 us
    pallas_call x9, Pallas kernels, add_gram(): call('gram_k', lambda place, *refs: gram_kernel(parts, place, *refs), (ro...  32.7 us
    squeeze x3, local copies, waits for them, and re-layouts, fast_body(): lax.dynamic_slice(slab_field, (first, start, 0, 0), (1, size, ys, zs))[0]  27 us
    ppermute x25, starting transfers between devices, pair_swap(): return lax.ppermute(value, 'ba', [(i, i ^ distance) for i in range(4)])  24.7 us
    pallas_call x2, Pallas kernels, core_of(): call('core_k', lambda place, *refs: core_kernel([len(group) for group in...  15.5 us
  transfers between devices with their start and end apart: 79, of which 38 were waited for; matrix products, arithmetic and copies ran while one was open for 5% of the time, Pallas kernels for 20%

profile of v6, /device:TPU:0, one launch (start us, length us, event | category | flops | bytes accessed | tf_op | source)
XLA Modules:
  0.0 540.7 jit_solution(8538597319896017882)
XLA Ops:
  15.9 12.2 %dynamic-slice_bitcast_fusion.1 = f32[112,128,256]{2,1,0:T(8,128)} fusion(f32[4,128,128,256]{3,2,1,0:T(8,128)} %refs_0_.19, s32[]{:T(128)S(6)} %select_n.61), kind=kLoop, calls=%fused_computation.1 | loop fusion | bytes 29360132 | tf_op jit(solution)/shard_map/squeeze | solution.py:435
  28.1 11.4 %collective-permute-done.1.recv_ref = f32[4,32,16,128]{3,2,1,0:T(8,128)S(1)} collective-permute-done((f32[4,32,16,128]{3,2,1,0:T(8,128)}, f32[4,32,16,128]{3,2,1,0:T(8,128)S(1)}, u32[]{:S(2)}, u32[]{:S(2)}) %collective-permute-start.1) | collective-permute-done | bytes 1048608 | tf_op jit(solution)/shard_map/ppermute | solution.py:357
  41.6 11.6 %dynamic-slice_bitcast_fusion = f32[128,128,256]{2,1,0:T(8,128)} fusion(f32[4,128,128,256]{3,2,1,0:T(8,128)} %refs_0_.19, s32[]{:T(128)S(6)} %select_n.62), kind=kLoop, calls=%fused_computation | loop fusion | bytes 33554436 | tf_op jit(solution)/shard_map/squeeze | solution.py:435
  68.6 9.1 %collective-permute-done.5.refs_9_ = f32[32,16,128]{2,1,0:T(8,128)S(1)} collective-permute-done((f32[32,16,128]{2,1,0:T(8,128)S(1)}, f32[32,16,128]{2,1,0:T(8,128)S(1)}, u32[]{:S(2)}, u32[]{:S(2)}) %collective-permute-start.5) | collective-permute-done | bytes 262176 | tf_op jit(solution)/shard_map/ppermute | solution.py:361
  96.3 9.8 %collective-permute-done.4.recv_ref = f32[4,32,16,128]{3,2,1,0:T(8,128)S(1)} collective-permute-done((f32[4,32,16,128]{3,2,1,0:T(8,128)S(1)}, f32[4,32,16,128]{3,2,1,0:T(8,128)S(1)}, u32[]{:S(2)}, u32[]{:S(2)}) %collective-permute-start.4) | collective-permute-done | bytes 1048608 | tf_op jit(solution)/shard_map/ppermute | solution.py:357
  125.0 8.5 %collective-permute-done.13.refs_11_ = f32[32,16,128]{2,1,0:T(8,128)S(1)} collective-permute-done((f32[32,16,128]{2,1,0:T(8,128)S(1)}, f32[32,16,128]{2,1,0:T(8,128)S(1)}, u32[]{:S(2)}, u32[]{:S(2)}) %collective-permute-start.13) | collective-permute-done | bytes 262176 | tf_op jit(solution)/shard_map/ppermute | solution.py:361
  160.7 13.2 %project_k.17 = (f32[4,4,128,128]{3,2,1,0:T(8,128)}, f32[4,4,128,128]{3,2,1,0:T(8,128)}, f32[4,4,128,128]{3,2,1,0:T(8,128)}, f32[4,4,128,128]{3,2,1,0:T(8,128)},...) custom-call(s32[3]{0:T(128)S(1)} %pad_add_fusion.place, ...), custom_call_target="tpu_custom_call" | custom-call | tf_op jit(solution)/shard_map/project_k/pallas_call | solution.py:92
  184.3 13.1 %project_k.19 = (f32[4,4,128,128]{3,2,1,0:T(8,128)}, f32[4,4,128,128]{3,2,1,0:T(8,128)}, f32[4,4,128,128]{3,2,1,0:T(8,128)}, f32[4,4,128,128]{3,2,1,0:T(8,128)},...) custom-call(s32[3]{0:T(128)S(1)} %pad_add_fusion.place, ...), custom_call_target="tpu_custom_call", output_to_operand_aliasing={{0}: (4, {}), {1}: (5, {}), {2}: (6, {}), {3}: (7, {}), {4}... | custom-call | tf_op jit(solution)/shard_map/project_k/pallas_call | solution.py:92
  215.9 9.1 %collective-permute-done.29.refs_22_ = f32[32,16,128]{2,1,0:T(8,128)S(1)} collective-permute-done((f32[32,16,128]{2,1,0:T(8,128)S(1)}, f32[32,16,128]{2,1,0:T(8,128)S(1)}, u32[]{:S(2)}, u32[]{:S(2)}) %collective-permute-start.29) | collective-permute-done | bytes 262176 | tf_op jit(solution)/shard_map/ppermute | solution.py:361
  241.3 10.3 %collective-permute-done.32.refs_23_ = f32[32,16,128]{2,1,0:T(8,128)S(1)} collective-permute-done((f32[32,16,128]{2,1,0:T(8,128)S(1)}, f32[32,16,128]{2,1,0:T(8,128)S(1)}, u32[]{:S(2)}, u32[]{:S(2)}) %collective-permute-start.32) | collective-permute-done | bytes 262176 | tf_op jit(solution)/shard_map/ppermute | solution.py:361
  258.0 7.3 %collective-permute-done.31.refs_16_ = f32[32,16,128]{2,1,0:T(8,128)S(1)} collective-permute-done((f32[32,16,128]{2,1,0:T(8,128)S(1)}, f32[32,16,128]{2,1,0:T(8,128)S(1)}, u32[]{:S(2)}, u32[]{:S(2)}) %collective-permute-start.31) | collective-permute-done | bytes 262176 | tf_op jit(solution)/shard_map/ppermute | solution.py:361
  265.3 8.8 %collective-permute-done.33.refs_24_ = f32[32,16,128]{2,1,0:T(8,128)S(1)} collective-permute-done((f32[32,16,128]{2,1,0:T(8,128)S(1)}, f32[32,16,128]{2,1,0:T(8,128)S(1)}, u32[]{:S(2)}, u32[]{:S(2)}) %collective-permute-start.33) | collective-permute-done | bytes 262176 | tf_op jit(solution)/shard_map/ppermute | solution.py:361
  284.4 10.9 %gram_k.9.refs_0_ = f32[768,256]{1,0:T(8,128)S(1)} custom-call(s32[3]{0:T(128)S(1)} %pad_add_fusion.place, f32[768,256]{1,0:T(8,128)S(1)} %broadcast_in_dim.3.refs_0_, f32[32,16,128]{2,1,0:T(8,128)} %copy-done.8, f32[32,16,128]{2,1,0:T(8,128)} %copy-done.9, f32[32,16,128]{2,1,0:T(8,128)} %copy-done.10, f32[32,16,128]{2,1,0:T(8,128)} %copy-done.11, ...), custom_call_target="tpu_custom_call" | custom-call | tf_op jit(solution)/shard_map/gram_k/pallas_call | solution.py:161
  315.9 11.6 %collective-permute-done.41.refs_3_.refs_7_ = f32[4,128,128]{2,1,0:T(8,128)S(1)} collective-permute-done((f32[4,128,128]{2,1,0:T(8,128)S(1)}, f32[4,128,128]{2,1,0:T(8,128)S(1)}, u32[]{:S(2)}, u32[]{:S(2)}) %collective-permute-start.41) | collective-permute-done | bytes 262176 | tf_op jit(solution)/shard_map/ppermute | solution.py:361
  342.7 11.4 %collective-permute-done.45.refs_3_.refs_11_ = f32[4,128,128]{2,1,0:T(8,128)S(1)} collective-permute-done((f32[4,128,128]{2,1,0:T(8,128)S(1)}, f32[4,128,128]{2,1,0:T(8,128)S(1)}, u32[]{:S(2)}, u32[]{:S(2)}) %collective-permute-start.45) | collective-permute-done | bytes 262176 | tf_op jit(solution)/shard_map/ppermute | solution.py:361
  356.9 7.0 %collective-permute-start.48 = (f32[4,128,128]{2,1,0:T(8,128)S(1)}, f32[4,128,128]{2,1,0:T(8,128)S(1)}, u32[]{:S(2)}, u32[]{:S(2)}) collective-permute-start(f32[4,128,128]{2,1,0:T(8,128)S(1)} %get-tuple-element.307), channel_id=1, source_target_pairs={{0,4},{4,0},{8,12},{12,8},{1,5},{5,1},{9,13},{13,9},{2,6},{6,2},{1... | collective-permute-start | bytes 786440 | tf_op jit(solution)/shard_map/ppermute | solution.py:361
  368.7 7.7 %collective-permute-start.52 = (f32[4,128,128]{2,1,0:T(8,128)S(1)}, f32[4,128,128]{2,1,0:T(8,128)S(1)}, u32[]{:S(2)}, u32[]{:S(2)}) collective-permute-start(f32[4,128,128]{2,1,0:T(8,128)S(1)} %get-tuple-element.317), channel_id=1, source_target_pairs={{0,4},{4,0},{8,12},{12,8},{1,5},{5,1},{9,13},{13,9},{2,6},{6,2},{1... | collective-permute-start | bytes 786440 | tf_op jit(solution)/shard_map/ppermute | solution.py:361
  376.7 15.1 %collective-permute-done.49.refs_3_.refs_15_ = f32[4,128,128]{2,1,0:T(8,128)S(1)} collective-permute-done((f32[4,128,128]{2,1,0:T(8,128)S(1)}, f32[4,128,128]{2,1,0:T(8,128)S(1)}, u32[]{:S(2)}, u32[]{:S(2)}) %collective-permute-start.49) | collective-permute-done | bytes 262176 | tf_op jit(solution)/shard_map/ppermute | solution.py:361
  402.3 9.3 %collective-permute-start.57 = (f32[4,128,128]{2,1,0:T(8,128)S(1)}, f32[4,128,128]{2,1,0:T(8,128)S(1)}, u32[]{:S(2)}, u32[]{:S(2)}) collective-permute-start(f32[4,128,128]{2,1,0:T(8,128)S(1)} %get-tuple-element.329), channel_id=1, source_target_pairs={{0,8},{4,12},{8,0},{12,4},{1,9},{5,13},{9,1},{13,5},{2,10},{6,14},... | collective-permute-start | bytes 786440 | tf_op jit(solution)/shard_map/ppermute | solution.py:361
  417.4 11.3 %collective-permute-done.57.refs_3_.refs_23_ = f32[4,128,128]{2,1,0:T(8,128)S(1)} collective-permute-done((f32[4,128,128]{2,1,0:T(8,128)S(1)}, f32[4,128,128]{2,1,0:T(8,128)S(1)}, u32[]{:S(2)}, u32[]{:S(2)}) %collective-permute-start.57) | collective-permute-done | bytes 262176 | tf_op jit(solution)/shard_map/ppermute | solution.py:361
  444.4 8.8 %collective-permute-start.64 = (f32[4,128,128]{2,1,0:T(8,128)S(1)}, f32[4,128,128]{2,1,0:T(8,128)S(1)}, u32[]{:S(2)}, u32[]{:S(2)}) collective-permute-start(f32[4,128,128]{2,1,0:T(8,128)S(1)} %get-tuple-element.347), channel_id=1, source_target_pairs={{0,4},{4,0},{8,12},{12,8},{1,5},{5,1},{9,13},{13,9},{2,6},{6,2},{1... | collective-permute-start | bytes 786440 | tf_op jit(solution)/shard_map/ppermute | solution.py:361
  504.2 14.9 %subspace_k.1.refs_0_ = f32[512,128]{1,0:T(8,128)S(1)} custom-call(s32[3]{0:T(128)S(1)} %pad_add_fusion.place, f32[16,48,256]{2,1,0:T(8,128)S(1)} %constant_dynamic-update-slice_fusion.5.pieces_ref, f32[512,128]{1,0:T(8,128)S(1)} %copy-done.24), custom_call_target="tpu_custom_call" | custom-call | tf_op jit(solution)/shard_map/subspace_k/pallas_call | solution.py:243
  519.2 7.3 %core_k.2 = (f32[4,32,64,128]{3,2,1,0:T(8,128)}, f32[32,64,128]{2,1,0:T(8,128)}) custom-call(s32[3]{0:T(128)S(1)} %pad_add_fusion.place, f32[512,128]{1,0:T(8,128)S(1)} %subspace_k.1.refs_0_, f32[32,16,128]{2,1,0:T(8,128)} %copy-done.8, f32[32,16,128]{2,1,0:T(8,128)} %copy-done.9, f32[32,16,128]{2,1,0:T(8,128)} %copy-done.10, f32[32,16,128]{2,1,0:T(8,128)} %copy-done.11, ...), custom_call_target="tpu_custom_call" | custom-call | tf_op jit(solution)/shard_map/core_k/pallas_call | solution.py:316
  526.6 8.2 %core_k.3 = (f32[4,32,64,128]{3,2,1,0:T(8,128)}, f32[32,64,128]{2,1,0:T(8,128)}) custom-call(s32[3]{0:T(128)S(1)} %pad_add_fusion.place, f32[512,128]{1,0:T(8,128)S(1)} %subspace_k.1.refs_0_, f32[4,128,128]{2,1,0:T(8,128)} %copy-done.16, f32[4,128,128]{2,1,0:T(8,128)} %copy-done.54, f32[4,128,128]{2,1,0:T(8,128)} %copy-done.55, ...), custom_call_target="tpu_custom_call", output_to_operand_aliasing={{0}: (34, {})} | custom-call | tf_op jit(solution)/shard_map/core_k/pallas_call | solution.py:316
  (352 shorter events, 290.3 us)
Async XLA Ops:
  13.0 26.5 %collective-permute-start.1 = (f32[4,32,16,128]{3,2,1,0:T(8,128)}, f32[4,32,16,128]{3,2,1,0:T(8,128)S(1)}, u32[]{:S(2)}, u32[]{:S(2)}) collective-permute-start(f32[4,32,16,128]{3,2,1,0:T(8,128)} %get-tuple-element.180), channel_id=1, source_target_pairs={{0,2},{1,3},{2,0},{3,1},{4,6},{5,7},{6,4},{7,5},{8,10},{9,11},{10,... | collective-permute-start | bytes 3145736 | tf_op jit(solution)/shard_map/ppermute | solution.py:357
  28.1 25.1 %collective-permute-start.2 = (f32[112,128,256]{2,1,0:T(8,128)}, f32[112,128,256]{2,1,0:T(8,128)}, u32[]{:S(2)}, u32[]{:S(2)}) collective-permute-start(f32[112,128,256]{2,1,0:T(8,128)} %dynamic-slice_bitcast_fusion.1), channel_id=1, source_target_pairs={{0,1},{1,0},{2,3},{3,2},{4,5},{5,4},{6,7},{7,6},{8,9},{9,8},{10,11... | collective-permute-start | bytes 44040200 | tf_op jit(solution)/shard_map/ppermute | solution.py:357
  53.2 107.5 %collective-permute-start.20 = (f32[128,128,256]{2,1,0:T(8,128)}, f32[128,128,256]{2,1,0:T(8,128)S(1)}, u32[]{:S(2)}, u32[]{:S(2)}) collective-permute-start(f32[128,128,256]{2,1,0:T(8,128)} %dynamic-slice_bitcast_fusion), channel_id=1, source_target_pairs={{0,1},{1,0},{2,3},{3,2},{4,5},{5,4},{6,7},{7,6},{8,9},{9,8},{10,11... | collective-permute-start | bytes 50331656 | tf_op jit(solution)/shard_map/ppermute | solution.py:357
  57.6 30.1 %collective-permute-start.3 = (f32[4,32,16,128]{3,2,1,0:T(8,128)S(1)}, f32[4,32,16,128]{3,2,1,0:T(8,128)S(1)}, u32[]{:S(2)}, u32[]{:S(2)}) collective-permute-start(f32[4,32,16,128]{3,2,1,0:T(8,128)S(1)} %get-tuple-element.184), channel_id=1, source_target_pairs={{0,2},{1,3},{2,0},{3,1},{4,6},{5,7},{6,4},{7,5},{8,10},{9,11},{10,... | collective-permute-start | bytes 3145736 | tf_op jit(solution)/shard_map/ppermute | solution.py:357
  63.8 42.3 %collective-permute-start.4 = (f32[4,32,16,128]{3,2,1,0:T(8,128)S(1)}, f32[4,32,16,128]{3,2,1,0:T(8,128)S(1)}, u32[]{:S(2)}, u32[]{:S(2)}) collective-permute-start(f32[4,32,16,128]{3,2,1,0:T(8,128)S(1)} %get-tuple-element.188), channel_id=1, source_target_pairs={{0,2},{1,3},{2,0},{3,1},{4,6},{5,7},{6,4},{7,5},{8,10},{9,11},{10,... | collective-permute-start | bytes 3145736 | tf_op jit(solution)/shard_map/ppermute | solution.py:357
  87.7 57.1 %collective-permute-start.8 = (f32[4,32,16,128]{3,2,1,0:T(8,128)S(1)}, f32[4,32,16,128]{3,2,1,0:T(8,128)S(1)}, u32[]{:S(2)}, u32[]{:S(2)}) collective-permute-start(f32[4,32,16,128]{3,2,1,0:T(8,128)S(1)} %get-tuple-element.195), channel_id=1, source_target_pairs={{0,2},{1,3},{2,0},{3,1},{4,6},{5,7},{6,4},{7,5},{8,10},{9,11},{10,... | collective-permute-start | bytes 3145736 | tf_op jit(solution)/shard_map/ppermute | solution.py:357
  90.6 23.8 %collective-permute-start.9 = (f32[32,16,128]{2,1,0:T(8,128)S(1)}, f32[32,16,128]{2,1,0:T(8,128)S(1)}, u32[]{:S(2)}, u32[]{:S(2)}) collective-permute-start(f32[32,16,128]{2,1,0:T(8,128)S(1)} %get-tuple-element.200), channel_id=1, source_target_pairs={{0,4},{4,0},{8,12},{12,8},{1,5},{5,1},{9,13},{13,9},{2,6},{6,2},{1... | collective-permute-start | bytes 786440 | tf_op jit(solution)/shard_map/ppermute | solution.py:361
  115.9 35.5 %collective-permute-start.12 = (f32[4,32,16,128]{3,2,1,0:T(8,128)S(1)}, f32[4,32,16,128]{3,2,1,0:T(8,128)S(1)}, u32[]{:S(2)}, u32[]{:S(2)}) collective-permute-start(f32[4,32,16,128]{3,2,1,0:T(8,128)S(1)} %get-tuple-element.205), channel_id=1, source_target_pairs={{0,2},{1,3},{2,0},{3,1},{4,6},{5,7},{6,4},{7,5},{8,10},{9,11},{10,... | collective-permute-start | bytes 3145736 | tf_op jit(solution)/shard_map/ppermute | solution.py:357
  144.8 52.8 %collective-permute-start.16 = (f32[4,32,16,128]{3,2,1,0:T(8,128)S(1)}, f32[4,32,16,128]{3,2,1,0:T(8,128)S(1)}, u32[]{:S(2)}, u32[]{:S(2)}) collective-permute-start(f32[4,32,16,128]{3,2,1,0:T(8,128)S(1)} %get-tuple-element.215), channel_id=1, source_target_pairs={{0,2},{1,3},{2,0},{3,1},{4,6},{5,7},{6,4},{7,5},{8,10},{9,11},{10,... | collective-permute-start | bytes 3145736 | tf_op jit(solution)/shard_map/ppermute | solution.py:357
  146.7 27.2 %collective-permute-start.17 = (f32[32,16,128]{2,1,0:T(8,128)S(1)}, f32[32,16,128]{2,1,0:T(8,128)S(1)}, u32[]{:S(2)}, u32[]{:S(2)}) collective-permute-start(f32[32,16,128]{2,1,0:T(8,128)S(1)} %get-tuple-element.220), channel_id=1, source_target_pairs={{0,4},{4,0},{8,12},{12,8},{1,5},{5,1},{9,13},{13,9},{2,6},{6,2},{1... | collective-permute-start | bytes 786440 | tf_op jit(solution)/shard_map/ppermute | solution.py:361
  151.0 22.9 %collective-permute-start.18 = (f32[32,16,128]{2,1,0:T(8,128)S(1)}, f32[32,16,128]{2,1,0:T(8,128)S(1)}, u32[]{:S(2)}, u32[]{:S(2)}) collective-permute-start(f32[32,16,128]{2,1,0:T(8,128)S(1)} %get-tuple-element.222), channel_id=1, source_target_pairs={{0,8},{4,12},{8,0},{12,4},{1,9},{5,13},{9,1},{13,5},{2,10},{6,14},... | collective-permute-start | bytes 786440 | tf_op jit(solution)/shard_map/ppermute | solution.py:361
  174.0 51.0 %collective-permute-start.21 = (f32[4,32,16,128]{3,2,1,0:T(8,128)S(1)}, f32[4,32,16,128]{3,2,1,0:T(8,128)S(1)}, u32[]{:S(2)}, u32[]{:S(2)}) collective-permute-start(f32[4,32,16,128]{3,2,1,0:T(8,128)S(1)} %get-tuple-element.227), channel_id=1, source_target_pairs={{0,2},{1,3},{2,0},{3,1},{4,6},{5,7},{6,4},{7,5},{8,10},{9,11},{10,... | collective-permute-start | bytes 3145736 | tf_op jit(solution)/shard_map/ppermute | solution.py:357
  197.5 33.8 %collective-permute-start.25 = (f32[4,32,16,128]{3,2,1,0:T(8,128)S(1)}, f32[4,32,16,128]{3,2,1,0:T(8,128)S(1)}, u32[]{:S(2)}, u32[]{:S(2)}) collective-permute-start(f32[4,32,16,128]{3,2,1,0:T(8,128)S(1)} %get-tuple-element.253), channel_id=1, source_target_pairs={{0,2},{1,3},{2,0},{3,1},{4,6},{5,7},{6,4},{7,5},{8,10},{9,11},{10,... | collective-permute-start | bytes 3145736 | tf_op jit(solution)/shard_map/ppermute | solution.py:357
  225.0 49.2 %collective-permute-start.35 = (f32[4,4,128,128]{3,2,1,0:T(8,128)}, f32[4,4,128,128]{3,2,1,0:T(8,128)S(1)}, u32[]{:S(2)}, u32[]{:S(2)}) collective-permute-start(f32[4,4,128,128]{3,2,1,0:T(8,128)} %get-tuple-element.274), channel_id=1, source_target_pairs={{0,2},{1,3},{2,0},{3,1},{4,6},{5,7},{6,4},{7,5},{8,10},{9,11},{10,... | collective-permute-start | bytes 3145736 | tf_op jit(solution)/shard_map/ppermute | solution.py:357
  251.7 49.5 %collective-permute-start.39 = (f32[4,4,128,128]{3,2,1,0:T(8,128)}, f32[4,4,128,128]{3,2,1,0:T(8,128)S(1)}, u32[]{:S(2)}, u32[]{:S(2)}) collective-permute-start(f32[4,4,128,128]{3,2,1,0:T(8,128)} %get-tuple-element.284), channel_id=1, source_target_pairs={{0,2},{1,3},{2,0},{3,1},{4,6},{5,7},{6,4},{7,5},{8,10},{9,11},{10,... | collective-permute-start | bytes 3145736 | tf_op jit(solution)/shard_map/ppermute | solution.py:357
  274.2 53.4 %collective-permute-start.43 = (f32[4,4,128,128]{3,2,1,0:T(8,128)}, f32[4,4,128,128]{3,2,1,0:T(8,128)S(1)}, u32[]{:S(2)}, u32[]{:S(2)}) collective-permute-start(f32[4,4,128,128]{3,2,1,0:T(8,128)} %get-tuple-element.294), channel_id=1, source_target_pairs={{0,2},{1,3},{2,0},{3,1},{4,6},{5,7},{6,4},{7,5},{8,10},{9,11},{10,... | collective-permute-start | bytes 3145736 | tf_op jit(solution)/shard_map/ppermute | solution.py:357
  301.2 52.9 %collective-permute-start.47 = (f32[4,4,128,128]{3,2,1,0:T(8,128)S(1)}, f32[4,4,128,128]{3,2,1,0:T(8,128)S(1)}, u32[]{:S(2)}, u32[]{:S(2)}) collective-permute-start(f32[4,4,128,128]{3,2,1,0:T(8,128)S(1)} %copy-done.25), channel_id=1, source_target_pairs={{0,2},{1,3},{2,0},{3,1},{4,6},{5,7},{6,4},{7,5},{8,10},{9,11},{10,... | collective-permute-start | bytes 3145736 | tf_op jit(solution)/shard_map/ppermute | solution.py:357
  327.5 40.5 %collective-permute-start.51 = (f32[4,4,128,128]{3,2,1,0:T(8,128)S(1)}, f32[4,4,128,128]{3,2,1,0:T(8,128)S(1)}, u32[]{:S(2)}, u32[]{:S(2)}) collective-permute-start(f32[4,4,128,128]{3,2,1,0:T(8,128)S(1)} %copy-done.26), channel_id=1, source_target_pairs={{0,2},{1,3},{2,0},{3,1},{4,6},{5,7},{6,4},{7,5},{8,10},{9,11},{10,... | collective-permute-start | bytes 3145736 | tf_op jit(solution)/shard_map/ppermute | solution.py:357
  354.1 46.0 %collective-permute-start.55 = (f32[4,4,128,128]{3,2,1,0:T(8,128)S(1)}, f32[4,4,128,128]{3,2,1,0:T(8,128)S(1)}, u32[]{:S(2)}, u32[]{:S(2)}) collective-permute-start(f32[4,4,128,128]{3,2,1,0:T(8,128)S(1)} %copy-done.27), channel_id=1, source_target_pairs={{0,2},{1,3},{2,0},{3,1},{4,6},{5,7},{6,4},{7,5},{8,10},{9,11},{10,... | collective-permute-start | bytes 3145736 | tf_op jit(solution)/shard_map/ppermute | solution.py:357
  363.8 28.0 %collective-permute-start.49 = (f32[4,128,128]{2,1,0:T(8,128)S(1)}, f32[4,128,128]{2,1,0:T(8,128)S(1)}, u32[]{:S(2)}, u32[]{:S(2)}) collective-permute-start(f32[4,128,128]{2,1,0:T(8,128)S(1)} %get-tuple-element.309), channel_id=1, source_target_pairs={{0,8},{4,12},{8,0},{12,4},{1,9},{5,13},{9,1},{13,5},{2,10},{6,14},... | collective-permute-start | bytes 786440 | tf_op jit(solution)/shard_map/ppermute | solution.py:361
  368.7 28.8 %collective-permute-start.52 = (f32[4,128,128]{2,1,0:T(8,128)S(1)}, f32[4,128,128]{2,1,0:T(8,128)S(1)}, u32[]{:S(2)}, u32[]{:S(2)}) collective-permute-start(f32[4,128,128]{2,1,0:T(8,128)S(1)} %get-tuple-element.317), channel_id=1, source_target_pairs={{0,4},{4,0},{8,12},{12,8},{1,5},{5,1},{9,13},{13,9},{2,6},{6,2},{1... | collective-permute-start | bytes 786440 | tf_op jit(solution)/shard_map/ppermute | solution.py:361
  393.1 23.6 %collective-permute-start.59 = (f32[4,4,128,128]{3,2,1,0:T(8,128)S(1)}, f32[4,4,128,128]{3,2,1,0:T(8,128)S(1)}, u32[]{:S(2)}, u32[]{:S(2)}) collective-permute-start(f32[4,4,128,128]{3,2,1,0:T(8,128)S(1)} %copy-done.28), channel_id=1, source_target_pairs={{0,2},{1,3},{2,0},{3,1},{4,6},{5,7},{6,4},{7,5},{8,10},{9,11},{10,... | collective-permute-start | bytes 3145736 | tf_op jit(solution)/shard_map/ppermute | solution.py:357
  400.1 42.9 %collective-permute-start.63 = (f32[4,4,128,128]{3,2,1,0:T(8,128)S(1)}, f32[4,4,128,128]{3,2,1,0:T(8,128)S(1)}, u32[]{:S(2)}, u32[]{:S(2)}) collective-permute-start(f32[4,4,128,128]{3,2,1,0:T(8,128)S(1)} %copy-done.29), channel_id=1, source_target_pairs={{0,2},{1,3},{2,0},{3,1},{4,6},{5,7},{6,4},{7,5},{8,10},{9,11},{10,... | collective-permute-start | bytes 3145736 | tf_op jit(solution)/shard_map/ppermute | solution.py:357
  402.3 26.4 %collective-permute-start.57 = (f32[4,128,128]{2,1,0:T(8,128)S(1)}, f32[4,128,128]{2,1,0:T(8,128)S(1)}, u32[]{:S(2)}, u32[]{:S(2)}) collective-permute-start(f32[4,128,128]{2,1,0:T(8,128)S(1)} %get-tuple-element.329), channel_id=1, source_target_pairs={{0,8},{4,12},{8,0},{12,4},{1,9},{5,13},{9,1},{13,5},{2,10},{6,14},... | collective-permute-start | bytes 786440 | tf_op jit(solution)/shard_map/ppermute | solution.py:361
  (133 other events, 3783.8 us)

commit v7 on v6

--- a/solution.py
+++ b/solution.py
@@ -11,7 +11,7 @@
 HIGHEST = lax.Precision.HIGHEST
 MIB = 1 << 20
 X_PARTS = (16,) * 8
-R_PARTS = (4,) * 8
+R_PARTS = (4,) * 7 + (2, 2)
 LANES = 128
 PAIRS = ((0, 0), (1, 0), (1, 1))
 

time: 550 us -> 561 us (1.020)
  waiting for transfers between devices: 204 us -> 214 us
    ppermute x54 -> x57, waiting for transfers between devices: 164 us -> 175 us  [z_swap(): return lax.ppermute(value, 'aa', [(i, i ^ d) for i in range(4)])]
    ppermute x54 -> x57, starting transfers between devices: 132 us -> 129 us  [z_swap(): return lax.ppermute(value, 'aa', [(i, i ^ d) for i in range(4)])]
    ppermute x25 -> x26, waiting for transfers between devices: 40.6 us -> 38.8 us  [pair_swap(): return lax.ppermute(value, 'ba', [(i, i ^ distance) for i in range(4)])]
    pallas_call x9 -> x10, Pallas kernels: 32.7 us -> 34.3 us  [add_gram(): call('gram_k', lambda place, *refs: gram_kernel(parts, place, *refs), (ro...]
    unnamed x162 -> x174, local copies, waits for them, and re-layouts: 10.2 us -> 11.5 us
    ppermute x25 -> x26, starting transfers between devices: 24.7 us -> 25.5 us  [pair_swap(): return lax.ppermute(value, 'ba', [(i, i ^ distance) for i in range(4)])]
    pallas_call x16 -> x17, Pallas kernels: 11.1 us -> 11.7 us  [add_up(): call('add_k', add_kernel, (rows // block,), [spec, spec], [out] * 4, [jax...]
  transfers between devices with their start and end apart: 79 -> 83, of which waited for: 38 -> 39; matrix products, arithmetic and copies ran while one was open for 5% -> 5% of each run, Pallas kernels for 20% -> 20%
where the time goes in v7:
time: 561 us; the launch traced here: 552 us
  waiting for transfers between devices  214 us (38%)
  starting transfers between devices  154 us (27%)
  Pallas kernels  140 us (25%)
  local copies, waits for them, and re-layouts  40.1 us (7%)
    ppermute x57, waiting for transfers between devices, z_swap(): return lax.ppermute(value, 'aa', [(i, i ^ d) for i in range(4)])  175 us
    ppermute x57, starting transfers between devices, z_swap(): return lax.ppermute(value, 'aa', [(i, i ^ d) for i in range(4)])  129 us
    pallas_call x10, Pallas kernels, project(): call('project_k', lambda place, *refs: project_kernel(parts, len(before),...  61.7 us
    ppermute x26, waiting for transfers between devices, pair_swap(): return lax.ppermute(value, 'ba', [(i, i ^ distance) for i in range(4)])  38.8 us
    pallas_call x10, Pallas kernels, add_gram(): call('gram_k', lambda place, *refs: gram_kernel(parts, place, *refs), (ro...  34.3 us
    squeeze x3, local copies, waits for them, and re-layouts, fast_body(): lax.dynamic_slice(slab_field, (first, start, 0, 0), (1, size, ys, zs))[0]  26.9 us
    ppermute x26, starting transfers between devices, pair_swap(): return lax.ppermute(value, 'ba', [(i, i ^ distance) for i in range(4)])  25.5 us
    pallas_call x2, Pallas kernels, core_of(): call('core_k', lambda place, *refs: core_kernel([len(group) for group in...  15.5 us
  transfers between devices with their start and end apart: 83, of which 39 were waited for; matrix products, arithmetic and copies ran while one was open for 5% of the time, Pallas kernels for 20%

profile of v7, /device:TPU:0, one launch (start us, length us, event | category | flops | bytes accessed | tf_op | source)
XLA Modules:
  0.0 551.7 jit_solution(1269065809865134086)
XLA Ops:
  15.9 12.2 %dynamic-slice_bitcast_fusion.1 = f32[112,128,256]{2,1,0:T(8,128)} fusion(f32[4,128,128,256]{3,2,1,0:T(8,128)} %refs_0_.19, s32[]{:T(128)S(6)} %select_n.61), kind=kLoop, calls=%fused_computation.1 | loop fusion | bytes 29360132 | tf_op jit(solution)/shard_map/squeeze | solution.py:435
  28.1 11.5 %collective-permute-done.1.recv_ref = f32[4,32,16,128]{3,2,1,0:T(8,128)S(1)} collective-permute-done((f32[4,32,16,128]{3,2,1,0:T(8,128)}, f32[4,32,16,128]{3,2,1,0:T(8,128)S(1)}, u32[]{:S(2)}, u32[]{:S(2)}) %collective-permute-start.1) | collective-permute-done | bytes 1048608 | tf_op jit(solution)/shard_map/ppermute | solution.py:357
  41.6 11.6 %dynamic-slice_bitcast_fusion = f32[128,128,256]{2,1,0:T(8,128)} fusion(f32[4,128,128,256]{3,2,1,0:T(8,128)} %refs_0_.19, s32[]{:T(128)S(6)} %select_n.62), kind=kLoop, calls=%fused_computation | loop fusion | bytes 33554436 | tf_op jit(solution)/shard_map/squeeze | solution.py:435
  68.6 9.1 %collective-permute-done.5.refs_9_ = f32[32,16,128]{2,1,0:T(8,128)S(1)} collective-permute-done((f32[32,16,128]{2,1,0:T(8,128)S(1)}, f32[32,16,128]{2,1,0:T(8,128)S(1)}, u32[]{:S(2)}, u32[]{:S(2)}) %collective-permute-start.5) | collective-permute-done | bytes 262176 | tf_op jit(solution)/shard_map/ppermute | solution.py:361
  96.3 9.8 %collective-permute-done.4.recv_ref = f32[4,32,16,128]{3,2,1,0:T(8,128)S(1)} collective-permute-done((f32[4,32,16,128]{3,2,1,0:T(8,128)S(1)}, f32[4,32,16,128]{3,2,1,0:T(8,128)S(1)}, u32[]{:S(2)}, u32[]{:S(2)}) %collective-permute-start.4) | collective-permute-done | bytes 1048608 | tf_op jit(solution)/shard_map/ppermute | solution.py:357
  125.0 8.5 %collective-permute-done.13.refs_11_ = f32[32,16,128]{2,1,0:T(8,128)S(1)} collective-permute-done((f32[32,16,128]{2,1,0:T(8,128)S(1)}, f32[32,16,128]{2,1,0:T(8,128)S(1)}, u32[]{:S(2)}, u32[]{:S(2)}) %collective-permute-start.13) | collective-permute-done | bytes 262176 | tf_op jit(solution)/shard_map/ppermute | solution.py:361
  157.7 13.2 %project_k.17 = (f32[4,4,128,128]{3,2,1,0:T(8,128)}, f32[4,4,128,128]{3,2,1,0:T(8,128)}, f32[4,4,128,128]{3,2,1,0:T(8,128)}, f32[4,4,128,128]{3,2,1,0:T(8,128)},...) custom-call(s32[3]{0:T(128)S(1)} %pad_add_fusion.place, ...), custom_call_target="tpu_custom_call" | custom-call | tf_op jit(solution)/shard_map/project_k/pallas_call | solution.py:92
  184.9 13.0 %project_k.19 = (f32[4,4,128,128]{3,2,1,0:T(8,128)}, f32[4,4,128,128]{3,2,1,0:T(8,128)}, f32[4,4,128,128]{3,2,1,0:T(8,128)}, f32[4,4,128,128]{3,2,1,0:T(8,128)},...) custom-call(s32[3]{0:T(128)S(1)} %pad_add_fusion.place, ...), custom_call_target="tpu_custom_call", output_to_operand_aliasing={{0}: (4, {}), {1}: (5, {}), {2}: (6, {}), {3}: (7, {}), {4}... | custom-call | tf_op jit(solution)/shard_map/project_k/pallas_call | solution.py:92
  205.7 6.5 %collective-permute-done.26.refs_14_ = f32[32,16,128]{2,1,0:T(8,128)S(1)} collective-permute-done((f32[32,16,128]{2,1,0:T(8,128)S(1)}, f32[32,16,128]{2,1,0:T(8,128)S(1)}, u32[]{:S(2)}, u32[]{:S(2)}) %collective-permute-start.26) | collective-permute-done | bytes 262176 | tf_op jit(solution)/shard_map/ppermute | solution.py:361
  217.7 8.0 %collective-permute-done.29.refs_22_ = f32[32,16,128]{2,1,0:T(8,128)S(1)} collective-permute-done((f32[32,16,128]{2,1,0:T(8,128)S(1)}, f32[32,16,128]{2,1,0:T(8,128)S(1)}, u32[]{:S(2)}, u32[]{:S(2)}) %collective-permute-start.29) | collective-permute-done | bytes 262176 | tf_op jit(solution)/shard_map/ppermute | solution.py:361
  232.1 8.0 %collective-permute-done.28.refs_15_ = f32[32,16,128]{2,1,0:T(8,128)S(1)} collective-permute-done((f32[32,16,128]{2,1,0:T(8,128)S(1)}, f32[32,16,128]{2,1,0:T(8,128)S(1)}, u32[]{:S(2)}, u32[]{:S(2)}) %collective-permute-start.28) | collective-permute-done | bytes 262176 | tf_op jit(solution)/shard_map/ppermute | solution.py:361
  242.9 8.7 %collective-permute-done.32.refs_23_ = f32[32,16,128]{2,1,0:T(8,128)S(1)} collective-permute-done((f32[32,16,128]{2,1,0:T(8,128)S(1)}, f32[32,16,128]{2,1,0:T(8,128)S(1)}, u32[]{:S(2)}, u32[]{:S(2)}) %collective-permute-start.32) | collective-permute-done | bytes 262176 | tf_op jit(solution)/shard_map/ppermute | solution.py:361
  261.8 13.1 %collective-permute-done.33.refs_24_ = f32[32,16,128]{2,1,0:T(8,128)S(1)} collective-permute-done((f32[32,16,128]{2,1,0:T(8,128)S(1)}, f32[32,16,128]{2,1,0:T(8,128)S(1)}, u32[]{:S(2)}, u32[]{:S(2)}) %collective-permute-start.33) | collective-permute-done | bytes 262176 | tf_op jit(solution)/shard_map/ppermute | solution.py:361
  285.2 10.8 %gram_k.10.refs_0_ = f32[768,256]{1,0:T(8,128)S(1)} custom-call(s32[3]{0:T(128)S(1)} %pad_add_fusion.place, f32[768,256]{1,0:T(8,128)S(1)} %broadcast_in_dim.3.refs_0_, f32[32,16,128]{2,1,0:T(8,128)} %copy-done.9, f32[32,16,128]{2,1,0:T(8,128)} %copy-done.10, f32[32,16,128]{2,1,0:T(8,128)} %copy-done.11, f32[32,16,128]{2,1,0:T(8,128)} %copy-done.12, ...), custom_call_target="tpu_custom_call" | custom-call | tf_op jit(solution)/shard_map/gram_k/pallas_call | solution.py:161
  316.5 12.4 %collective-permute-done.41.refs_3_.refs_7_ = f32[4,128,128]{2,1,0:T(8,128)S(1)} collective-permute-done((f32[4,128,128]{2,1,0:T(8,128)S(1)}, f32[4,128,128]{2,1,0:T(8,128)S(1)}, u32[]{:S(2)}, u32[]{:S(2)}) %collective-permute-start.41) | collective-permute-done | bytes 262176 | tf_op jit(solution)/shard_map/ppermute | solution.py:361
  342.9 12.7 %collective-permute-done.45.refs_3_.refs_11_ = f32[4,128,128]{2,1,0:T(8,128)S(1)} collective-permute-done((f32[4,128,128]{2,1,0:T(8,128)S(1)}, f32[4,128,128]{2,1,0:T(8,128)S(1)}, u32[]{:S(2)}, u32[]{:S(2)}) %collective-permute-start.45) | collective-permute-done | bytes 262176 | tf_op jit(solution)/shard_map/ppermute | solution.py:361
  368.3 12.7 %collective-permute-done.49.refs_3_.refs_15_ = f32[4,128,128]{2,1,0:T(8,128)S(1)} collective-permute-done((f32[4,128,128]{2,1,0:T(8,128)S(1)}, f32[4,128,128]{2,1,0:T(8,128)S(1)}, u32[]{:S(2)}, u32[]{:S(2)}) %collective-permute-start.49) | collective-permute-done | bytes 262176 | tf_op jit(solution)/shard_map/ppermute | solution.py:361
  392.9 10.6 %collective-permute-start.56 = (f32[4,128,128]{2,1,0:T(8,128)S(1)}, f32[4,128,128]{2,1,0:T(8,128)S(1)}, u32[]{:S(2)}, u32[]{:S(2)}) collective-permute-start(f32[4,128,128]{2,1,0:T(8,128)S(1)} %get-tuple-element.341), channel_id=1, source_target_pairs={{0,4},{4,0},{8,12},{12,8},{1,5},{5,1},{9,13},{13,9},{2,6},{6,2},{1... | collective-permute-start | bytes 786440 | tf_op jit(solution)/shard_map/ppermute | solution.py:361
  405.2 13.3 %collective-permute-done.53.refs_3_.refs_19_ = f32[4,128,128]{2,1,0:T(8,128)S(1)} collective-permute-done((f32[4,128,128]{2,1,0:T(8,128)S(1)}, f32[4,128,128]{2,1,0:T(8,128)S(1)}, u32[]{:S(2)}, u32[]{:S(2)}) %collective-permute-start.53) | collective-permute-done | bytes 262176 | tf_op jit(solution)/shard_map/ppermute | solution.py:361
  436.4 14.6 %collective-permute-done.61.refs_3_.refs_27_ = f32[4,128,128]{2,1,0:T(8,128)S(1)} collective-permute-done((f32[4,128,128]{2,1,0:T(8,128)S(1)}, f32[4,128,128]{2,1,0:T(8,128)S(1)}, u32[]{:S(2)}, u32[]{:S(2)}) %collective-permute-start.61) | collective-permute-done | bytes 262176 | tf_op jit(solution)/shard_map/ppermute | solution.py:361
  454.4 7.0 %collective-permute-start.64 = (f32[2,128,128]{2,1,0:T(8,128)S(1)}, f32[2,128,128]{2,1,0:T(8,128)S(1)}, u32[]{:S(2)}, u32[]{:S(2)}) collective-permute-start(f32[2,128,128]{2,1,0:T(8,128)S(1)} %get-tuple-element.361), channel_id=1, source_target_pairs={{0,4},{4,0},{8,12},{12,8},{1,5},{5,1},{9,13},{13,9},{2,6},{6,2},{1... | collective-permute-start | bytes 393224 | tf_op jit(solution)/shard_map/ppermute | solution.py:361
  515.3 14.9 %subspace_k.1.refs_0_ = f32[512,128]{1,0:T(8,128)S(1)} custom-call(s32[3]{0:T(128)S(1)} %pad_add_fusion.place, f32[16,48,256]{2,1,0:T(8,128)S(1)} %constant_dynamic-update-slice_fusion.5.pieces_ref, f32[512,128]{1,0:T(8,128)S(1)} %copy-done.26), custom_call_target="tpu_custom_call" | custom-call | tf_op jit(solution)/shard_map/subspace_k/pallas_call | solution.py:243
  530.3 7.2 %core_k.2 = (f32[4,32,64,128]{3,2,1,0:T(8,128)}, f32[32,64,128]{2,1,0:T(8,128)}) custom-call(s32[3]{0:T(128)S(1)} %pad_add_fusion.place, f32[512,128]{1,0:T(8,128)S(1)} %subspace_k.1.refs_0_, f32[32,16,128]{2,1,0:T(8,128)} %copy-done.9, f32[32,16,128]{2,1,0:T(8,128)} %copy-done.10, f32[32,16,128]{2,1,0:T(8,128)} %copy-done.11, f32[32,16,128]{2,1,0:T(8,128)} %copy-done.12, ...), custom_call_target="tpu_custom_call" | custom-call | tf_op jit(solution)/shard_map/core_k/pallas_call | solution.py:316
  537.7 8.2 %core_k.3 = (f32[4,32,64,128]{3,2,1,0:T(8,128)}, f32[32,64,128]{2,1,0:T(8,128)}) custom-call(s32[3]{0:T(128)S(1)} %pad_add_fusion.place, f32[512,128]{1,0:T(8,128)S(1)} %subspace_k.1.refs_0_, f32[4,128,128]{2,1,0:T(8,128)} %copy-done.17, f32[4,128,128]{2,1,0:T(8,128)} %copy-done.55, f32[4,128,128]{2,1,0:T(8,128)} %copy-done.56, ...), custom_call_target="tpu_custom_call", output_to_operand_aliasing={{0}: (38, {})} | custom-call | tf_op jit(solution)/shard_map/core_k/pallas_call | solution.py:316
  (374 shorter events, 291.6 us)
Async XLA Ops:
  13.0 26.5 %collective-permute-start.1 = (f32[4,32,16,128]{3,2,1,0:T(8,128)}, f32[4,32,16,128]{3,2,1,0:T(8,128)S(1)}, u32[]{:S(2)}, u32[]{:S(2)}) collective-permute-start(f32[4,32,16,128]{3,2,1,0:T(8,128)} %get-tuple-element.192), channel_id=1, source_target_pairs={{0,2},{1,3},{2,0},{3,1},{4,6},{5,7},{6,4},{7,5},{8,10},{9,11},{10,... | collective-permute-start | bytes 3145736 | tf_op jit(solution)/shard_map/ppermute | solution.py:357
  28.1 25.1 %collective-permute-start.2 = (f32[112,128,256]{2,1,0:T(8,128)}, f32[112,128,256]{2,1,0:T(8,128)}, u32[]{:S(2)}, u32[]{:S(2)}) collective-permute-start(f32[112,128,256]{2,1,0:T(8,128)} %dynamic-slice_bitcast_fusion.1), channel_id=1, source_target_pairs={{0,1},{1,0},{2,3},{3,2},{4,5},{5,4},{6,7},{7,6},{8,9},{9,8},{10,11... | collective-permute-start | bytes 44040200 | tf_op jit(solution)/shard_map/ppermute | solution.py:357
  53.2 98.2 %collective-permute-start.20 = (f32[128,128,256]{2,1,0:T(8,128)}, f32[128,128,256]{2,1,0:T(8,128)S(1)}, u32[]{:S(2)}, u32[]{:S(2)}) collective-permute-start(f32[128,128,256]{2,1,0:T(8,128)} %dynamic-slice_bitcast_fusion), channel_id=1, source_target_pairs={{0,1},{1,0},{2,3},{3,2},{4,5},{5,4},{6,7},{7,6},{8,9},{9,8},{10,11... | collective-permute-start | bytes 50331656 | tf_op jit(solution)/shard_map/ppermute | solution.py:357
  57.6 30.1 %collective-permute-start.3 = (f32[4,32,16,128]{3,2,1,0:T(8,128)S(1)}, f32[4,32,16,128]{3,2,1,0:T(8,128)S(1)}, u32[]{:S(2)}, u32[]{:S(2)}) collective-permute-start(f32[4,32,16,128]{3,2,1,0:T(8,128)S(1)} %get-tuple-element.196), channel_id=1, source_target_pairs={{0,2},{1,3},{2,0},{3,1},{4,6},{5,7},{6,4},{7,5},{8,10},{9,11},{10,... | collective-permute-start | bytes 3145736 | tf_op jit(solution)/shard_map/ppermute | solution.py:357
  63.8 42.3 %collective-permute-start.4 = (f32[4,32,16,128]{3,2,1,0:T(8,128)S(1)}, f32[4,32,16,128]{3,2,1,0:T(8,128)S(1)}, u32[]{:S(2)}, u32[]{:S(2)}) collective-permute-start(f32[4,32,16,128]{3,2,1,0:T(8,128)S(1)} %get-tuple-element.200), channel_id=1, source_target_pairs={{0,2},{1,3},{2,0},{3,1},{4,6},{5,7},{6,4},{7,5},{8,10},{9,11},{10,... | collective-permute-start | bytes 3145736 | tf_op jit(solution)/shard_map/ppermute | solution.py:357
  87.7 57.0 %collective-permute-start.8 = (f32[4,32,16,128]{3,2,1,0:T(8,128)S(1)}, f32[4,32,16,128]{3,2,1,0:T(8,128)S(1)}, u32[]{:S(2)}, u32[]{:S(2)}) collective-permute-start(f32[4,32,16,128]{3,2,1,0:T(8,128)S(1)} %get-tuple-element.207), channel_id=1, source_target_pairs={{0,2},{1,3},{2,0},{3,1},{4,6},{5,7},{6,4},{7,5},{8,10},{9,11},{10,... | collective-permute-start | bytes 3145736 | tf_op jit(solution)/shard_map/ppermute | solution.py:357
  90.6 23.7 %collective-permute-start.9 = (f32[32,16,128]{2,1,0:T(8,128)S(1)}, f32[32,16,128]{2,1,0:T(8,128)S(1)}, u32[]{:S(2)}, u32[]{:S(2)}) collective-permute-start(f32[32,16,128]{2,1,0:T(8,128)S(1)} %get-tuple-element.212), channel_id=1, source_target_pairs={{0,4},{4,0},{8,12},{12,8},{1,5},{5,1},{9,13},{13,9},{2,6},{6,2},{1... | collective-permute-start | bytes 786440 | tf_op jit(solution)/shard_map/ppermute | solution.py:361
  115.9 55.1 %collective-permute-start.12 = (f32[4,32,16,128]{3,2,1,0:T(8,128)S(1)}, f32[4,32,16,128]{3,2,1,0:T(8,128)S(1)}, u32[]{:S(2)}, u32[]{:S(2)}) collective-permute-start(f32[4,32,16,128]{3,2,1,0:T(8,128)S(1)} %get-tuple-element.217), channel_id=1, source_target_pairs={{0,2},{1,3},{2,0},{3,1},{4,6},{5,7},{6,4},{7,5},{8,10},{9,11},{10,... | collective-permute-start | bytes 3145736 | tf_op jit(solution)/shard_map/ppermute | solution.py:357
  144.7 53.5 %collective-permute-start.16 = (f32[4,32,16,128]{3,2,1,0:T(8,128)S(1)}, f32[4,32,16,128]{3,2,1,0:T(8,128)S(1)}, u32[]{:S(2)}, u32[]{:S(2)}) collective-permute-start(f32[4,32,16,128]{3,2,1,0:T(8,128)S(1)} %get-tuple-element.227), channel_id=1, source_target_pairs={{0,2},{1,3},{2,0},{3,1},{4,6},{5,7},{6,4},{7,5},{8,10},{9,11},{10,... | collective-permute-start | bytes 3145736 | tf_op jit(solution)/shard_map/ppermute | solution.py:357
  146.7 24.3 %collective-permute-start.17 = (f32[32,16,128]{2,1,0:T(8,128)S(1)}, f32[32,16,128]{2,1,0:T(8,128)S(1)}, u32[]{:S(2)}, u32[]{:S(2)}) collective-permute-start(f32[32,16,128]{2,1,0:T(8,128)S(1)} %get-tuple-element.232), channel_id=1, source_target_pairs={{0,4},{4,0},{8,12},{12,8},{1,5},{5,1},{9,13},{13,9},{2,6},{6,2},{1... | collective-permute-start | bytes 786440 | tf_op jit(solution)/shard_map/ppermute | solution.py:361
  171.7 54.0 %collective-permute-start.21 = (f32[4,32,16,128]{3,2,1,0:T(8,128)S(1)}, f32[4,32,16,128]{3,2,1,0:T(8,128)S(1)}, u32[]{:S(2)}, u32[]{:S(2)}) collective-permute-start(f32[4,32,16,128]{3,2,1,0:T(8,128)S(1)} %get-tuple-element.239), channel_id=1, source_target_pairs={{0,2},{1,3},{2,0},{3,1},{4,6},{5,7},{6,4},{7,5},{8,10},{9,11},{10,... | collective-permute-start | bytes 3145736 | tf_op jit(solution)/shard_map/ppermute | solution.py:357
  198.2 33.9 %collective-permute-start.25 = (f32[4,32,16,128]{3,2,1,0:T(8,128)S(1)}, f32[4,32,16,128]{3,2,1,0:T(8,128)S(1)}, u32[]{:S(2)}, u32[]{:S(2)}) collective-permute-start(f32[4,32,16,128]{3,2,1,0:T(8,128)S(1)} %get-tuple-element.267), channel_id=1, source_target_pairs={{0,2},{1,3},{2,0},{3,1},{4,6},{5,7},{6,4},{7,5},{8,10},{9,11},{10,... | collective-permute-start | bytes 3145736 | tf_op jit(solution)/shard_map/ppermute | solution.py:357
  225.7 49.2 %collective-permute-start.35 = (f32[4,4,128,128]{3,2,1,0:T(8,128)}, f32[4,4,128,128]{3,2,1,0:T(8,128)S(1)}, u32[]{:S(2)}, u32[]{:S(2)}) collective-permute-start(f32[4,4,128,128]{3,2,1,0:T(8,128)} %get-tuple-element.288), channel_id=1, source_target_pairs={{0,2},{1,3},{2,0},{3,1},{4,6},{5,7},{6,4},{7,5},{8,10},{9,11},{10,... | collective-permute-start | bytes 3145736 | tf_op jit(solution)/shard_map/ppermute | solution.py:357
  251.6 50.8 %collective-permute-start.39 = (f32[4,4,128,128]{3,2,1,0:T(8,128)}, f32[4,4,128,128]{3,2,1,0:T(8,128)S(1)}, u32[]{:S(2)}, u32[]{:S(2)}) collective-permute-start(f32[4,4,128,128]{3,2,1,0:T(8,128)} %get-tuple-element.298), channel_id=1, source_target_pairs={{0,2},{1,3},{2,0},{3,1},{4,6},{5,7},{6,4},{7,5},{8,10},{9,11},{10,... | collective-permute-start | bytes 3145736 | tf_op jit(solution)/shard_map/ppermute | solution.py:357
  274.9 54.0 %collective-permute-start.43 = (f32[4,4,128,128]{3,2,1,0:T(8,128)}, f32[4,4,128,128]{3,2,1,0:T(8,128)S(1)}, u32[]{:S(2)}, u32[]{:S(2)}) collective-permute-start(f32[4,4,128,128]{3,2,1,0:T(8,128)} %get-tuple-element.308), channel_id=1, source_target_pairs={{0,2},{1,3},{2,0},{3,1},{4,6},{5,7},{6,4},{7,5},{8,10},{9,11},{10,... | collective-permute-start | bytes 3145736 | tf_op jit(solution)/shard_map/ppermute | solution.py:357
  302.4 53.2 %collective-permute-start.47 = (f32[4,4,128,128]{3,2,1,0:T(8,128)S(1)}, f32[4,4,128,128]{3,2,1,0:T(8,128)S(1)}, u32[]{:S(2)}, u32[]{:S(2)}) collective-permute-start(f32[4,4,128,128]{3,2,1,0:T(8,128)S(1)} %copy-done.27), channel_id=1, source_target_pairs={{0,2},{1,3},{2,0},{3,1},{4,6},{5,7},{6,4},{7,5},{8,10},{9,11},{10,... | collective-permute-start | bytes 3145736 | tf_op jit(solution)/shard_map/ppermute | solution.py:357
  328.9 52.2 %collective-permute-start.51 = (f32[4,4,128,128]{3,2,1,0:T(8,128)S(1)}, f32[4,4,128,128]{3,2,1,0:T(8,128)S(1)}, u32[]{:S(2)}, u32[]{:S(2)}) collective-permute-start(f32[4,4,128,128]{3,2,1,0:T(8,128)S(1)} %copy-done.28), channel_id=1, source_target_pairs={{0,2},{1,3},{2,0},{3,1},{4,6},{5,7},{6,4},{7,5},{8,10},{9,11},{10,... | collective-permute-start | bytes 3145736 | tf_op jit(solution)/shard_map/ppermute | solution.py:357
  355.6 36.6 %collective-permute-start.55 = (f32[4,4,128,128]{3,2,1,0:T(8,128)S(1)}, f32[4,4,128,128]{3,2,1,0:T(8,128)S(1)}, u32[]{:S(2)}, u32[]{:S(2)}) collective-permute-start(f32[4,4,128,128]{3,2,1,0:T(8,128)S(1)} %copy-done.29), channel_id=1, source_target_pairs={{0,2},{1,3},{2,0},{3,1},{4,6},{5,7},{6,4},{7,5},{8,10},{9,11},{10,... | collective-permute-start | bytes 3145736 | tf_op jit(solution)/shard_map/ppermute | solution.py:357
  381.1 46.4 %collective-permute-start.59 = (f32[4,4,128,128]{3,2,1,0:T(8,128)S(1)}, f32[4,4,128,128]{3,2,1,0:T(8,128)S(1)}, u32[]{:S(2)}, u32[]{:S(2)}) collective-permute-start(f32[4,4,128,128]{3,2,1,0:T(8,128)S(1)} %copy-done.30), channel_id=1, source_target_pairs={{0,2},{1,3},{2,0},{3,1},{4,6},{5,7},{6,4},{7,5},{8,10},{9,11},{10,... | collective-permute-start | bytes 3145736 | tf_op jit(solution)/shard_map/ppermute | solution.py:357
  392.2 26.3 %collective-permute-start.53 = (f32[4,128,128]{2,1,0:T(8,128)S(1)}, f32[4,128,128]{2,1,0:T(8,128)S(1)}, u32[]{:S(2)}, u32[]{:S(2)}) collective-permute-start(f32[4,128,128]{2,1,0:T(8,128)S(1)} %get-tuple-element.333), channel_id=1, source_target_pairs={{0,8},{4,12},{8,0},{12,4},{1,9},{5,13},{9,1},{13,5},{2,10},{6,14},... | collective-permute-start | bytes 786440 | tf_op jit(solution)/shard_map/ppermute | solution.py:361
  392.9 34.5 %collective-permute-start.56 = (f32[4,128,128]{2,1,0:T(8,128)S(1)}, f32[4,128,128]{2,1,0:T(8,128)S(1)}, u32[]{:S(2)}, u32[]{:S(2)}) collective-permute-start(f32[4,128,128]{2,1,0:T(8,128)S(1)} %get-tuple-element.341), channel_id=1, source_target_pairs={{0,4},{4,0},{8,12},{12,8},{1,5},{5,1},{9,13},{13,9},{2,6},{6,2},{1... | collective-permute-start | bytes 786440 | tf_op jit(solution)/shard_map/ppermute | solution.py:361
  403.5 23.9 %collective-permute-start.57 = (f32[4,128,128]{2,1,0:T(8,128)S(1)}, f32[4,128,128]{2,1,0:T(8,128)S(1)}, u32[]{:S(2)}, u32[]{:S(2)}) collective-permute-start(f32[4,128,128]{2,1,0:T(8,128)S(1)} %get-tuple-element.343), channel_id=1, source_target_pairs={{0,8},{4,12},{8,0},{12,4},{1,9},{5,13},{9,1},{13,5},{2,10},{6,14},... | collective-permute-start | bytes 786440 | tf_op jit(solution)/shard_map/ppermute | solution.py:361
  427.4 39.5 %collective-permute-start.67 = (f32[4,2,128,128]{3,2,1,0:T(8,128)S(1)}, f32[4,2,128,128]{3,2,1,0:T(8,128)S(1)}, u32[]{:S(2)}, u32[]{:S(2)}) collective-permute-start(f32[4,2,128,128]{3,2,1,0:T(8,128)S(1)} %copy-done.77), channel_id=1, source_target_pairs={{0,2},{1,3},{2,0},{3,1},{4,6},{5,7},{6,4},{7,5},{8,10},{9,11},{10,... | collective-permute-start | bytes 1572872 | tf_op jit(solution)/shard_map/ppermute | solution.py:357
  435.1 26.3 %collective-permute-start.60 = (f32[4,128,128]{2,1,0:T(8,128)S(1)}, f32[4,128,128]{2,1,0:T(8,128)S(1)}, u32[]{:S(2)}, u32[]{:S(2)}) collective-permute-start(f32[4,128,128]{2,1,0:T(8,128)S(1)} %get-tuple-element.351), channel_id=1, source_target_pairs={{0,4},{4,0},{8,12},{12,8},{1,5},{5,1},{9,13},{13,9},{2,6},{6,2},{1... | collective-permute-start | bytes 786440 | tf_op jit(solution)/shard_map/ppermute | solution.py:361
  (143 other events, 4216.9 us)

commit v8 on v6

--- a/solution.py
+++ b/solution.py
@@ -416,7 +416,7 @@
         i = len(came)
         earlier = []
         if i >= 2:
-            earlier = [came[i - 2]] + (lines[i - 3][1:] if i >= 3 else [])
+            earlier = [came[i - 2]] + (lines[i - 3][2:3] if i >= 3 else []) + (lines[i - 4][1:] if i >= 4 else [])
         if i in (6, 7):
             earlier.append(halves[i - 6])
         if i >= count + 3:

time: 550 us -> 547 us (level)
  starting transfers between devices: 157 us -> 142 us
  waiting for transfers between devices: 204 us -> 215 us
    ppermute x54, waiting for transfers between devices: 164 us -> 180 us  [z_swap(): return lax.ppermute(value, 'aa', [(i, i ^ d) for i in range(4)])]
    ppermute x54, starting transfers between devices: 132 us -> 116 us  [z_swap(): return lax.ppermute(value, 'aa', [(i, i ^ d) for i in range(4)])]
    ppermute x25, waiting for transfers between devices: 40.6 us -> 34.5 us  [pair_swap(): return lax.ppermute(value, 'ba', [(i, i ^ distance) for i in range(4)])]
    unnamed x162 -> x166, local copies, waits for them, and re-layouts: 10.2 us -> 12.2 us
  transfers between devices with their start and end apart: 79 -> 79, of which waited for: 38 -> 43; matrix products, arithmetic and copies ran while one was open for 5% -> 5% of each run, Pallas kernels for 20% -> 20%
where the time goes in v8:
time: 547 us; the launch traced here: 538 us
  waiting for transfers between devices  215 us (39%)
  starting transfers between devices  142 us (26%)
  Pallas kernels  138 us (25%)
  local copies, waits for them, and re-layouts  40.8 us (7%)
    ppermute x54, waiting for transfers between devices, z_swap(): return lax.ppermute(value, 'aa', [(i, i ^ d) for i in range(4)])  180 us
    ppermute x54, starting transfers between devices, z_swap(): return lax.ppermute(value, 'aa', [(i, i ^ d) for i in range(4)])  116 us
    pallas_call x10, Pallas kernels, project(): call('project_k', lambda place, *refs: project_kernel(parts, len(before),...  61.8 us
    ppermute x25, waiting for transfers between devices, pair_swap(): return lax.ppermute(value, 'ba', [(i, i ^ distance) for i in range(4)])  34.5 us
    pallas_call x9, Pallas kernels, add_gram(): call('gram_k', lambda place, *refs: gram_kernel(parts, place, *refs), (ro...  32.5 us
    squeeze x3, local copies, waits for them, and re-layouts, fast_body(): lax.dynamic_slice(slab_field, (first, start, 0, 0), (1, size, ys, zs))[0]  26.9 us
    ppermute x25, starting transfers between devices, pair_swap(): return lax.ppermute(value, 'ba', [(i, i ^ distance) for i in range(4)])  25.1 us
    pallas_call x2, Pallas kernels, core_of(): call('core_k', lambda place, *refs: core_kernel([len(group) for group in...  15.5 us
  transfers between devices with their start and end apart: 79, of which 43 were waited for; matrix products, arithmetic and copies ran while one was open for 5% of the time, Pallas kernels for 20%

profile of v8, /device:TPU:0, one launch (start us, length us, event | category | flops | bytes accessed | tf_op | source)
XLA Modules:
  0.0 537.8 jit_solution(9122809573932367770)
XLA Ops:
  15.9 12.2 %dynamic-slice_bitcast_fusion.1 = f32[112,128,256]{2,1,0:T(8,128)} fusion(f32[4,128,128,256]{3,2,1,0:T(8,128)} %refs_0_.19, s32[]{:T(128)S(6)} %select_n.61), kind=kLoop, calls=%fused_computation.1 | loop fusion | bytes 29360132 | tf_op jit(solution)/shard_map/squeeze | solution.py:435
  28.1 11.4 %collective-permute-done.1.recv_ref = f32[4,32,16,128]{3,2,1,0:T(8,128)S(1)} collective-permute-done((f32[4,32,16,128]{3,2,1,0:T(8,128)}, f32[4,32,16,128]{3,2,1,0:T(8,128)S(1)}, u32[]{:S(2)}, u32[]{:S(2)}) %collective-permute-start.1) | collective-permute-done | bytes 1048608 | tf_op jit(solution)/shard_map/ppermute | solution.py:357
  42.3 11.6 %dynamic-slice_bitcast_fusion = f32[128,128,256]{2,1,0:T(8,128)} fusion(f32[4,128,128,256]{3,2,1,0:T(8,128)} %refs_0_.19, s32[]{:T(128)S(6)} %select_n.62), kind=kLoop, calls=%fused_computation | loop fusion | bytes 33554436 | tf_op jit(solution)/shard_map/squeeze | solution.py:435
  72.1 7.8 %collective-permute-done.5.refs_17_ = f32[32,16,128]{2,1,0:T(8,128)S(1)} collective-permute-done((f32[32,16,128]{2,1,0:T(8,128)}, f32[32,16,128]{2,1,0:T(8,128)S(1)}, u32[]{:S(2)}, u32[]{:S(2)}) %collective-permute-start.5) | collective-permute-done | bytes 262176 | tf_op jit(solution)/shard_map/ppermute | solution.py:361
  124.1 11.7 %collective-permute-done.12.refs_19_ = f32[32,16,128]{2,1,0:T(8,128)S(1)} collective-permute-done((f32[32,16,128]{2,1,0:T(8,128)S(1)}, f32[32,16,128]{2,1,0:T(8,128)S(1)}, u32[]{:S(2)}, u32[]{:S(2)}) %collective-permute-start.12) | collective-permute-done | bytes 262176 | tf_op jit(solution)/shard_map/ppermute | solution.py:361
  152.5 8.2 %collective-permute-start.20 = (f32[32,16,128]{2,1,0:T(8,128)S(1)}, f32[32,16,128]{2,1,0:T(8,128)S(1)}, u32[]{:S(2)}, u32[]{:S(2)}) collective-permute-start(f32[32,16,128]{2,1,0:T(8,128)S(1)} %get-tuple-element.229), channel_id=1, source_target_pairs={{0,4},{4,0},{8,12},{12,8},{1,5},{5,1},{9,13},{13,9},{2,6},{6,2},{1... | collective-permute-start | bytes 786440 | tf_op jit(solution)/shard_map/ppermute | solution.py:361
  168.8 13.2 %project_k.17 = (f32[4,4,128,128]{3,2,1,0:T(8,128)}, f32[4,4,128,128]{3,2,1,0:T(8,128)}, f32[4,4,128,128]{3,2,1,0:T(8,128)}, f32[4,4,128,128]{3,2,1,0:T(8,128)},...) custom-call(s32[3]{0:T(128)S(1)} %pad_add_fusion.place, ...), custom_call_target="tpu_custom_call" | custom-call | tf_op jit(solution)/shard_map/project_k/pallas_call | solution.py:92
  186.6 13.1 %project_k.19 = (f32[4,4,128,128]{3,2,1,0:T(8,128)}, f32[4,4,128,128]{3,2,1,0:T(8,128)}, f32[4,4,128,128]{3,2,1,0:T(8,128)}, f32[4,4,128,128]{3,2,1,0:T(8,128)},...) custom-call(s32[3]{0:T(128)S(1)} %pad_add_fusion.place, ...), custom_call_target="tpu_custom_call", output_to_operand_aliasing={{0}: (4, {}), {1}: (5, {}), {2}: (6, {}), {3}: (7, {}), {4}... | custom-call | tf_op jit(solution)/shard_map/project_k/pallas_call | solution.py:92
  216.7 7.6 %collective-permute-start.26 = (f32[32,16,128]{2,1,0:T(8,128)S(1)}, f32[32,16,128]{2,1,0:T(8,128)S(1)}, u32[]{:S(2)}, u32[]{:S(2)}) collective-permute-start(f32[32,16,128]{2,1,0:T(8,128)S(1)} %get-tuple-element.256), channel_id=1, source_target_pairs={{0,4},{4,0},{8,12},{12,8},{1,5},{5,1},{9,13},{13,9},{2,6},{6,2},{1... | collective-permute-start | bytes 786440 | tf_op jit(solution)/shard_map/ppermute | solution.py:361
  233.2 7.5 %collective-permute-done.27.refs_30_ = f32[32,16,128]{2,1,0:T(8,128)S(1)} collective-permute-done((f32[32,16,128]{2,1,0:T(8,128)S(1)}, f32[32,16,128]{2,1,0:T(8,128)S(1)}, u32[]{:S(2)}, u32[]{:S(2)}) %collective-permute-start.27) | collective-permute-done | bytes 262176 | tf_op jit(solution)/shard_map/ppermute | solution.py:361
  240.7 13.1 %collective-permute-done.32.refs_23_ = f32[32,16,128]{2,1,0:T(8,128)S(1)} collective-permute-done((f32[32,16,128]{2,1,0:T(8,128)S(1)}, f32[32,16,128]{2,1,0:T(8,128)S(1)}, u32[]{:S(2)}, u32[]{:S(2)}) %collective-permute-start.32) | collective-permute-done | bytes 262176 | tf_op jit(solution)/shard_map/ppermute | solution.py:361
  257.9 7.4 %collective-permute-done.28.refs_15_ = f32[32,16,128]{2,1,0:T(8,128)S(1)} collective-permute-done((f32[32,16,128]{2,1,0:T(8,128)S(1)}, f32[32,16,128]{2,1,0:T(8,128)S(1)}, u32[]{:S(2)}, u32[]{:S(2)}) %collective-permute-start.28) | collective-permute-done | bytes 262176 | tf_op jit(solution)/shard_map/ppermute | solution.py:361
  266.0 7.5 %collective-permute-start.31 = (f32[32,16,128]{2,1,0:T(8,128)S(1)}, f32[32,16,128]{2,1,0:T(8,128)S(1)}, u32[]{:S(2)}, u32[]{:S(2)}) collective-permute-start(f32[32,16,128]{2,1,0:T(8,128)S(1)} %get-tuple-element.266), channel_id=1, source_target_pairs={{0,4},{4,0},{8,12},{12,8},{1,5},{5,1},{9,13},{13,9},{2,6},{6,2},{1... | collective-permute-start | bytes 786440 | tf_op jit(solution)/shard_map/ppermute | solution.py:361
  284.8 10.7 %gram_k.9.refs_0_ = f32[768,256]{1,0:T(8,128)S(1)} custom-call(s32[3]{0:T(128)S(1)} %pad_add_fusion.place, f32[768,256]{1,0:T(8,128)S(1)} %broadcast_in_dim.3.refs_0_, f32[32,16,128]{2,1,0:T(8,128)} %copy-done.8, f32[32,16,128]{2,1,0:T(8,128)} %copy-done.9, f32[32,16,128]{2,1,0:T(8,128)} %copy-done.10, f32[32,16,128]{2,1,0:T(8,128)} %copy-done.11, ...), custom_call_target="tpu_custom_call" | custom-call | tf_op jit(solution)/shard_map/gram_k/pallas_call | solution.py:161
  303.2 8.0 %collective-permute-done.36.refs_2_ = f32[4,128,128]{2,1,0:T(8,128)S(1)} collective-permute-done((f32[4,128,128]{2,1,0:T(8,128)S(1)}, f32[4,128,128]{2,1,0:T(8,128)S(1)}, u32[]{:S(2)}, u32[]{:S(2)}) %collective-permute-start.36) | collective-permute-done | bytes 262176 | tf_op jit(solution)/shard_map/ppermute | solution.py:361
  332.6 7.0 %collective-permute-done.45.refs_3_.refs_11_ = f32[4,128,128]{2,1,0:T(8,128)S(1)} collective-permute-done((f32[4,128,128]{2,1,0:T(8,128)S(1)}, f32[4,128,128]{2,1,0:T(8,128)S(1)}, u32[]{:S(2)}, u32[]{:S(2)}) %collective-permute-start.45) | collective-permute-done | bytes 262176 | tf_op jit(solution)/shard_map/ppermute | solution.py:361
  343.7 9.9 %collective-permute-done.46.refs_4_.refs_12_ = f32[4,128,128]{2,1,0:T(8,128)S(1)} collective-permute-done((f32[4,128,128]{2,1,0:T(8,128)S(1)}, f32[4,128,128]{2,1,0:T(8,128)S(1)}, u32[]{:S(2)}, u32[]{:S(2)}) %collective-permute-start.46) | collective-permute-done | bytes 262176 | tf_op jit(solution)/shard_map/ppermute | solution.py:361
  353.6 8.4 %collective-permute-start.48 = (f32[4,128,128]{2,1,0:T(8,128)S(1)}, f32[4,128,128]{2,1,0:T(8,128)S(1)}, u32[]{:S(2)}, u32[]{:S(2)}) collective-permute-start(f32[4,128,128]{2,1,0:T(8,128)S(1)} %get-tuple-element.307), channel_id=1, source_target_pairs={{0,4},{4,0},{8,12},{12,8},{1,5},{5,1},{9,13},{13,9},{2,6},{6,2},{1... | collective-permute-start | bytes 786440 | tf_op jit(solution)/shard_map/ppermute | solution.py:361
  373.3 14.7 %collective-permute-done.49.refs_3_.refs_15_ = f32[4,128,128]{2,1,0:T(8,128)S(1)} collective-permute-done((f32[4,128,128]{2,1,0:T(8,128)S(1)}, f32[4,128,128]{2,1,0:T(8,128)S(1)}, u32[]{:S(2)}, u32[]{:S(2)}) %collective-permute-start.49) | collective-permute-done | bytes 262176 | tf_op jit(solution)/shard_map/ppermute | solution.py:361
  391.6 7.7 %collective-permute-done.53.refs_3_.refs_19_ = f32[4,128,128]{2,1,0:T(8,128)S(1)} collective-permute-done((f32[4,128,128]{2,1,0:T(8,128)S(1)}, f32[4,128,128]{2,1,0:T(8,128)S(1)}, u32[]{:S(2)}, u32[]{:S(2)}) %collective-permute-start.53) | collective-permute-done | bytes 262176 | tf_op jit(solution)/shard_map/ppermute | solution.py:361
  417.0 12.8 %collective-permute-done.57.refs_3_.refs_23_ = f32[4,128,128]{2,1,0:T(8,128)S(1)} collective-permute-done((f32[4,128,128]{2,1,0:T(8,128)S(1)}, f32[4,128,128]{2,1,0:T(8,128)S(1)}, u32[]{:S(2)}, u32[]{:S(2)}) %collective-permute-start.57) | collective-permute-done | bytes 262176 | tf_op jit(solution)/shard_map/ppermute | solution.py:361
  501.4 14.9 %subspace_k.1.refs_0_ = f32[512,128]{1,0:T(8,128)S(1)} custom-call(s32[3]{0:T(128)S(1)} %pad_add_fusion.place, f32[16,48,256]{2,1,0:T(8,128)S(1)} %constant_dynamic-update-slice_fusion.5.pieces_ref, f32[512,128]{1,0:T(8,128)S(1)} %copy-done.24), custom_call_target="tpu_custom_call" | custom-call | tf_op jit(solution)/shard_map/subspace_k/pallas_call | solution.py:243
  516.3 7.3 %core_k.2 = (f32[4,32,64,128]{3,2,1,0:T(8,128)}, f32[32,64,128]{2,1,0:T(8,128)}) custom-call(s32[3]{0:T(128)S(1)} %pad_add_fusion.place, f32[512,128]{1,0:T(8,128)S(1)} %subspace_k.1.refs_0_, f32[32,16,128]{2,1,0:T(8,128)} %copy-done.8, f32[32,16,128]{2,1,0:T(8,128)} %copy-done.9, f32[32,16,128]{2,1,0:T(8,128)} %copy-done.10, f32[32,16,128]{2,1,0:T(8,128)} %copy-done.11, ...), custom_call_target="tpu_custom_call" | custom-call | tf_op jit(solution)/shard_map/core_k/pallas_call | solution.py:316
  523.8 8.2 %core_k.3 = (f32[4,32,64,128]{3,2,1,0:T(8,128)}, f32[32,64,128]{2,1,0:T(8,128)}) custom-call(s32[3]{0:T(128)S(1)} %pad_add_fusion.place, f32[512,128]{1,0:T(8,128)S(1)} %subspace_k.1.refs_0_, f32[4,128,128]{2,1,0:T(8,128)} %copy-done.16, f32[4,128,128]{2,1,0:T(8,128)} %copy-done.57, f32[4,128,128]{2,1,0:T(8,128)} %copy-done.56, ...), custom_call_target="tpu_custom_call", output_to_operand_aliasing={{0}: (34, {})} | custom-call | tf_op jit(solution)/shard_map/core_k/pallas_call | solution.py:316
  (356 shorter events, 293.4 us)
Async XLA Ops:
  13.0 26.5 %collective-permute-start.1 = (f32[4,32,16,128]{3,2,1,0:T(8,128)}, f32[4,32,16,128]{3,2,1,0:T(8,128)S(1)}, u32[]{:S(2)}, u32[]{:S(2)}) collective-permute-start(f32[4,32,16,128]{3,2,1,0:T(8,128)} %get-tuple-element.180), channel_id=1, source_target_pairs={{0,2},{1,3},{2,0},{3,1},{4,6},{5,7},{6,4},{7,5},{8,10},{9,11},{10,... | collective-permute-start | bytes 3145736 | tf_op jit(solution)/shard_map/ppermute | solution.py:357
  53.9 114.8 %collective-permute-start.18 = (f32[128,128,256]{2,1,0:T(8,128)}, f32[128,128,256]{2,1,0:T(8,128)S(1)}, u32[]{:S(2)}, u32[]{:S(2)}) collective-permute-start(f32[128,128,256]{2,1,0:T(8,128)} %dynamic-slice_bitcast_fusion), channel_id=1, source_target_pairs={{0,1},{1,0},{2,3},{3,2},{4,5},{5,4},{6,7},{7,6},{8,9},{9,8},{10,11... | collective-permute-start | bytes 50331656 | tf_op jit(solution)/shard_map/ppermute | solution.py:357
  58.3 26.0 %collective-permute-start.3 = (f32[4,32,16,128]{3,2,1,0:T(8,128)S(1)}, f32[4,32,16,128]{3,2,1,0:T(8,128)S(1)}, u32[]{:S(2)}, u32[]{:S(2)}) collective-permute-start(f32[4,32,16,128]{3,2,1,0:T(8,128)S(1)} %get-tuple-element.184), channel_id=1, source_target_pairs={{0,2},{1,3},{2,0},{3,1},{4,6},{5,7},{6,4},{7,5},{8,10},{9,11},{10,... | collective-permute-start | bytes 3145736 | tf_op jit(solution)/shard_map/ppermute | solution.py:357
  64.5 47.8 %collective-permute-start.4 = (f32[4,32,16,128]{3,2,1,0:T(8,128)S(1)}, f32[4,32,16,128]{3,2,1,0:T(8,128)S(1)}, u32[]{:S(2)}, u32[]{:S(2)}) collective-permute-start(f32[4,32,16,128]{3,2,1,0:T(8,128)S(1)} %get-tuple-element.188), channel_id=1, source_target_pairs={{0,2},{1,3},{2,0},{3,1},{4,6},{5,7},{6,4},{7,5},{8,10},{9,11},{10,... | collective-permute-start | bytes 3145736 | tf_op jit(solution)/shard_map/ppermute | solution.py:357
  84.3 51.5 %collective-permute-start.6 = (f32[4,32,16,128]{3,2,1,0:T(8,128)S(1)}, f32[4,32,16,128]{3,2,1,0:T(8,128)S(1)}, u32[]{:S(2)}, u32[]{:S(2)}) collective-permute-start(f32[4,32,16,128]{3,2,1,0:T(8,128)S(1)} %get-tuple-element.193), channel_id=1, source_target_pairs={{0,2},{1,3},{2,0},{3,1},{4,6},{5,7},{6,4},{7,5},{8,10},{9,11},{10,... | collective-permute-start | bytes 3145736 | tf_op jit(solution)/shard_map/ppermute | solution.py:357
  112.5 52.7 %collective-permute-start.10 = (f32[4,32,16,128]{3,2,1,0:T(8,128)S(1)}, f32[4,32,16,128]{3,2,1,0:T(8,128)S(1)}, u32[]{:S(2)}, u32[]{:S(2)}) collective-permute-start(f32[4,32,16,128]{3,2,1,0:T(8,128)S(1)} %get-tuple-element.201), channel_id=1, source_target_pairs={{0,2},{1,3},{2,0},{3,1},{4,6},{5,7},{6,4},{7,5},{8,10},{9,11},{10,... | collective-permute-start | bytes 3145736 | tf_op jit(solution)/shard_map/ppermute | solution.py:357
  135.8 63.9 %collective-permute-start.14 = (f32[4,32,16,128]{3,2,1,0:T(8,128)S(1)}, f32[4,32,16,128]{3,2,1,0:T(8,128)S(1)}, u32[]{:S(2)}, u32[]{:S(2)}) collective-permute-start(f32[4,32,16,128]{3,2,1,0:T(8,128)S(1)} %get-tuple-element.211), channel_id=1, source_target_pairs={{0,2},{1,3},{2,0},{3,1},{4,6},{5,7},{6,4},{7,5},{8,10},{9,11},{10,... | collective-permute-start | bytes 3145736 | tf_op jit(solution)/shard_map/ppermute | solution.py:357
  147.1 34.9 %collective-permute-start.16 = (f32[32,16,128]{2,1,0:T(8,128)S(1)}, f32[32,16,128]{2,1,0:T(8,128)S(1)}, u32[]{:S(2)}, u32[]{:S(2)}) collective-permute-start(f32[32,16,128]{2,1,0:T(8,128)S(1)} %get-tuple-element.218), channel_id=1, source_target_pairs={{0,8},{4,12},{8,0},{12,4},{1,9},{5,13},{9,1},{13,5},{2,10},{6,14},... | collective-permute-start | bytes 786440 | tf_op jit(solution)/shard_map/ppermute | solution.py:361
  152.5 29.5 %collective-permute-start.20 = (f32[32,16,128]{2,1,0:T(8,128)S(1)}, f32[32,16,128]{2,1,0:T(8,128)S(1)}, u32[]{:S(2)}, u32[]{:S(2)}) collective-permute-start(f32[32,16,128]{2,1,0:T(8,128)S(1)} %get-tuple-element.229), channel_id=1, source_target_pairs={{0,4},{4,0},{8,12},{12,8},{1,5},{5,1},{9,13},{13,9},{2,6},{6,2},{1... | collective-permute-start | bytes 786440 | tf_op jit(solution)/shard_map/ppermute | solution.py:361
  165.1 34.6 %collective-permute-start.22 = (f32[32,16,128]{2,1,0:T(8,128)S(1)}, f32[32,16,128]{2,1,0:T(8,128)S(1)}, u32[]{:S(2)}, u32[]{:S(2)}) collective-permute-start(f32[32,16,128]{2,1,0:T(8,128)S(1)} %get-tuple-element.232), channel_id=1, source_target_pairs={{0,12},{4,8},{8,4},{12,0},{1,13},{5,9},{9,5},{13,1},{2,14},{6,10},... | collective-permute-start | bytes 786440 | tf_op jit(solution)/shard_map/ppermute | solution.py:361
  182.0 47.0 %collective-permute-start.19 = (f32[4,32,16,128]{3,2,1,0:T(8,128)S(1)}, f32[4,32,16,128]{3,2,1,0:T(8,128)S(1)}, u32[]{:S(2)}, u32[]{:S(2)}) collective-permute-start(f32[4,32,16,128]{3,2,1,0:T(8,128)S(1)} %get-tuple-element.223), channel_id=1, source_target_pairs={{0,2},{1,3},{2,0},{3,1},{4,6},{5,7},{6,4},{7,5},{8,10},{9,11},{10,... | collective-permute-start | bytes 3145736 | tf_op jit(solution)/shard_map/ppermute | solution.py:357
  199.8 41.0 %collective-permute-start.23 = (f32[4,32,16,128]{3,2,1,0:T(8,128)S(1)}, f32[4,32,16,128]{3,2,1,0:T(8,128)S(1)}, u32[]{:S(2)}, u32[]{:S(2)}) collective-permute-start(f32[4,32,16,128]{3,2,1,0:T(8,128)S(1)} %get-tuple-element.249), channel_id=1, source_target_pairs={{0,2},{1,3},{2,0},{3,1},{4,6},{5,7},{6,4},{7,5},{8,10},{9,11},{10,... | collective-permute-start | bytes 3145736 | tf_op jit(solution)/shard_map/ppermute | solution.py:357
  229.0 48.5 %collective-permute-start.35 = (f32[4,4,128,128]{3,2,1,0:T(8,128)}, f32[4,4,128,128]{3,2,1,0:T(8,128)S(1)}, u32[]{:S(2)}, u32[]{:S(2)}) collective-permute-start(f32[4,4,128,128]{3,2,1,0:T(8,128)} %get-tuple-element.274), channel_id=1, source_target_pairs={{0,2},{1,3},{2,0},{3,1},{4,6},{5,7},{6,4},{7,5},{8,10},{9,11},{10,... | collective-permute-start | bytes 3145736 | tf_op jit(solution)/shard_map/ppermute | solution.py:357
  253.8 45.0 %collective-permute-start.39 = (f32[4,4,128,128]{3,2,1,0:T(8,128)}, f32[4,4,128,128]{3,2,1,0:T(8,128)S(1)}, u32[]{:S(2)}, u32[]{:S(2)}) collective-permute-start(f32[4,4,128,128]{3,2,1,0:T(8,128)} %get-tuple-element.284), channel_id=1, source_target_pairs={{0,2},{1,3},{2,0},{3,1},{4,6},{5,7},{6,4},{7,5},{8,10},{9,11},{10,... | collective-permute-start | bytes 3145736 | tf_op jit(solution)/shard_map/ppermute | solution.py:357
  277.5 47.8 %collective-permute-start.43 = (f32[4,4,128,128]{3,2,1,0:T(8,128)}, f32[4,4,128,128]{3,2,1,0:T(8,128)S(1)}, u32[]{:S(2)}, u32[]{:S(2)}) collective-permute-start(f32[4,4,128,128]{3,2,1,0:T(8,128)} %get-tuple-element.294), channel_id=1, source_target_pairs={{0,2},{1,3},{2,0},{3,1},{4,6},{5,7},{6,4},{7,5},{8,10},{9,11},{10,... | collective-permute-start | bytes 3145736 | tf_op jit(solution)/shard_map/ppermute | solution.py:357
  298.8 40.9 %collective-permute-start.47 = (f32[4,4,128,128]{3,2,1,0:T(8,128)S(1)}, f32[4,4,128,128]{3,2,1,0:T(8,128)S(1)}, u32[]{:S(2)}, u32[]{:S(2)}) collective-permute-start(f32[4,4,128,128]{3,2,1,0:T(8,128)S(1)} %copy-done.27), channel_id=1, source_target_pairs={{0,2},{1,3},{2,0},{3,1},{4,6},{5,7},{6,4},{7,5},{8,10},{9,11},{10,... | collective-permute-start | bytes 3145736 | tf_op jit(solution)/shard_map/ppermute | solution.py:357
  325.4 41.9 %collective-permute-start.51 = (f32[4,4,128,128]{3,2,1,0:T(8,128)S(1)}, f32[4,4,128,128]{3,2,1,0:T(8,128)S(1)}, u32[]{:S(2)}, u32[]{:S(2)}) collective-permute-start(f32[4,4,128,128]{3,2,1,0:T(8,128)S(1)} %copy-done.28), channel_id=1, source_target_pairs={{0,2},{1,3},{2,0},{3,1},{4,6},{5,7},{6,4},{7,5},{8,10},{9,11},{10,... | collective-permute-start | bytes 3145736 | tf_op jit(solution)/shard_map/ppermute | solution.py:357
  339.7 59.6 %collective-permute-start.55 = (f32[4,4,128,128]{3,2,1,0:T(8,128)S(1)}, f32[4,4,128,128]{3,2,1,0:T(8,128)S(1)}, u32[]{:S(2)}, u32[]{:S(2)}) collective-permute-start(f32[4,4,128,128]{3,2,1,0:T(8,128)S(1)} %copy-done.29), channel_id=1, source_target_pairs={{0,2},{1,3},{2,0},{3,1},{4,6},{5,7},{6,4},{7,5},{8,10},{9,11},{10,... | collective-permute-start | bytes 3145736 | tf_op jit(solution)/shard_map/ppermute | solution.py:357
  362.0 26.0 %collective-permute-start.49 = (f32[4,128,128]{2,1,0:T(8,128)S(1)}, f32[4,128,128]{2,1,0:T(8,128)S(1)}, u32[]{:S(2)}, u32[]{:S(2)}) collective-permute-start(f32[4,128,128]{2,1,0:T(8,128)S(1)} %get-tuple-element.309), channel_id=1, source_target_pairs={{0,8},{4,12},{8,0},{12,4},{1,9},{5,13},{9,1},{13,5},{2,10},{6,14},... | collective-permute-start | bytes 786440 | tf_op jit(solution)/shard_map/ppermute | solution.py:361
  362.0 26.0 %collective-permute-start.50 = (f32[4,128,128]{2,1,0:T(8,128)S(1)}, f32[4,128,128]{2,1,0:T(8,128)S(1)}, u32[]{:S(2)}, u32[]{:S(2)}) collective-permute-start(f32[4,128,128]{2,1,0:T(8,128)S(1)} %get-tuple-element.311), channel_id=1, source_target_pairs={{0,12},{4,8},{8,4},{12,0},{1,13},{5,9},{9,5},{13,1},{2,14},{6,10},... | collective-permute-start | bytes 786440 | tf_op jit(solution)/shard_map/ppermute | solution.py:361
  367.9 31.4 %collective-permute-start.53 = (f32[4,128,128]{2,1,0:T(8,128)S(1)}, f32[4,128,128]{2,1,0:T(8,128)S(1)}, u32[]{:S(2)}, u32[]{:S(2)}) collective-permute-start(f32[4,128,128]{2,1,0:T(8,128)S(1)} %get-tuple-element.319), channel_id=1, source_target_pairs={{0,8},{4,12},{8,0},{12,4},{1,9},{5,13},{9,1},{13,5},{2,10},{6,14},... | collective-permute-start | bytes 786440 | tf_op jit(solution)/shard_map/ppermute | solution.py:361
  388.0 28.3 %collective-permute-start.59 = (f32[4,4,128,128]{3,2,1,0:T(8,128)S(1)}, f32[4,4,128,128]{3,2,1,0:T(8,128)S(1)}, u32[]{:S(2)}, u32[]{:S(2)}) collective-permute-start(f32[4,4,128,128]{3,2,1,0:T(8,128)S(1)} %copy-done.30), channel_id=1, source_target_pairs={{0,2},{1,3},{2,0},{3,1},{4,6},{5,7},{6,4},{7,5},{8,10},{9,11},{10,... | collective-permute-start | bytes 3145736 | tf_op jit(solution)/shard_map/ppermute | solution.py:357
  399.3 47.9 %collective-permute-start.63 = (f32[4,4,128,128]{3,2,1,0:T(8,128)S(1)}, f32[4,4,128,128]{3,2,1,0:T(8,128)S(1)}, u32[]{:S(2)}, u32[]{:S(2)}) collective-permute-start(f32[4,4,128,128]{3,2,1,0:T(8,128)S(1)} %copy-done.31), channel_id=1, source_target_pairs={{0,2},{1,3},{2,0},{3,1},{4,6},{5,7},{6,4},{7,5},{8,10},{9,11},{10,... | collective-permute-start | bytes 3145736 | tf_op jit(solution)/shard_map/ppermute | solution.py:357
  415.4 26.3 %collective-permute-start.56 = (f32[4,128,128]{2,1,0:T(8,128)S(1)}, f32[4,128,128]{2,1,0:T(8,128)S(1)}, u32[]{:S(2)}, u32[]{:S(2)}) collective-permute-start(f32[4,128,128]{2,1,0:T(8,128)S(1)} %get-tuple-element.327), channel_id=1, source_target_pairs={{0,4},{4,0},{8,12},{12,8},{1,5},{5,1},{9,13},{13,9},{2,6},{6,2},{1... | collective-permute-start | bytes 786440 | tf_op jit(solution)/shard_map/ppermute | solution.py:361
  (135 other events, 3445.9 us)
